TPU v7x, 512 devices: a whole 4x8x8 slice. The times are simulated.
512 devices in a mesh: ctx: 64 (over y, z_hi, x), tp: 8 (over z_lo, core).
Axes of the slice: x: 4, y: 8, z: 8 (z_hi: 2, z_lo: 4; z = z_hi * 4 + z_lo), core: 2. Of those that a mesh axis runs over, the one named last changes fastest.
Arguments:
- queries: bfloat16 [8192, 4096], P('ctx', 'tp'), may hold values from -5 to 5
- keys: bfloat16 [8192, 1024], P('ctx', 'tp'), may hold values from -5 to 5
- values: bfloat16 [8192, 1024], P('ctx', 'tp'), may hold values from -6 to 6
- out_grad: bfloat16 [8192, 4096], P('ctx', 'tp'), may hold values from -6 to 6
- features: bfloat16 [8192, 4096], P('ctx'), may hold values from -6 to 6
- segment_ids: int32 [8192], replicated, may hold values from 0 to 15, never falling along the last dimension, each value on 1 to 6144 neighbouring positions
Outputs:
- query_grads: bfloat16 [8192, 4096], P('ctx', 'tp')
- weight_grad: float32 [4096, 1024], P('tp')
Inputs may be any that keep to these rules, and one draw needn't show every extreme that they name: `segment_ids`: never falling along the sequence; each document has 1 to 6144 tokens and one has exactly 6144.
All inputs are finite; a program needn't handle non-finite values.
Results may differ from a plain program's by a relative error of at most 0.024.
Values may be sent and summed in bfloat16 or wider, within the bound.
No kernel may reach another device: no remote copies, remote signals or barrier semaphores. Data moves between devices by JAX's collectives and lax.ppermute only.
A program may use at most 64 MiB of HBM per device.

v0:
```python
import math

import jax
import jax.numpy as jnp
from jax import lax
from jax.sharding import PartitionSpec as P

HD = 128


def per_device(queries, keys, values, out_grad, features, segment_ids):
    rows = queries.shape[0]
    heads_q = queries.shape[1] // HD
    heads_kv = keys.shape[1] // HD
    group = heads_q // heads_kv
    tokens = segment_ids.shape[0]
    width = math.gcd(tokens, 1024)
    scale = HD ** (-0.5)
    first = lax.axis_index("ctx") * rows
    gathered = (
        lax.all_gather(keys, "ctx", axis=0, tiled=True),
        lax.all_gather(values, "ctx", axis=0, tiled=True),
    )
    key_all = gathered[0].reshape(tokens, heads_kv, HD)
    value_all = gathered[1].reshape(tokens, heads_kv, HD)
    query_heads = queries.reshape(rows, heads_kv, group, HD)
    grad_heads = out_grad.reshape(rows, heads_kv, group, HD)
    seg_own = lax.dynamic_slice_in_dim(segment_ids, first, rows, 0)
    pos_own = first + jnp.arange(rows, dtype=jnp.int32)
    last_row = first + rows - 1
    seg_first = seg_own[0]

    def active(start, count):
        seg_end = lax.dynamic_index_in_dim(segment_ids, start + count - 1, 0, keepdims=False)
        return (start <= last_row) & (seg_end >= seg_first)

    def masked_scores(start, count):
        key_block = lax.dynamic_slice_in_dim(key_all, start, count, 0)
        seg_block = lax.dynamic_slice_in_dim(segment_ids, start, count, 0)
        pos_block = start + jnp.arange(count, dtype=jnp.int32)
        allowed = (pos_block[None, :] <= pos_own[:, None]) & (
            seg_block[None, :] == seg_own[:, None]
        )
        scores = (
            jnp.einsum("qngd,knd->ngqk", query_heads, key_block, preferred_element_type=jnp.float32)
            * scale
        )
        return (jnp.where(allowed, scores, -1e30), allowed)

    starts = jnp.arange(tokens // width, dtype=jnp.int32) * width

    def forward_step(carry, start):

        def forward_work(state):
            top, total, accum = state
            scores, allowed = masked_scores(start, width)
            top_new = jnp.maximum(top, jnp.max(scores, axis=-1))
            factor = jnp.exp(top - top_new)
            weights = jnp.where(allowed, jnp.exp(scores - top_new[..., None]), 0.0)
            value_block = lax.dynamic_slice_in_dim(value_all, start, width, 0)
            update = jnp.einsum(
                "ngqk,knd->ngqd",
                weights.astype(jnp.bfloat16),
                value_block,
                preferred_element_type=jnp.float32,
            )
            accum = accum * factor[..., None] + update
            total = total * factor + jnp.sum(weights, axis=-1)
            return (top_new, total, accum)

        def keep(state):
            return state

        return (lax.cond(active(start, width), forward_work, keep, carry), None)

    initial = (
        jnp.full((heads_kv, group, rows), -1e30, jnp.float32),
        jnp.zeros((heads_kv, group, rows), jnp.float32),
        jnp.zeros((heads_kv, group, rows, HD), jnp.float32),
    )
    (top, total, accum), _ = lax.scan(forward_step, initial, starts)
    attended = (accum / total[..., None]).astype(jnp.bfloat16)
    log_total = top + jnp.log(total)
    delta = jnp.einsum("qngd,ngqd->ngq", grad_heads, attended, preferred_element_type=jnp.float32)

    def probabilities(start, count):
        scores, allowed = masked_scores(start, count)
        return jnp.where(allowed, jnp.exp(scores - log_total[..., None]), 0.0)

    def query_update(carry, start, probs):
        key_block = lax.dynamic_slice_in_dim(key_all, start, width, 0)
        value_block = lax.dynamic_slice_in_dim(value_all, start, width, 0)
        dprob = jnp.einsum(
            "qngd,knd->ngqk", grad_heads, value_block, preferred_element_type=jnp.float32
        )
        dscore = probs * (dprob - delta[..., None])
        return carry + jnp.einsum(
            "ngqk,knd->qngd",
            dscore.astype(jnp.bfloat16),
            key_block,
            preferred_element_type=jnp.float32,
        )

    def value_part(probs, count):
        part = jnp.einsum(
            "ngqk,qngd->knd",
            probs.astype(jnp.bfloat16),
            grad_heads,
            preferred_element_type=jnp.float32,
        )
        return part.reshape(count, heads_kv * HD)

    zero_grad = jnp.zeros((rows, heads_kv, group, HD), jnp.float32)

    def after_step(carry, start):

        def after_work(state):
            probs = probabilities(start, width)
            return (query_update(state, start, probs), value_part(probs, width))

        def rest(state):
            return (state, jnp.zeros((width, heads_kv * HD), jnp.float32))

        return lax.cond(active(start, width), after_work, rest, carry)

    query_accum, blocks = lax.scan(after_step, zero_grad, starts)
    value_grad = lax.psum_scatter(
        blocks.reshape(tokens, heads_kv * HD), "ctx", scatter_dimension=0, tiled=True
    )
    query_grads = (query_accum * scale).astype(jnp.bfloat16).reshape(rows, heads_q * HD)
    value_b = value_grad.astype(jnp.bfloat16)
    factor_tokens = 1.0 / math.sqrt(tokens)
    contract = (((0,), (0,)), ((), ()))
    own_term = lax.dot_general(features, value_b, contract, preferred_element_type=jnp.float32)
    summed = lax.psum(own_term, "ctx")
    weight_grad = (
        lax.all_to_all(
            summed.astype(jnp.bfloat16), "tp", split_axis=0, concat_axis=1, tiled=True
        ).astype(summed.dtype)
        * factor_tokens
    )
    return (query_grads, weight_grad)


def solution(mesh):
    placed = (P("ctx", "tp"), P("ctx", "tp"), P("ctx", "tp"), P("ctx", "tp"), P("ctx", None), P())
    return jax.shard_map(
        per_device,
        mesh=mesh,
        in_specs=placed,
        out_specs=(P("ctx", "tp"), P("tp", None)),
        check_vma=False,
    )
```

profile of v0, /device:TPU:6, one launch (start us, length us, event | category | flops | bytes accessed | tf_op | source)
XLA Modules:
  0.0 1425.9 jit_solution(11759114608969016191)
XLA Ops:
  13.4 142.8 %all-gather.3.cloned.1.call-done = bf16[8192,128]{1,0:T(8,128)(2,1)} async-done(((bf16[128,128]{1,0:T(8,128)(2,1)}), bf16[8192,128]{1,0:T(8,128)(2,1)}) %all-gather.3.cloned.1.call-update) | async-done | bytes 2097168 | tf_op jit(solution)/shard_map/all_gather | solution.py:21
  156.2 136.8 %all-gather.5.cloned.1.call-done = bf16[8192,128]{1,0:T(8,128)(2,1)} async-done(((bf16[128,128]{1,0:T(8,128)(2,1)}), bf16[8192,128]{1,0:T(8,128)(2,1)}) %all-gather.5.cloned.1.call-update) | async-done | bytes 2097168 | tf_op jit(solution)/shard_map/all_gather | solution.py:22
  293.0 45.4 %while.39 = (s32[]{:T(128)}, f32[1,4,128]{2,1,0:T(4,128)S(1)}, f32[1,4,128]{2,1,0:T(4,128)S(1)}, f32[1,4,128,128]{3,2,1,0:T(8,128)S(1)}, s32[8]{0:T(128)S(1)}, /...) while((s32[]{:T(128)}, f32[1,4,128]{2,1,0:T(4,128)S(1)}, ...), condition=%wide.region_5.6_spmd.clone, body=%wide.region_0.5_spmd.clone.sunk | while | flops 275778176 | bytes 8051651 | solution.py:81
  297.7 7.7 conditional.6
  303.1 1.8 fusion.7
  339.0 66.5 %while.40 = (s32[]{:T(128)}, f32[128,1,4,128]{0,3,2,1:T(8,128)S(1)}, f32[8,1024,128]{2,1,0:T(8,128)}, s32[8]{0:T(128)S(1)}, s32[]{:T(128)}, /*index=5*/s32[8192]...) while((s32[]{:T(128)}, ...), condition=%wide.region_9.10_spmd.clone, body=%wide.region_6.9_spmd.clone.sunk | while | flops 541525120 | bytes 9859503 | solution.py:126
  343.7 8.5 conditional.7
  347.6 1.7 fusion.31
  350.5 1.7 fusion.33
  352.2 1.9 constant_dynamic-update-slice_fusion.2
  359.5 1.9 constant_dynamic-update-slice_fusion.2
  366.9 1.9 constant_dynamic-update-slice_fusion.2
  374.2 1.9 constant_dynamic-update-slice_fusion.2
  381.6 1.9 constant_dynamic-update-slice_fusion.2
  389.0 1.9 constant_dynamic-update-slice_fusion.2
  396.3 1.9 constant_dynamic-update-slice_fusion.2
  403.7 1.9 constant_dynamic-update-slice_fusion.2
  405.6 518.5 %reduce-scatter.2.cloned.1.call-done = f32[128,128]{1,0:T(8,128)} async-done(((f32[8192,128]{1,0:T(8,128)}), f32[128,128]{1,0:T(8,128)}) %reduce-scatter.2.cloned.1.call-update) | async-done | bytes 65552 | tf_op jit(solution)/shard_map/reduce_scatter | solution.py:127
  925.4 452.8 %all-reduce.1 = bf16[4096,128]{0,1:T(8,128)(2,1)} all-reduce(f32[4096,128]{0,1:T(8,128)S(1)} %convolution_bitcast_fusion.3), channel_id=1, replica_groups=mesh['ctx'=64,'tp'=8] {'ctx'}, use_global_device_ids=true, to_apply=%region_11.12 | all-reduce | flops 524288 | bytes 3145728 | tf_op jit(solution)/shard_map/psum | solution.py:135
  1378.2 2.4 copy.48
  1380.5 8.6 all-to-all-start
  1389.9 26.1 %all-to-all-done = bf16[8,512,128]{1,2,0:T(8,128)(2,1)} async-done(((bf16[8,512,128]{1,2,0:T(8,128)(2,1)}), bf16[8,512,128]{1,2,0:T(8,128)(2,1)}, u32[]{:S(2)}, u32[]{:S(2)}) %all-to-all-start) | async-done | bytes 1048608 | tf_op jit(solution)/shard_map/all_to_all | solution.py:137
  1416.0 1.5 convert_multiply_fusion
  1417.5 1.8 copy.33
  (110 shorter events, 58.8 us)
Async XLA Ops:
  7.2 916.9 %copy-start = (bf16[128,4096]{1,0:T(8,128)(2,1)S(1)}, bf16[128,4096]{1,0:T(8,128)(2,1)}, u32[]{:S(2)}) copy-start(bf16[128,4096]{1,0:T(8,128)(2,1)} %param.18) | copy-start | bytes 3145732
  7.2 149.0 %all-gather.3.cloned.1.call-start = ((), (), s32[]{:S(2)}) async-start(), calls=%async_computation.2 | async-start | bytes 2129920 | tf_op jit(solution)/shard_map/all_gather | solution.py:21
  7.9 285.1 %all-gather.5.cloned.1.call-start = ((), (), s32[]{:S(2)}) async-start(), calls=%async_computation.3 | async-start | bytes 2129920 | tf_op jit(solution)/shard_map/all_gather | solution.py:22
  8.7 915.4 %reduce-scatter.2.cloned.1.call-start = ((), (), s32[]{:S(2)}) async-start(), calls=%async_computation.4 | async-start | bytes 4259840 | tf_op jit(solution)/shard_map/reduce_scatter | solution.py:127
  1380.5 35.5 %all-to-all-start = ((bf16[8,512,128]{1,2,0:T(8,128)(2,1)}), bf16[8,512,128]{1,2,0:T(8,128)(2,1)}, u32[]{:S(2)}, u32[]{:S(2)}) async-start(bf16[8,512,128]{1,2,0:T(8,128)(2,1)} %bitcast.133), calls=%async_computation.1 | async-start | bytes 2097152 | tf_op jit(solution)/shard_map/all_to_all | solution.py:137
Sparse Core Ops, SparseCore 0:
  12.5 143.6 all-gather.2
  160.7 132.2 all-gather.4
  405.7 518.3 reduce-scatter.1
where the time goes:
time: 1450 us; the launch traced here: 1430 us
  waiting for transfers between devices  826 us (57%)
  blocking collectives  453 us (31%)
  local copies, waits for them, and re-layouts  63.4 us (4%)
  loops' own time  47.9 us (3%)
    reduce_scatter x1, waiting for transfers between devices, per_device(): lax.psum_scatter(blocks.reshape(tokens, heads_kv * HD), 'ctx', scatter_di...  519 us
    psum x1, blocking collectives, per_device(): summed = lax.psum(own_term, 'ctx')  453 us
    all_gather x1, waiting for transfers between devices, per_device(): lax.all_gather(keys, 'ctx', axis=0, tiled=True)  143 us
    all_gather x1, waiting for transfers between devices, per_device(): lax.all_gather(values, 'ctx', axis=0, tiled=True)  137 us
  transfers between devices with their start and end apart: 4, of which 4 were waited for; matrix products, arithmetic and copies ran while one was open for 0% of the time, Pallas kernels for 0%

commit v1 on v0

v1 whole, which is shorter than its diff:
```python
import math

import jax
import jax.numpy as jnp
from jax import lax
from jax.experimental import pallas as pl
from jax.experimental.pallas import tpu as pltpu
from jax.sharding import Mesh, PartitionSpec as P

HD = 128
GROUP = 4
DIMS = (8, 2, 4, 4, 2)
AXES = ("y", "zh", "x", "zl", "core")
CTX = ("y", "zh", "x")
TP = ("zl", "core")
BLOCK = 128
CHUNK = 256
LOW = -1e30
FLOOR = -1e29
SCALE = HD ** (-0.5)
SCALE2 = SCALE * math.log2(math.e)
NT = (((1,), (1,)), ((), ()))
TN = (((0,), (0,)), ((), ()))


def chunk_scores(j, x, nx, pos_q, start, kv_ref):
    at = pl.ds(pl.multiple_of(j * CHUNK, CHUNK), CHUNK)
    k = kv_ref[at, 0:HD]
    v = kv_ref[at, HD : 2 * HD]
    r = lax.broadcasted_iota(jnp.int32, (CHUNK, 1), 0)
    per = CHUNK // BLOCK
    pos_k = (j * per + r // BLOCK) * (nx * BLOCK) + x * BLOCK + r % BLOCK
    allowed = (pos_k <= pos_q) & (pos_k >= start)
    return at, k, v, allowed


def head_of(q_ref, n):
    nx, rows, _ = q_ref.shape
    q = q_ref[:, :, n * HD : (n + 1) * HD].reshape(nx * rows, HD)
    do = q_ref[:, :, (GROUP + n) * HD : (GROUP + n + 1) * HD].reshape(nx * rows, HD)
    return q, do


def stats_kernel(nx, sc_ref, start_ref, q_ref, kv_ref, out_ref):
    g, low, x = sc_ref[0], sc_ref[1], sc_ref[2]
    span = nx * BLOCK
    pos_q = g * span + lax.broadcasted_iota(jnp.int32, (1, span), 1)
    start = start_ref[...]
    out_ref[0] = jnp.full((GROUP, span), FLOOR, jnp.float32)
    out_ref[1] = jnp.zeros((GROUP, span), jnp.float32)
    out_ref[2] = jnp.zeros((GROUP, span), jnp.float32)
    per = CHUNK // BLOCK

    def body(j, carry):
        _, k, v, allowed = chunk_scores(j, x, nx, pos_q, start, kv_ref)
        for n in range(GROUP):
            q, do = head_of(q_ref, n)
            s = lax.dot_general(k, q, NT, preferred_element_type=jnp.float32) * SCALE2
            s = jnp.where(allowed, s, LOW)
            dp = lax.dot_general(v, do, NT, preferred_element_type=jnp.float32)
            m_old = out_ref[0, n : n + 1, :]
            m = jnp.maximum(m_old, jnp.max(s, axis=0, keepdims=True))
            alpha = jnp.exp2(m_old - m)
            w = jnp.exp2(s - m)
            out_ref[0, n : n + 1, :] = m
            out_ref[1, n : n + 1, :] = out_ref[1, n : n + 1, :] * alpha + jnp.sum(
                w, axis=0, keepdims=True
            )
            out_ref[2, n : n + 1, :] = out_ref[2, n : n + 1, :] * alpha + jnp.sum(
                w * dp, axis=0, keepdims=True
            )
        return carry

    lax.fori_loop(low // per, g // per + 1, body, 0)


def grad_kernel(nx, sc_ref, start_ref, st_ref, q_ref, kv_ref, dq_ref, dv_ref, acc_ref):
    g, low, x = sc_ref[0], sc_ref[1], sc_ref[2]
    span = nx * BLOCK
    pos_q = g * span + lax.broadcasted_iota(jnp.int32, (1, span), 1)
    start = start_ref[...]
    acc_ref[...] = jnp.zeros(acc_ref.shape, jnp.float32)
    dv_ref[...] = jnp.zeros(dv_ref.shape, dv_ref.dtype)
    per = CHUNK // BLOCK
    top = st_ref[0, 0]
    for i in range(1, nx):
        top = jnp.maximum(top, st_ref[i, 0])
    total = jnp.zeros_like(top)
    num = jnp.zeros_like(top)
    for i in range(nx):
        f = jnp.exp2(st_ref[i, 0] - top)
        total = total + st_ref[i, 1] * f
        num = num + st_ref[i, 2] * f
    log_total = top + jnp.log2(total)
    delta = num / total

    def body(j, carry):
        at, k, v, allowed = chunk_scores(j, x, nx, pos_q, start, kv_ref)
        dv = jnp.zeros((CHUNK, HD), jnp.float32)
        for n in range(GROUP):
            q, do = head_of(q_ref, n)
            s = lax.dot_general(k, q, NT, preferred_element_type=jnp.float32) * SCALE2
            s = jnp.where(allowed, s, LOW)
            dp = lax.dot_general(v, do, NT, preferred_element_type=jnp.float32)
            p = jnp.exp2(s - log_total[n : n + 1, :])
            ds = (p * (dp - delta[n : n + 1, :])).astype(jnp.bfloat16)
            dv = dv + jnp.dot(p.astype(jnp.bfloat16), do, preferred_element_type=jnp.float32)
            acc_ref[n] += lax.dot_general(k, ds, TN, preferred_element_type=jnp.float32)
        dv_ref[at, :] = dv.astype(dv_ref.dtype)
        return carry

    lax.fori_loop(low // per, g // per + 1, body, 0)
    for n in range(GROUP):
        dq_ref[:, n * HD : (n + 1) * HD] = (acc_ref[n] * SCALE).T.astype(dq_ref.dtype)


def spread(piece, axes, count):
    copies = jnp.broadcast_to(piece[None], (count,) + piece.shape)
    return lax.all_to_all(copies, axes, split_axis=0, concat_axis=0, tiled=True)


def per_device(queries, keys, values, out_grad, features, segment_ids):
    ny, nzh, nx, nzl, ncore = (lax.axis_size(a) for a in AXES)
    groups, tps = ny * nzh, nzl * ncore
    tokens = segment_ids.shape[0]
    rows = queries.shape[0]
    span = nx * rows
    g = lax.axis_index(("y", "zh"))
    x = lax.axis_index("x")
    t = lax.axis_index(TP)
    bf16, f32 = jnp.bfloat16, jnp.float32

    kv = spread(jnp.concatenate([keys, values], axis=1), ("y", "zh"), groups)
    kv = kv.reshape(groups * rows, 2 * HD)
    qd = spread(jnp.concatenate([queries, out_grad], axis=1), "x", nx)

    seg_q = lax.dynamic_slice_in_dim(segment_ids, g * span, span, 0)
    ids = jnp.arange(16, dtype=jnp.int32)
    firsts = jnp.sum((segment_ids[None, :] < ids[:, None]).astype(jnp.int32), axis=1)
    start = jnp.sum(jnp.where(seg_q[None, :] == ids[:, None], firsts[:, None], 0), axis=0)
    low = start[0] // span
    scalars = jnp.stack([g, low, x]).astype(jnp.int32)
    start = start.reshape(1, span)

    smem = pl.BlockSpec(memory_space=pltpu.SMEM)
    vmem = pl.BlockSpec(memory_space=pltpu.VMEM)
    params = pltpu.CompilerParams(vmem_limit_bytes=48 * 1024 * 1024)
    stats = pl.pallas_call(
        lambda *refs: stats_kernel(nx, *refs),
        out_shape=jax.ShapeDtypeStruct((3, GROUP, span), f32),
        in_specs=[smem, vmem, vmem, vmem],
        out_specs=vmem,
        compiler_params=params,
    )(scalars, start, qd, kv)
    all_stats = spread(stats, "x", nx)
    dq_part, dv_part = pl.pallas_call(
        lambda *refs: grad_kernel(nx, *refs),
        out_shape=(
            jax.ShapeDtypeStruct((span, GROUP * HD), bf16),
            jax.ShapeDtypeStruct((groups * rows, HD), bf16),
        ),
        in_specs=[smem, vmem, vmem, vmem, vmem],
        out_specs=(vmem, vmem),
        scratch_shapes=[pltpu.VMEM((GROUP, HD, span), f32)],
        compiler_params=params,
    )(scalars, start, all_stats, qd, kv)

    dv = lax.all_to_all(
        dv_part.reshape(groups, rows, HD), ("y", "zh"), split_axis=0, concat_axis=0, tiled=True
    )
    value_b = jnp.sum(dv.astype(f32), axis=0).astype(bf16)
    value_all = lax.all_gather(value_b, TP, axis=1, tiled=True)
    share = features.shape[1] // tps
    own = lax.dynamic_slice_in_dim(features, t * share, share, 1)
    term = lax.dot_general(own, value_all, TN, preferred_element_type=f32)
    ctx = groups * nx
    pieces = lax.all_to_all(
        term.astype(bf16).reshape(ctx, share // ctx, value_all.shape[1]),
        CTX, split_axis=0, concat_axis=0, tiled=True,
    )
    summed = (jnp.sum(pieces.astype(f32), axis=0) * (1.0 / math.sqrt(tokens))).astype(bf16)
    weight_grad = spread(summed, CTX, ctx).reshape(share, value_all.shape[1]).astype(f32)

    dq = lax.all_to_all(
        dq_part.reshape(nx, rows, GROUP * HD), "x", split_axis=0, concat_axis=0, tiled=True
    )
    query_grads = jnp.sum(dq.astype(f32), axis=0).astype(bf16)
    return (query_grads, weight_grad)


def solution(mesh):
    fine = Mesh(mesh.devices.reshape(DIMS), AXES)
    split = P(CTX, TP)
    return jax.shard_map(
        per_device,
        mesh=fine,
        in_specs=(split, split, split, split, P(CTX, None), P()),
        out_specs=(split, P(TP, None)),
        check_vma=False,
    )
```

time: 1450 us -> 230 us (0.16); the launches traced: 1430 us -> 229 us
  waiting for transfers between devices: 826 us -> 93.5 us
  blocking collectives: 453 us -> 60.4 us
  local copies, waits for them, and re-layouts: 63.4 us -> 4.74 us
  starting transfers between devices: 8.71 us -> 57.9 us
  loops' own time: 47.9 us -> 0 us
    reduce_scatter x1 -> x0, waiting for transfers between devices: 519 us -> none  [per_device(): lax.psum_scatter(blocks.reshape(tokens, heads_kv * HD), 'ctx', scatter_di...]
    psum x1 -> x0, blocking collectives: 453 us -> none  [per_device(): summed = lax.psum(own_term, 'ctx')]
    all_gather x2 -> x0, waiting for transfers between devices: 280 us -> none  [the longest x1 143 us: per_device(): lax.all_gather(keys, 'ctx', axis=0, tiled=True)]
    all_to_all x1 -> x5, waiting for transfers between devices: 26.1 us -> 93.5 us  [the longest x3 69.9 us: spread(): return lax.all_to_all(copies, axes, split_axis=0, concat_axis=0, tiled=True)]
    all_to_all x1 -> x5, starting transfers between devices: 8.6 us -> 57.9 us  [the longest x3 33.1 us: spread(): return lax.all_to_all(copies, axes, split_axis=0, concat_axis=0, tiled=True)]
    another operation x18 -> x0, loops' own time: 47.9 us -> none  [the longest x1 21.7 us: per_device(): query_accum, blocks = lax.scan(after_step, zero_grad, starts)]
    all_to_all x0 -> x2, blocking collectives: none -> 47.3 us  [the longest x1 39.1 us: per_device(): lax.all_to_all(term.astype(bf16).reshape(ctx, share // ctx, value_all.sha...]
    dynamic_slice x35 -> x1, local copies, waits for them, and re-layouts: 33.6 us -> 0.08 us  [per_device(): seg_q = lax.dynamic_slice_in_dim(segment_ids, g * span, span, 0)]
  transfers between devices with their start and end apart: 4 -> 5, of which waited for: 4 -> 5; matrix products, arithmetic and copies ran while one was open for 0% -> 1% of each run, Pallas kernels for 0% -> 0%
where the time goes in v1:
time: 230 us; the launch traced here: 229 us
  waiting for transfers between devices  93.5 us (41%)
  blocking collectives  60.4 us (26%)
  starting transfers between devices  57.9 us (25%)
  Pallas kernels  4.81 us (2%)
  local copies, waits for them, and re-layouts  4.74 us (2%)
  other arithmetic  4 us (2%)
  between operations  3.31 us (1%)
    all_to_all x3, waiting for transfers between devices, spread(): return lax.all_to_all(copies, axes, split_axis=0, concat_axis=0, tiled=True)  69.9 us
    all_to_all x1, blocking collectives, per_device(): lax.all_to_all(term.astype(bf16).reshape(ctx, share // ctx, value_all.sha...  39.1 us
    all_to_all x3, starting transfers between devices, spread(): return lax.all_to_all(copies, axes, split_axis=0, concat_axis=0, tiled=True)  33.1 us
    all_to_all x1, starting transfers between devices, per_device(): lax.all_to_all(dv_part.reshape(groups, rows, HD), ('y', 'zh'), split_axis...  20.3 us
    all_to_all x1, waiting for transfers between devices, per_device(): lax.all_to_all(dv_part.reshape(groups, rows, HD), ('y', 'zh'), split_axis...  17.7 us
    all_gather x1, blocking collectives, per_device(): value_all = lax.all_gather(value_b, TP, axis=1, tiled=True)  13.1 us
    all_to_all x1, blocking collectives, spread(): return lax.all_to_all(copies, axes, split_axis=0, concat_axis=0, tiled=True)  8.19 us
    all_to_all x1, waiting for transfers between devices, per_device(): lax.all_to_all(dq_part.reshape(nx, rows, GROUP * HD), 'x', split_axis=0,...  5.84 us
  transfers between devices with their start and end apart: 5, of which 5 were waited for; matrix products, arithmetic and copies ran while one was open for 1% of the time, Pallas kernels for 0%

profile of v1, /device:TPU:6, one launch (start us, length us, event | category | flops | bytes accessed | tf_op | source)
XLA Modules:
  0.0 229.0 jit_solution(14234449629858599230)
XLA Ops:
  0.7 1.1 pad_maximum_fusion
  1.7 1.1 broadcast_in_dim.22
  2.8 9.3 %all-to-all-start = ((bf16[4,128,1024]{2,1,0:T(8,128)(2,1)}), bf16[4,128,1024]{2,1,0:T(8,128)(2,1)S(1)}, u32[]{:S(2)}, u32[]{:S(2)}) async-start(bf16[4,128,1024]{2,1,0:T(8,128)(2,1)} %broadcast_in_dim.22), calls=%async_computation | async-start | bytes 2097152 | tf_op jit(solution)/shard_map/all_to_all | solution.py:119
  12.2 8.8 %all-to-all-done.refs_2_.refs_3_ = bf16[4,128,1024]{2,1,0:T(8,128)(2,1)S(1)} async-done(((bf16[4,128,1024]{2,1,0:T(8,128)(2,1)}), bf16[4,128,1024]{2,1,0:T(8,128)(2,1)S(1)}, u32[]{:S(2)}, u32[]{:S(2)}) %all-to-all-start) | async-done | bytes 1048608 | tf_op jit(solution)/shard_map/all_to_all | solution.py:119
  21.0 1.1 broadcast_in_dim.23
  22.1 15.3 %all-to-all-start.1 = ((bf16[16,128,256]{2,1,0:T(8,128)(2,1)}), bf16[16,128,256]{2,1,0:T(8,128)(2,1)S(1)}, u32[]{:S(2)}, u32[]{:S(2)}) async-start(bf16[16,128,256]{2,1,0:T(8,128)(2,1)} %broadcast_in_dim.23), calls=%async_computation.1 | async-start | bytes 2097152 | tf_op jit(solution)/shard_map/all_to_all | solution.py:119
  37.7 0.6 slice.3
  41.0 32.6 %all-to-all-done.1 = bf16[16,128,256]{2,1,0:T(8,128)(2,1)S(1)} async-done(((bf16[16,128,256]{2,1,0:T(8,128)(2,1)}), bf16[16,128,256]{2,1,0:T(8,128)(2,1)S(1)}, u32[]{:S(2)}, u32[]{:S(2)}) %all-to-all-start.1) | async-done | bytes 1048608 | tf_op jit(solution)/shard_map/all_to_all | solution.py:119
  73.5 1.6 shard_map.77
  75.2 8.2 %all_to_all.35.refs_2_ = f32[4,3,4,512]{3,2,1,0:T(4,128)S(1)} all-to-all(f32[4,3,4,512]{3,2,1,0:T(4,128)S(1)} %broadcast_in_dim.24), channel_id=1, replica_groups=mesh['y'=8,'zh'=2,'x'=4,'zl'=4,'core'=2] {'x'}, dimensions={0} | all-to-all | bytes 196608 | tf_op jit(solution)/shard_map/all_to_all | solution.py:119
  83.4 3.2 %shard_map.78 = (bf16[512,512]{1,0:T(8,128)(2,1)}, bf16[2048,128]{1,0:T(8,128)(2,1)S(1)}) custom-call(s32[3]{0:T(128)S(1)} %pad_add_fusion.refs_0_, s32[1,512]{1,0:T(1,128)S(1)} %bitcast.18, f32[4,3,4,512]{3,2,1,0:T(4,128)S(1)} %all_to_all.35.refs_2_, bf16[4,128,1024]{2,1,0:T(8,128)(2,1)S(1)} %all-to-all-done.refs_2_.refs_3_, bf16[2048,256]{1,0:T(8,128)(2,1)S(1)} %bitcast.15), custom_call_target="tpu_custom_call" | custom-call | tf_op jit(solution)/shard_map/pallas_call | solution.py:156
  86.6 0.8 copy-done.1
  87.3 20.3 %all-to-all-start.4 = ((bf16[16,128,128]{2,1,0:T(8,128)(2,1)}), bf16[16,128,128]{2,1,0:T(8,128)(2,1)S(1)}, u32[]{:S(2)}, u32[]{:S(2)}) async-start(bf16[16,128,128]{2,1,0:T(8,128)(2,1)} %bitcast.16), calls=%async_computation.4 | async-start | bytes 1048576 | tf_op jit(solution)/shard_map/all_to_all | solution.py:168
  107.7 17.7 %all-to-all-done.4 = bf16[16,128,128]{2,1,0:T(8,128)(2,1)S(1)} async-done(((bf16[16,128,128]{2,1,0:T(8,128)(2,1)}), bf16[16,128,128]{2,1,0:T(8,128)(2,1)S(1)}, u32[]{:S(2)}, u32[]{:S(2)}) %all-to-all-start.4) | async-done | bytes 524320 | tf_op jit(solution)/shard_map/all_to_all | solution.py:168
  125.5 13.1 %all_gather.3 = bf16[128,1024]{1,0:T(8,128)(2,1)S(1)} all-gather(bf16[128,128]{1,0:T(8,128)(2,1)S(1)} %reduce_sum.54), channel_id=1, replica_groups=mesh['y'=8,'zh'=2,'x'=4,'zl'=4,'core'=2] {'zl','core'}, dimensions={1}, use_global_device_ids=true | all-gather | bytes 294912 | tf_op jit(solution)/shard_map/all_gather | solution.py:172
  138.6 0.5 fusion
  139.1 39.1 %all_to_all.36 = bf16[64,8,1024]{2,1,0:T(8,128)(2,1)S(1)} all-to-all(bf16[64,8,1024]{2,1,0:T(8,128)(2,1)S(1)} %fusion), channel_id=1, replica_groups=mesh['y'=8,'zh'=2,'x'=4,'zl'=4,'core'=2] {'y','zh','x'}, dimensions={0} | all-to-all | bytes 2097152 | tf_op jit(solution)/shard_map/all_to_all | solution.py:177
  178.1 4.5 %all-to-all-start.3 = ((bf16[4,128,512]{2,1,0:T(8,128)(2,1)}), bf16[4,128,512]{2,1,0:T(8,128)(2,1)S(1)}, u32[]{:S(2)}, u32[]{:S(2)}) async-start(bf16[4,128,512]{2,1,0:T(8,128)(2,1)} %bitcast.6), calls=%async_computation.3 | async-start | bytes 1048576 | tf_op jit(solution)/shard_map/all_to_all | solution.py:184
  182.8 5.8 %all-to-all-done.3 = bf16[4,128,512]{2,1,0:T(8,128)(2,1)S(1)} async-done(((bf16[4,128,512]{2,1,0:T(8,128)(2,1)}), bf16[4,128,512]{2,1,0:T(8,128)(2,1)S(1)}, u32[]{:S(2)}, u32[]{:S(2)}) %all-to-all-start.3) | async-done | bytes 524320 | tf_op jit(solution)/shard_map/all_to_all | solution.py:184
  188.6 1.1 broadcast_in_dim.25
  189.7 8.5 %all-to-all-start.6 = ((bf16[64,8,1024]{2,1,0:T(8,128)(2,1)}), bf16[64,8,1024]{2,1,0:T(8,128)(2,1)S(1)}, u32[]{:S(2)}, u32[]{:S(2)}) async-start(bf16[64,8,1024]{2,1,0:T(8,128)(2,1)} %broadcast_in_dim.25), calls=%async_computation.6 | async-start | bytes 2097152 | tf_op jit(solution)/shard_map/all_to_all | solution.py:119
  198.2 0.7 reduce_sum.53
  199.0 28.5 %all-to-all-done.6 = bf16[64,8,1024]{2,1,0:T(8,128)(2,1)S(1)} async-done(((bf16[64,8,1024]{2,1,0:T(8,128)(2,1)}), bf16[64,8,1024]{2,1,0:T(8,128)(2,1)S(1)}, u32[]{:S(2)}, u32[]{:S(2)}) %all-to-all-start.6) | async-done | bytes 1048608 | tf_op jit(solution)/shard_map/all_to_all | solution.py:119
  227.5 1.6 bitcast_convert_fusion
  (18 shorter events, 0.7 us)
Async XLA Ops:
  0.6 138.0 %copy-start = (bf16[128,4096]{1,0:T(8,128)(2,1)S(1)}, bf16[128,4096]{1,0:T(8,128)(2,1)}, u32[]{:S(2)}) copy-start(bf16[128,4096]{1,0:T(8,128)(2,1)} %param.10) | copy-start | bytes 3145732
  0.6 11.5 %copy-start.3 = (bf16[128,128]{1,0:T(8,128)(2,1)S(1)}, bf16[128,128]{1,0:T(8,128)(2,1)}, u32[]{:S(2)}) copy-start(bf16[128,128]{1,0:T(8,128)(2,1)} %param.8) | copy-start | bytes 98308
  0.7 11.5 %copy-start.4 = (bf16[128,128]{1,0:T(8,128)(2,1)S(1)}, bf16[128,128]{1,0:T(8,128)(2,1)}, u32[]{:S(2)}) copy-start(bf16[128,128]{1,0:T(8,128)(2,1)} %param.7) | copy-start | bytes 98308
  2.8 18.2 %all-to-all-start = ((bf16[4,128,1024]{2,1,0:T(8,128)(2,1)}), bf16[4,128,1024]{2,1,0:T(8,128)(2,1)S(1)}, u32[]{:S(2)}, u32[]{:S(2)}) async-start(bf16[4,128,1024]{2,1,0:T(8,128)(2,1)} %broadcast_in_dim.22), calls=%async_computation | async-start | bytes 2097152 | tf_op jit(solution)/shard_map/all_to_all | solution.py:119
  12.2 25.2 %copy-start.2 = (s32[8192]{0:T(1024)S(1)}, s32[8192]{0:T(1024)}, u32[]{:S(2)}) copy-start(s32[8192]{0:T(1024)} %param.11) | copy-start | bytes 98308
  22.1 51.4 %all-to-all-start.1 = ((bf16[16,128,256]{2,1,0:T(8,128)(2,1)}), bf16[16,128,256]{2,1,0:T(8,128)(2,1)S(1)}, u32[]{:S(2)}, u32[]{:S(2)}) async-start(bf16[16,128,256]{2,1,0:T(8,128)(2,1)} %broadcast_in_dim.23), calls=%async_computation.1 | async-start | bytes 2097152 | tf_op jit(solution)/shard_map/all_to_all | solution.py:119
  86.6 0.8 copy-start.1
  87.3 38.1 %all-to-all-start.4 = ((bf16[16,128,128]{2,1,0:T(8,128)(2,1)}), bf16[16,128,128]{2,1,0:T(8,128)(2,1)S(1)}, u32[]{:S(2)}, u32[]{:S(2)}) async-start(bf16[16,128,128]{2,1,0:T(8,128)(2,1)} %bitcast.16), calls=%async_computation.4 | async-start | bytes 1048576 | tf_op jit(solution)/shard_map/all_to_all | solution.py:168
  178.1 10.5 %all-to-all-start.3 = ((bf16[4,128,512]{2,1,0:T(8,128)(2,1)}), bf16[4,128,512]{2,1,0:T(8,128)(2,1)S(1)}, u32[]{:S(2)}, u32[]{:S(2)}) async-start(bf16[4,128,512]{2,1,0:T(8,128)(2,1)} %bitcast.6), calls=%async_computation.3 | async-start | bytes 1048576 | tf_op jit(solution)/shard_map/all_to_all | solution.py:184
  189.7 37.7 %all-to-all-start.6 = ((bf16[64,8,1024]{2,1,0:T(8,128)(2,1)}), bf16[64,8,1024]{2,1,0:T(8,128)(2,1)S(1)}, u32[]{:S(2)}, u32[]{:S(2)}) async-start(bf16[64,8,1024]{2,1,0:T(8,128)(2,1)} %broadcast_in_dim.25), calls=%async_computation.6 | async-start | bytes 2097152 | tf_op jit(solution)/shard_map/all_to_all | solution.py:119

commit v2 on v1

v2 whole, which is shorter than its diff:
```python
import math

import jax
import jax.numpy as jnp
from jax import lax
from jax.experimental import pallas as pl
from jax.experimental.pallas import tpu as pltpu
from jax.sharding import Mesh, PartitionSpec as P

HD = 128
GROUP = 4
DIMS = (8, 2, 4, 4, 2)
AXES = ("y", "zh", "x", "zl", "core")
CTX = ("y", "zh", "x")
TP = ("zl", "core")
BLOCK = 128
CHUNK = 256
PER = CHUNK // BLOCK
LOW = -1e30
FLOOR = -1e29
SCALE = HD ** (-0.5)
SCALE2 = SCALE * math.log2(math.e)
NT = (((1,), (1,)), ((), ()))
TN = (((0,), (0,)), ((), ()))


def lanes_of(ref_row, places):
    return jnp.concatenate([ref_row[:, pl.ds(p, BLOCK)] for p in places], axis=1)


def places_of(x, nx):
    return [pl.multiple_of(lax.rem(x + nx - d, nx) * BLOCK, BLOCK) for d in range(nx)]


def positions_of(g, x, nx):
    span = nx * BLOCK
    lane = lax.broadcasted_iota(jnp.int32, (1, BLOCK), 1)
    return jnp.concatenate([g * span + p + lane for p in places_of(x, nx)], axis=1)


def chunk_of(j, kv_ref):
    at = pl.ds(pl.multiple_of(j * CHUNK, CHUNK), CHUNK)
    return at, kv_ref[at, 0:HD], kv_ref[at, HD : 2 * HD]


def allowed_in(j, x, nx, pos_q, start):
    r = lax.broadcasted_iota(jnp.int32, (CHUNK, 1), 0)
    pos_k = (j * PER + r // BLOCK) * (nx * BLOCK) + x * BLOCK + r % BLOCK
    return (pos_k <= pos_q) & (pos_k >= start)


def head_of(q_refs, n):
    q = jnp.concatenate([r[:, n * HD : (n + 1) * HD] for r in q_refs], axis=0)
    do = jnp.concatenate([r[:, (GROUP + n) * HD : (GROUP + n + 1) * HD] for r in q_refs], axis=0)
    return q, do


def over_chunks(g, low, high, nx, step):
    width = PER * nx * BLOCK
    first, last = low // width, g // PER
    clear = jnp.minimum((high + width - 1) // width, last)

    def masked(j, carry):
        step(j, True)
        return carry

    def free(j, carry):
        step(j, False)
        return carry

    lax.fori_loop(first, clear, masked, 0)
    lax.fori_loop(clear, last, free, 0)
    step(last, True)


def stats_kernel(nx, sc_ref, start_ref, *refs):
    q_refs, kv_ref, out_ref, st_ref = refs[:nx], refs[nx], refs[-2], refs[-1]
    g, low, high, x = sc_ref[0], sc_ref[1], sc_ref[2], sc_ref[3]
    span = nx * BLOCK
    pos_q = positions_of(g, x, nx)
    start = lanes_of(start_ref, places_of(x, nx))
    st_ref[0] = jnp.full((GROUP, span), FLOOR, jnp.float32)
    st_ref[1] = jnp.zeros((GROUP, span), jnp.float32)
    st_ref[2] = jnp.zeros((GROUP, span), jnp.float32)

    def step(j, masked):
        _, k, v = chunk_of(j, kv_ref)
        if masked:
            allowed = allowed_in(j, x, nx, pos_q, start)
        for n in range(GROUP):
            q, do = head_of(q_refs, n)
            s = lax.dot_general(k, q, NT, preferred_element_type=jnp.float32) * SCALE2
            if masked:
                s = jnp.where(allowed, s, LOW)
            dp = lax.dot_general(v, do, NT, preferred_element_type=jnp.float32)
            m_old = st_ref[0, n : n + 1, :]
            m = jnp.maximum(m_old, jnp.max(s, axis=0, keepdims=True))
            alpha = jnp.exp2(m_old - m)
            w = jnp.exp2(s - m)
            st_ref[0, n : n + 1, :] = m
            st_ref[1, n : n + 1, :] = st_ref[1, n : n + 1, :] * alpha + jnp.sum(
                w, axis=0, keepdims=True
            )
            st_ref[2, n : n + 1, :] = st_ref[2, n : n + 1, :] * alpha + jnp.sum(
                w * dp, axis=0, keepdims=True
            )

    over_chunks(g, low, high, nx, step)
    for d, p in enumerate(places_of(x, nx)):
        for k in range(3):
            out_ref[k, :, pl.ds(p, BLOCK)] = st_ref[k, :, d * BLOCK : (d + 1) * BLOCK]


def grad_kernel(nx, sc_ref, start_ref, st_ref, *refs):
    q_refs, kv_ref = refs[:nx], refs[nx]
    dq_refs, dv_ref, acc_ref = refs[nx + 1 : 2 * nx + 1], refs[2 * nx + 1], refs[2 * nx + 2]
    g, low, high, x = sc_ref[0], sc_ref[1], sc_ref[2], sc_ref[3]
    places = places_of(x, nx)
    pos_q = positions_of(g, x, nx)
    start = lanes_of(start_ref, places)
    acc_ref[...] = jnp.zeros(acc_ref.shape, jnp.float32)
    dv_ref[...] = jnp.zeros(dv_ref.shape, dv_ref.dtype)
    part = [[lanes_of(st_ref.at[i, k], places) for k in range(3)] for i in range(nx)]
    top = part[0][0]
    for i in range(1, nx):
        top = jnp.maximum(top, part[i][0])
    total = jnp.zeros_like(top)
    num = jnp.zeros_like(top)
    for i in range(nx):
        f = jnp.exp2(part[i][0] - top)
        total = total + part[i][1] * f
        num = num + part[i][2] * f
    log_total = top + jnp.log2(total)
    delta = num / total

    def step(j, masked):
        at, k, v = chunk_of(j, kv_ref)
        if masked:
            allowed = allowed_in(j, x, nx, pos_q, start)
        dv = jnp.zeros((CHUNK, HD), jnp.float32)
        for n in range(GROUP):
            q, do = head_of(q_refs, n)
            s = lax.dot_general(k, q, NT, preferred_element_type=jnp.float32) * SCALE2
            if masked:
                s = jnp.where(allowed, s, LOW)
            dp = lax.dot_general(v, do, NT, preferred_element_type=jnp.float32)
            p = jnp.exp2(s - log_total[n : n + 1, :])
            ds = (p * (dp - delta[n : n + 1, :])).astype(jnp.bfloat16)
            dv = dv + jnp.dot(p.astype(jnp.bfloat16), do, preferred_element_type=jnp.float32)
            acc_ref[n] += lax.dot_general(k, ds, TN, preferred_element_type=jnp.float32)
        dv_ref[at, :] = dv.astype(dv_ref.dtype)

    over_chunks(g, low, high, nx, step)
    for n in range(GROUP):
        dq = (acc_ref[n] * SCALE).T.astype(jnp.bfloat16)
        for d in range(nx):
            dq_refs[d][:, n * HD : (n + 1) * HD] = dq[d * BLOCK : (d + 1) * BLOCK]


def regroup_kernel(nx, tps, sc_ref, f_ref, *out_refs):
    x = sc_ref[3]
    share = f_ref.shape[1] // tps
    wide = share // nx
    for d, out_ref in enumerate(out_refs):
        to = lax.rem(x + d, nx) * wide
        for t in range(tps):
            at = pl.multiple_of(t * share + to, wide)
            out_ref[:, t * wide : (t + 1) * wide] = f_ref[:, pl.ds(at, wide)]


def weight_kernel(nx, sc_ref, v_ref, *refs):
    f_refs, out_ref = refs[:nx], refs[nx]
    ny, tps, part, _ = out_ref.shape
    x = sc_ref[3]
    f = jnp.concatenate([r[...] for r in f_refs], axis=0)
    v = jnp.concatenate([v_ref[lax.rem(x + nx - d, nx)] for d in range(nx)], axis=0)
    term = lax.dot_general(v, f, TN, preferred_element_type=jnp.float32).T
    for t in range(tps):
        for y in range(ny):
            at = (t * ny + y) * part
            out_ref[y, t] = term[at : at + part].astype(out_ref.dtype)


def spread(piece, axes, count):
    copies = jnp.broadcast_to(piece[None], (count,) + piece.shape)
    return lax.all_to_all(copies, axes, split_axis=0, concat_axis=0, tiled=True)


def shift(a, axis, by):
    n = lax.axis_size(axis)
    return lax.ppermute(a, axis, [(i, (i + by) % n) for i in range(n)])


def per_device(queries, keys, values, out_grad, features, segment_ids):
    ny, nzh, nx, nzl, ncore = (lax.axis_size(a) for a in AXES)
    groups, tps = ny * nzh, nzl * ncore
    tokens = segment_ids.shape[0]
    rows = queries.shape[0]
    span = nx * rows
    g = lax.axis_index(("y", "zh"))
    x = lax.axis_index("x")
    bf16, f32 = jnp.bfloat16, jnp.float32

    own = jnp.concatenate([queries, out_grad], axis=1)
    qd = [own] + [shift(own, "x", d) for d in range(1, nx)]
    kv = spread(jnp.concatenate([keys, values], axis=1), ("y", "zh"), groups)
    kv = kv.reshape(groups * rows, 2 * HD)

    seg_q = lax.dynamic_slice_in_dim(segment_ids, g * span, span, 0)
    ids = jnp.arange(16, dtype=jnp.int32)
    firsts = jnp.sum((segment_ids[None, :] < ids[:, None]).astype(jnp.int32), axis=1)
    start = jnp.sum(jnp.where(seg_q[None, :] == ids[:, None], firsts[:, None], 0), axis=0)
    scalars = jnp.stack([g, start[0], start[span - 1], x]).astype(jnp.int32)
    start = start.reshape(1, span)

    smem = pl.BlockSpec(memory_space=pltpu.SMEM)
    vmem = pl.BlockSpec(memory_space=pltpu.VMEM)
    params = pltpu.CompilerParams(vmem_limit_bytes=48 * 1024 * 1024)

    wide = features.shape[1] // nx
    mine = pl.pallas_call(
        lambda *refs: regroup_kernel(nx, tps, *refs),
        out_shape=[jax.ShapeDtypeStruct((rows, wide), bf16)] * nx,
        in_specs=[smem, vmem],
        out_specs=[vmem] * nx,
        compiler_params=params,
    )(scalars, features)
    from_x = [mine[0]] + [shift(mine[d], "x", d) for d in range(1, nx)]

    stats = pl.pallas_call(
        lambda *refs: stats_kernel(nx, *refs),
        out_shape=jax.ShapeDtypeStruct((3, GROUP, span), f32),
        in_specs=[smem, vmem] + [vmem] * (nx + 1) + [pl.BlockSpec(memory_space=pl.ANY)] * nx,
        out_specs=vmem,
        scratch_shapes=[pltpu.VMEM((3, GROUP, span), f32)],
        compiler_params=params,
    )(scalars, start, *qd, kv, *from_x)
    all_stats = spread(stats, "x", nx)
    *dq_parts, dv_part = pl.pallas_call(
        lambda *refs: grad_kernel(nx, *refs),
        out_shape=[jax.ShapeDtypeStruct((rows, GROUP * HD), bf16)] * nx
        + [jax.ShapeDtypeStruct((groups * rows, HD), bf16)],
        in_specs=[smem, vmem, vmem] + [vmem] * (nx + 1),
        out_specs=[vmem] * (nx + 1),
        scratch_shapes=[pltpu.VMEM((GROUP, HD, span), f32)],
        compiler_params=params,
    )(scalars, start, all_stats, *qd, kv)

    dv = lax.all_to_all(
        dv_part.reshape(groups, rows, HD), ("y", "zh"), split_axis=0, concat_axis=0, tiled=True
    )
    dq = dq_parts[0].astype(f32)
    for d in range(1, nx):
        dq = dq + shift(dq_parts[d], "x", -d).astype(f32)
    query_grads = dq.astype(bf16)

    value_b = jnp.sum(dv.astype(f32), axis=0).astype(bf16)
    value_x = spread(value_b, "x", nx)
    part = wide // (tps * ny)
    term = pl.pallas_call(
        lambda *refs: weight_kernel(nx, *refs),
        out_shape=jax.ShapeDtypeStruct((ny, tps, part, HD), bf16),
        in_specs=[smem] + [vmem] * (nx + 1),
        out_specs=vmem,
        compiler_params=params,
    )(scalars, value_x, *from_x)
    pieces = lax.all_to_all(term, "y", split_axis=0, concat_axis=0, tiled=True)
    summed = jnp.sum(pieces.astype(f32), axis=0).astype(bf16)
    turned = lax.all_to_all(
        jnp.broadcast_to(summed[None], (nzh,) + summed.shape).reshape(nzh * tps, part, HD),
        ("zh",) + TP, split_axis=0, concat_axis=0, tiled=True,
    ).reshape(nzh, tps, part, HD)
    own_rows = jnp.sum(turned.astype(f32), axis=0) * (1.0 / math.sqrt(tokens))
    own_rows = own_rows.astype(bf16).transpose(1, 0, 2).reshape(part, tps * HD)
    weight_grad = spread(own_rows, ("x", "y"), nx * ny)
    return (query_grads, weight_grad.reshape(wide // tps * nx, tps * HD).astype(f32))


def solution(mesh):
    fine = Mesh(mesh.devices.reshape(DIMS), AXES)
    split = P(CTX, TP)
    return jax.shard_map(
        per_device,
        mesh=fine,
        in_specs=(split, split, split, split, P(CTX, None), P()),
        out_specs=(split, P(TP, None)),
        check_vma=False,
    )
```

time: 230 us -> 180 us (0.78)
  waiting for transfers between devices: 93.5 us -> 33.3 us
  blocking collectives: 60.4 us -> 78.5 us
  starting transfers between devices: 57.9 us -> 50.2 us
  between operations: 3.31 us -> 0.94 us
    all_to_all x3 -> x2, waiting for transfers between devices: 69.9 us -> 14.6 us  [spread(): return lax.all_to_all(copies, axes, split_axis=0, concat_axis=0, tiled=True)]
    ppermute x0 -> x9, starting transfers between devices: none -> 28.7 us  [shift(): return lax.ppermute(a, axis, [(i, (i + by) % n) for i in range(n)])]
    all_to_all x2 -> x0, starting transfers between devices: 24.8 us -> none  [the longest x1 20.3 us: per_device(): lax.all_to_all(dv_part.reshape(groups, rows, HD), ('y', 'zh'), split_axis...]
    all_to_all x2 -> x0, waiting for transfers between devices: 23.6 us -> none  [the longest x1 17.7 us: per_device(): lax.all_to_all(dv_part.reshape(groups, rows, HD), ('y', 'zh'), split_axis...]
    all_to_all x1 -> x3, blocking collectives: 39.1 us -> 61.8 us  [the longest x1 36.6 us: per_device(): lax.all_to_all(dv_part.reshape(groups, rows, HD), ('y', 'zh'), split_axis...]
    ppermute x0 -> x9, waiting for transfers between devices: none -> 18.6 us  [shift(): return lax.ppermute(a, axis, [(i, (i + by) % n) for i in range(n)])]
    all_gather x1 -> x0, blocking collectives: 13.1 us -> none  [per_device(): value_all = lax.all_gather(value_b, TP, axis=1, tiled=True)]
    all_to_all x3 -> x2, starting transfers between devices: 33.1 us -> 21.5 us  [spread(): return lax.all_to_all(copies, axes, split_axis=0, concat_axis=0, tiled=True)]
  transfers between devices with their start and end apart: 5 -> 11, of which waited for: 5 -> 7; matrix products, arithmetic and copies ran while one was open for 1% -> 2% of each run, Pallas kernels for 0% -> 0%
where the time goes in v2:
time: 180 us; the launch traced here: 178 us
  blocking collectives  78.5 us (44%)
  starting transfers between devices  50.2 us (28%)
  waiting for transfers between devices  33.3 us (18%)
  Pallas kernels  5.72 us (3%)
  other arithmetic  4.91 us (3%)
  local copies, waits for them, and re-layouts  4.22 us (2%)
    all_to_all x1, blocking collectives, per_device(): lax.all_to_all(dv_part.reshape(groups, rows, HD), ('y', 'zh'), split_axis...  36.6 us
    ppermute x9, starting transfers between devices, shift(): return lax.ppermute(a, axis, [(i, (i + by) % n) for i in range(n)])  28.7 us
    all_to_all x2, starting transfers between devices, spread(): return lax.all_to_all(copies, axes, split_axis=0, concat_axis=0, tiled=True)  21.5 us
    ppermute x9, waiting for transfers between devices, shift(): return lax.ppermute(a, axis, [(i, (i + by) % n) for i in range(n)])  18.6 us
    all_to_all x2, blocking collectives, spread(): return lax.all_to_all(copies, axes, split_axis=0, concat_axis=0, tiled=True)  16.7 us
    all_to_all x2, waiting for transfers between devices, spread(): return lax.all_to_all(copies, axes, split_axis=0, concat_axis=0, tiled=True)  14.6 us
    all_to_all x1, blocking collectives, per_device(): pieces = lax.all_to_all(term, 'y', split_axis=0, concat_axis=0, tiled=True)  14.5 us
    all_to_all x1, blocking collectives, per_device(): lax.all_to_all(jnp.broadcast_to(summed[None], (nzh,) + summed.shape).resh...  10.7 us
  transfers between devices with their start and end apart: 11, of which 7 were waited for; matrix products, arithmetic and copies ran while one was open for 2% of the time, Pallas kernels for 0%

profile of v2, /device:TPU:6, one launch (start us, length us, event | category | flops | bytes accessed | tf_op | source)
XLA Modules:
  0.0 177.8 jit_solution(12229157143310180663)
XLA Ops:
  2.6 15.6 %all-to-all-start = ((bf16[16,128,256]{2,1,0:T(8,128)(2,1)}), bf16[16,128,256]{2,1,0:T(8,128)(2,1)S(1)}, u32[]{:S(2)}, u32[]{:S(2)}) async-start(bf16[16,128,256]{2,1,0:T(8,128)(2,1)} %broadcast_in_dim.26), calls=%async_computation | async-start | bytes 2097152 | tf_op jit(solution)/shard_map/all_to_all | solution.py:186
  18.3 2.7 %collective-permute-start.2 = (bf16[128,1024]{1,0:T(8,128)(2,1)S(1)}, bf16[128,1024]{1,0:T(8,128)(2,1)S(1)}, u32[]{:S(2)}, u32[]{:S(2)}) collective-permute-start(bf16[128,1024]{1,0:T(8,128)(2,1)S(1)} %constant_dynamic-update-slice_fusion.refs_2_.refs_3_), channel_id=1, source_target_pairs={{0,24},{8,0},{16,8},{24,16},{1,25},{9,1},{17,9},{25,17},{2,26},{10... | collective-permute-start | bytes 786440 | tf_op jit(solution)/shard_map/ppermute | solution.py:191
  21.1 3.0 %collective-permute-start.1 = (bf16[128,1024]{1,0:T(8,128)(2,1)S(1)}, bf16[128,1024]{1,0:T(8,128)(2,1)S(1)}, u32[]{:S(2)}, u32[]{:S(2)}) collective-permute-start(bf16[128,1024]{1,0:T(8,128)(2,1)S(1)} %constant_dynamic-update-slice_fusion.refs_2_.refs_3_), channel_id=1, source_target_pairs={{0,16},{8,24},{16,0},{24,8},{1,17},{9,25},{17,1},{25,9},{2,18},{10... | collective-permute-start | bytes 786440 | tf_op jit(solution)/shard_map/ppermute | solution.py:191
  24.1 4.0 %collective-permute-start = (bf16[128,1024]{1,0:T(8,128)(2,1)S(1)}, bf16[128,1024]{1,0:T(8,128)(2,1)S(1)}, u32[]{:S(2)}, u32[]{:S(2)}) collective-permute-start(bf16[128,1024]{1,0:T(8,128)(2,1)S(1)} %constant_dynamic-update-slice_fusion.refs_2_.refs_3_), channel_id=1, source_target_pairs={{0,8},{8,16},{16,24},{24,0},{1,9},{9,17},{17,25},{25,1},{2,10},{10... | collective-permute-start | bytes 786440 | tf_op jit(solution)/shard_map/ppermute | solution.py:191
  31.2 2.8 %collective-permute-start.3 = (bf16[128,1024]{1,0:T(8,128)(2,1)S(1)}, bf16[128,1024]{1,0:T(8,128)(2,1)S(1)}, u32[]{:S(2)}, u32[]{:S(2)}) collective-permute-start(bf16[128,1024]{1,0:T(8,128)(2,1)S(1)} %get-tuple-element.12), channel_id=1, source_target_pairs={{0,8},{8,16},{16,24},{24,0},{1,9},{9,17},{17,25},{25,1},{2,10},{10... | collective-permute-start | bytes 786440 | tf_op jit(solution)/shard_map/ppermute | solution.py:191
  34.0 3.2 %collective-permute-start.4 = (bf16[128,1024]{1,0:T(8,128)(2,1)S(1)}, bf16[128,1024]{1,0:T(8,128)(2,1)S(1)}, u32[]{:S(2)}, u32[]{:S(2)}) collective-permute-start(bf16[128,1024]{1,0:T(8,128)(2,1)S(1)} %get-tuple-element.13), channel_id=1, source_target_pairs={{0,16},{8,24},{16,0},{24,8},{1,17},{9,25},{17,1},{25,9},{2,18},{10... | collective-permute-start | bytes 786440 | tf_op jit(solution)/shard_map/ppermute | solution.py:191
  37.2 3.3 %collective-permute-start.5 = (bf16[128,1024]{1,0:T(8,128)(2,1)S(1)}, bf16[128,1024]{1,0:T(8,128)(2,1)S(1)}, u32[]{:S(2)}, u32[]{:S(2)}) collective-permute-start(bf16[128,1024]{1,0:T(8,128)(2,1)S(1)} %get-tuple-element.14), channel_id=1, source_target_pairs={{0,24},{8,0},{16,8},{24,16},{1,25},{9,1},{17,9},{25,17},{2,26},{10... | collective-permute-start | bytes 786440 | tf_op jit(solution)/shard_map/ppermute | solution.py:191
  40.5 4.2 %collective-permute-done.3.refs_8_.refs_3_ = bf16[128,1024]{1,0:T(8,128)(2,1)S(1)} collective-permute-done((bf16[128,1024]{1,0:T(8,128)(2,1)S(1)}, bf16[128,1024]{1,0:T(8,128)(2,1)S(1)}, u32[]{:S(2)}, u32[]{:S(2)}) %collective-permute-start.3) | collective-permute-done | bytes 262176 | tf_op jit(solution)/shard_map/ppermute | solution.py:191
  46.3 3.4 %collective-permute-done.5.refs_10_.refs_5_ = bf16[128,1024]{1,0:T(8,128)(2,1)S(1)} collective-permute-done((bf16[128,1024]{1,0:T(8,128)(2,1)S(1)}, bf16[128,1024]{1,0:T(8,128)(2,1)S(1)}, u32[]{:S(2)}, u32[]{:S(2)}) %collective-permute-start.5) | collective-permute-done | bytes 262176 | tf_op jit(solution)/shard_map/ppermute | solution.py:191
  49.7 7.6 %all-to-all-done = bf16[16,128,256]{2,1,0:T(8,128)(2,1)S(1)} async-done(((bf16[16,128,256]{2,1,0:T(8,128)(2,1)}), bf16[16,128,256]{2,1,0:T(8,128)(2,1)S(1)}, u32[]{:S(2)}, u32[]{:S(2)}) %all-to-all-start) | async-done | bytes 1048608 | tf_op jit(solution)/shard_map/all_to_all | solution.py:186
  57.3 1.7 shard_map.78
  59.0 8.3 %all_to_all.35.refs_2_ = f32[4,3,4,512]{3,2,1,0:T(4,128)S(1)} all-to-all(f32[4,3,4,512]{3,2,1,0:T(4,128)S(1)} %broadcast_in_dim.27), channel_id=1, replica_groups=mesh['y'=8,'zh'=2,'x'=4,'zl'=4,'core'=2] {'x'}, dimensions={0} | all-to-all | bytes 196608 | tf_op jit(solution)/shard_map/all_to_all | solution.py:186
  67.3 2.3 %shard_map.79 = (bf16[128,512]{1,0:T(8,128)(2,1)S(1)}, bf16[128,512]{1,0:T(8,128)(2,1)S(1)}, bf16[128,512]{1,0:T(8,128)(2,1)S(1)}, bf16[128,512]{1,0:T(8,128)(2,1)S(1)}, bf16[2048,128]{1,0:T(8,128)(2,1)S(1)}) custom-call(s32[4]{0:T(128)S(1)} %pad_add_fusion.refs_0_, s32[1,512]{1,0:T(1,128)S(1)} %bitcast.21, f32[4,3,4,512]{3,2,1,0:T(4,128)S(1)} %all_to_all.35.refs_2_, ...), custom_call_target="tpu_custom_call" | custom-call | tf_op jit(solution)/shard_map/pallas_call | solution.py:239
  70.8 36.6 %all_to_all.36 = bf16[16,128,128]{2,1,0:T(8,128)(2,1)S(1)} all-to-all(bf16[16,128,128]{2,1,0:T(8,128)(2,1)S(1)} %bitcast.19), channel_id=1, replica_groups=mesh['y'=8,'zh'=2,'x'=4,'zl'=4,'core'=2] {'y','zh'}, dimensions={0} | all-to-all | bytes 1048576 | tf_op jit(solution)/shard_map/all_to_all | solution.py:249
  107.5 8.4 %all_to_all.37.refs_1_ = bf16[4,128,128]{2,1,0:T(8,128)(2,1)S(1)} all-to-all(bf16[4,128,128]{2,1,0:T(8,128)(2,1)S(1)} %broadcast_in_dim.28), channel_id=1, replica_groups=mesh['y'=8,'zh'=2,'x'=4,'zl'=4,'core'=2] {'x'}, dimensions={0} | all-to-all | bytes 262144 | tf_op jit(solution)/shard_map/all_to_all | solution.py:186
  116.9 14.5 %all_to_all.38 = bf16[8,8,16,128]{3,2,1,0:T(8,128)(2,1)S(1)} all-to-all(bf16[8,8,16,128]{3,2,1,0:T(8,128)(2,1)S(1)} %shard_map.80), channel_id=1, replica_groups=mesh['y'=8,'zh'=2,'x'=4,'zl'=4,'core'=2] {'y'}, dimensions={0} | all-to-all | bytes 524288 | tf_op jit(solution)/shard_map/all_to_all | solution.py:267
  131.5 10.7 %all_to_all.39 = bf16[16,16,128]{2,1,0:T(8,128)(2,1)S(1)} all-to-all(bf16[16,16,128]{2,1,0:T(8,128)(2,1)S(1)} %bitcast.22), channel_id=1, replica_groups=mesh['y'=8,'zh'=2,'x'=4,'zl'=4,'core'=2] {'zh','zl','core'}, dimensions={0} | all-to-all | bytes 131072 | tf_op jit(solution)/shard_map/all_to_all | solution.py:269
  143.3 5.8 %all-to-all-start.6 = ((bf16[32,16,1024]{2,1,0:T(8,128)(2,1)}), bf16[32,16,1024]{2,1,0:T(8,128)(2,1)S(1)}, u32[]{:S(2)}, u32[]{:S(2)}) async-start(bf16[32,16,1024]{2,1,0:T(8,128)(2,1)} %broadcast_in_dim.31), calls=%async_computation.6 | async-start | bytes 2097152 | tf_op jit(solution)/shard_map/all_to_all | solution.py:186
  149.2 2.7 %collective-permute-start.6 = (bf16[128,512]{1,0:T(8,128)(2,1)S(1)}, bf16[128,512]{1,0:T(8,128)(2,1)S(1)}, u32[]{:S(2)}, u32[]{:S(2)}) collective-permute-start(bf16[128,512]{1,0:T(8,128)(2,1)S(1)} %copy-done.6), channel_id=1, source_target_pairs={{0,24},{8,0},{16,8},{24,16},{1,25},{9,1},{17,9},{25,17},{2,26},{10... | collective-permute-start | bytes 393224 | tf_op jit(solution)/shard_map/ppermute | solution.py:191
  151.9 2.8 %collective-permute-start.7 = (bf16[128,512]{1,0:T(8,128)(2,1)S(1)}, bf16[128,512]{1,0:T(8,128)(2,1)S(1)}, u32[]{:S(2)}, u32[]{:S(2)}) collective-permute-start(bf16[128,512]{1,0:T(8,128)(2,1)S(1)} %copy-done.4), channel_id=1, source_target_pairs={{0,16},{8,24},{16,0},{24,8},{1,17},{9,25},{17,1},{25,9},{2,18},{10... | collective-permute-start | bytes 393224 | tf_op jit(solution)/shard_map/ppermute | solution.py:191
  154.7 4.2 %collective-permute-start.8 = (bf16[128,512]{1,0:T(8,128)(2,1)S(1)}, bf16[128,512]{1,0:T(8,128)(2,1)S(1)}, u32[]{:S(2)}, u32[]{:S(2)}) collective-permute-start(bf16[128,512]{1,0:T(8,128)(2,1)S(1)} %copy-done.2), channel_id=1, source_target_pairs={{0,8},{8,16},{16,24},{24,0},{1,9},{9,17},{17,25},{25,1},{2,10},{10... | collective-permute-start | bytes 393224 | tf_op jit(solution)/shard_map/ppermute | solution.py:191
  158.9 6.2 %collective-permute-done.6 = bf16[128,512]{1,0:T(8,128)(2,1)S(1)} collective-permute-done((bf16[128,512]{1,0:T(8,128)(2,1)S(1)}, bf16[128,512]{1,0:T(8,128)(2,1)S(1)}, u32[]{:S(2)}, u32[]{:S(2)}) %collective-permute-start.6) | collective-permute-done | bytes 131104 | tf_op jit(solution)/shard_map/ppermute | solution.py:191
  165.1 3.3 %collective-permute-done.8 = bf16[128,512]{1,0:T(8,128)(2,1)S(1)} collective-permute-done((bf16[128,512]{1,0:T(8,128)(2,1)S(1)}, bf16[128,512]{1,0:T(8,128)(2,1)S(1)}, u32[]{:S(2)}, u32[]{:S(2)}) %collective-permute-start.8) | collective-permute-done | bytes 131104 | tf_op jit(solution)/shard_map/ppermute | solution.py:191
  169.2 7.0 %all-to-all-done.6 = bf16[32,16,1024]{2,1,0:T(8,128)(2,1)S(1)} async-done(((bf16[32,16,1024]{2,1,0:T(8,128)(2,1)}), bf16[32,16,1024]{2,1,0:T(8,128)(2,1)S(1)}, u32[]{:S(2)}, u32[]{:S(2)}) %all-to-all-start.6) | async-done | bytes 1048608 | tf_op jit(solution)/shard_map/all_to_all | solution.py:186
  (46 shorter events, 12.5 us)
Async XLA Ops:
  0.6 17.7 %copy-start.7 = (bf16[128,512]{1,0:T(8,128)(2,1)S(1)}, bf16[128,512]{1,0:T(8,128)(2,1)}, u32[]{:S(2)}) copy-start(bf16[128,512]{1,0:T(8,128)(2,1)} %param.6) | copy-start | bytes 393220
  0.6 17.7 %copy-start.8 = (bf16[128,512]{1,0:T(8,128)(2,1)S(1)}, bf16[128,512]{1,0:T(8,128)(2,1)}, u32[]{:S(2)}) copy-start(bf16[128,512]{1,0:T(8,128)(2,1)} %param.9) | copy-start | bytes 393220
  0.7 27.5 %copy-start.9 = (s32[8192]{0:T(1024)S(1)}, s32[8192]{0:T(1024)}, u32[]{:S(2)}) copy-start(s32[8192]{0:T(1024)} %param.11) | copy-start | bytes 98308
  0.7 29.7 %copy-start = (bf16[128,4096]{1,0:T(8,128)(2,1)S(1)}, bf16[128,4096]{1,0:T(8,128)(2,1)}, u32[]{:S(2)}) copy-start(bf16[128,4096]{1,0:T(8,128)(2,1)} %refs_1_.1) | copy-start | bytes 3145732
  2.6 54.6 %all-to-all-start = ((bf16[16,128,256]{2,1,0:T(8,128)(2,1)}), bf16[16,128,256]{2,1,0:T(8,128)(2,1)S(1)}, u32[]{:S(2)}, u32[]{:S(2)}) async-start(bf16[16,128,256]{2,1,0:T(8,128)(2,1)} %broadcast_in_dim.26), calls=%async_computation | async-start | bytes 2097152 | tf_op jit(solution)/shard_map/all_to_all | solution.py:186
  18.3 18.8 %collective-permute-start.2 = (bf16[128,1024]{1,0:T(8,128)(2,1)S(1)}, bf16[128,1024]{1,0:T(8,128)(2,1)S(1)}, u32[]{:S(2)}, u32[]{:S(2)}) collective-permute-start(bf16[128,1024]{1,0:T(8,128)(2,1)S(1)} %constant_dynamic-update-slice_fusion.refs_2_.refs_3_), channel_id=1, source_target_pairs={{0,24},{8,0},{16,8},{24,16},{1,25},{9,1},{17,9},{25,17},{2,26},{10... | collective-permute-start | bytes 786440 | tf_op jit(solution)/shard_map/ppermute | solution.py:191
  21.1 19.4 %collective-permute-start.1 = (bf16[128,1024]{1,0:T(8,128)(2,1)S(1)}, bf16[128,1024]{1,0:T(8,128)(2,1)S(1)}, u32[]{:S(2)}, u32[]{:S(2)}) collective-permute-start(bf16[128,1024]{1,0:T(8,128)(2,1)S(1)} %constant_dynamic-update-slice_fusion.refs_2_.refs_3_), channel_id=1, source_target_pairs={{0,16},{8,24},{16,0},{24,8},{1,17},{9,25},{17,1},{25,9},{2,18},{10... | collective-permute-start | bytes 786440 | tf_op jit(solution)/shard_map/ppermute | solution.py:191
  24.1 16.4 %collective-permute-start = (bf16[128,1024]{1,0:T(8,128)(2,1)S(1)}, bf16[128,1024]{1,0:T(8,128)(2,1)S(1)}, u32[]{:S(2)}, u32[]{:S(2)}) collective-permute-start(bf16[128,1024]{1,0:T(8,128)(2,1)S(1)} %constant_dynamic-update-slice_fusion.refs_2_.refs_3_), channel_id=1, source_target_pairs={{0,8},{8,16},{16,24},{24,0},{1,9},{9,17},{17,25},{25,1},{2,10},{10... | collective-permute-start | bytes 786440 | tf_op jit(solution)/shard_map/ppermute | solution.py:191
  31.2 13.5 %collective-permute-start.3 = (bf16[128,1024]{1,0:T(8,128)(2,1)S(1)}, bf16[128,1024]{1,0:T(8,128)(2,1)S(1)}, u32[]{:S(2)}, u32[]{:S(2)}) collective-permute-start(bf16[128,1024]{1,0:T(8,128)(2,1)S(1)} %get-tuple-element.12), channel_id=1, source_target_pairs={{0,8},{8,16},{16,24},{24,0},{1,9},{9,17},{17,25},{25,1},{2,10},{10... | collective-permute-start | bytes 786440 | tf_op jit(solution)/shard_map/ppermute | solution.py:191
  34.0 12.3 %collective-permute-start.4 = (bf16[128,1024]{1,0:T(8,128)(2,1)S(1)}, bf16[128,1024]{1,0:T(8,128)(2,1)S(1)}, u32[]{:S(2)}, u32[]{:S(2)}) collective-permute-start(bf16[128,1024]{1,0:T(8,128)(2,1)S(1)} %get-tuple-element.13), channel_id=1, source_target_pairs={{0,16},{8,24},{16,0},{24,8},{1,17},{9,25},{17,1},{25,9},{2,18},{10... | collective-permute-start | bytes 786440 | tf_op jit(solution)/shard_map/ppermute | solution.py:191
  37.2 12.5 %collective-permute-start.5 = (bf16[128,1024]{1,0:T(8,128)(2,1)S(1)}, bf16[128,1024]{1,0:T(8,128)(2,1)S(1)}, u32[]{:S(2)}, u32[]{:S(2)}) collective-permute-start(bf16[128,1024]{1,0:T(8,128)(2,1)S(1)} %get-tuple-element.14), channel_id=1, source_target_pairs={{0,24},{8,0},{16,8},{24,16},{1,25},{9,1},{17,9},{25,17},{2,26},{10... | collective-permute-start | bytes 786440 | tf_op jit(solution)/shard_map/ppermute | solution.py:191
  69.6 0.6 copy-start.3
  70.2 0.7 copy-start.5
  70.8 36.7 %copy-start.1 = (bf16[128,512]{1,0:T(8,128)(2,1)}, bf16[128,512]{1,0:T(8,128)(2,1)S(1)}, u32[]{:S(2)}) copy-start(bf16[128,512]{1,0:T(8,128)(2,1)S(1)} %get-tuple-element.18) | copy-start | bytes 393220
  131.4 17.7 %copy-start.6 = (bf16[128,512]{1,0:T(8,128)(2,1)S(1)}, bf16[128,512]{1,0:T(8,128)(2,1)}, u32[]{:S(2)}) copy-start(bf16[128,512]{1,0:T(8,128)(2,1)} %copy-done.5) | copy-start | bytes 393220
  131.4 20.5 %copy-start.4 = (bf16[128,512]{1,0:T(8,128)(2,1)S(1)}, bf16[128,512]{1,0:T(8,128)(2,1)}, u32[]{:S(2)}) copy-start(bf16[128,512]{1,0:T(8,128)(2,1)} %copy-done.3) | copy-start | bytes 393220
  131.4 23.2 %copy-start.2 = (bf16[128,512]{1,0:T(8,128)(2,1)S(1)}, bf16[128,512]{1,0:T(8,128)(2,1)}, u32[]{:S(2)}) copy-start(bf16[128,512]{1,0:T(8,128)(2,1)} %copy-done.1) | copy-start | bytes 393220
  143.3 32.8 %all-to-all-start.6 = ((bf16[32,16,1024]{2,1,0:T(8,128)(2,1)}), bf16[32,16,1024]{2,1,0:T(8,128)(2,1)S(1)}, u32[]{:S(2)}, u32[]{:S(2)}) async-start(bf16[32,16,1024]{2,1,0:T(8,128)(2,1)} %broadcast_in_dim.31), calls=%async_computation.6 | async-start | bytes 2097152 | tf_op jit(solution)/shard_map/all_to_all | solution.py:186
  149.2 15.9 %collective-permute-start.6 = (bf16[128,512]{1,0:T(8,128)(2,1)S(1)}, bf16[128,512]{1,0:T(8,128)(2,1)S(1)}, u32[]{:S(2)}, u32[]{:S(2)}) collective-permute-start(bf16[128,512]{1,0:T(8,128)(2,1)S(1)} %copy-done.6), channel_id=1, source_target_pairs={{0,24},{8,0},{16,8},{24,16},{1,25},{9,1},{17,9},{25,17},{2,26},{10... | collective-permute-start | bytes 393224 | tf_op jit(solution)/shard_map/ppermute | solution.py:191
  151.9 13.2 %collective-permute-start.7 = (bf16[128,512]{1,0:T(8,128)(2,1)S(1)}, bf16[128,512]{1,0:T(8,128)(2,1)S(1)}, u32[]{:S(2)}, u32[]{:S(2)}) collective-permute-start(bf16[128,512]{1,0:T(8,128)(2,1)S(1)} %copy-done.4), channel_id=1, source_target_pairs={{0,16},{8,24},{16,0},{24,8},{1,17},{9,25},{17,1},{25,9},{2,18},{10... | collective-permute-start | bytes 393224 | tf_op jit(solution)/shard_map/ppermute | solution.py:191
  154.7 13.8 %collective-permute-start.8 = (bf16[128,512]{1,0:T(8,128)(2,1)S(1)}, bf16[128,512]{1,0:T(8,128)(2,1)S(1)}, u32[]{:S(2)}, u32[]{:S(2)}) collective-permute-start(bf16[128,512]{1,0:T(8,128)(2,1)S(1)} %copy-done.2), channel_id=1, source_target_pairs={{0,8},{8,16},{16,24},{24,0},{1,9},{9,17},{17,25},{25,1},{2,10},{10... | collective-permute-start | bytes 393224 | tf_op jit(solution)/shard_map/ppermute | solution.py:191

commit v3 on v2

--- a/solution.py
+++ b/solution.py
@@ -108,7 +108,8 @@
     over_chunks(g, low, high, nx, step)
     for d, p in enumerate(places_of(x, nx)):
         for k in range(3):
-            out_ref[k, :, pl.ds(p, BLOCK)] = st_ref[k, :, d * BLOCK : (d + 1) * BLOCK]
+            for i in range(nx):
+                out_ref[i, k, :, pl.ds(p, BLOCK)] = st_ref[k, :, d * BLOCK : (d + 1) * BLOCK]
 
 
 def grad_kernel(nx, sc_ref, start_ref, st_ref, *refs):
@@ -157,7 +158,7 @@
             dq_refs[d][:, n * HD : (n + 1) * HD] = dq[d * BLOCK : (d + 1) * BLOCK]
 
 
-def regroup_kernel(nx, tps, sc_ref, f_ref, *out_refs):
+def regroup_kernel(nx, tps, sc_ref, f_ref, _, *out_refs):
     x = sc_ref[3]
     share = f_ref.shape[1] // tps
     wide = share // nx
@@ -181,9 +182,33 @@
             out_ref[y, t] = term[at : at + part].astype(out_ref.dtype)
 
 
-def spread(piece, axes, count):
-    copies = jnp.broadcast_to(piece[None], (count,) + piece.shape)
-    return lax.all_to_all(copies, axes, split_axis=0, concat_axis=0, tiled=True)
+def pair_kernel(k_ref, v_ref, out_ref):
+    for i in range(out_ref.shape[0]):
+        out_ref[i, :, 0:HD] = k_ref[...]
+        out_ref[i, :, HD : 2 * HD] = v_ref[...]
+
+
+def sum_kernel(in_ref, *refs):
+    out_ref = refs[-1]
+    total = in_ref[0].astype(jnp.float32)
+    for i in range(1, in_ref.shape[0]):
+        total = total + in_ref[i].astype(jnp.float32)
+    total = total.astype(out_ref.dtype)
+    for i in range(out_ref.shape[0]):
+        out_ref[i] = total
+
+
+def turn_kernel(nzh, factor, in_ref, out_ref):
+    tps = in_ref.shape[0] // nzh
+    parts = []
+    for t in range(tps):
+        total = in_ref[t].astype(jnp.float32)
+        for i in range(1, nzh):
+            total = total + in_ref[i * tps + t].astype(jnp.float32)
+        parts.append((total * factor).astype(out_ref.dtype))
+    whole = jnp.concatenate(parts, axis=1)
+    for i in range(out_ref.shape[0]):
+        out_ref[i] = whole
 
 
 def shift(a, axis, by):
@@ -201,9 +226,21 @@
     x = lax.axis_index("x")
     bf16, f32 = jnp.bfloat16, jnp.float32
 
+    smem = pl.BlockSpec(memory_space=pltpu.SMEM)
+    vmem = pl.BlockSpec(memory_space=pltpu.VMEM)
+    unread = pl.BlockSpec(memory_space=pl.ANY)
+    params = pltpu.CompilerParams(vmem_limit_bytes=20 * 1024 * 1024)
+
     own = jnp.concatenate([queries, out_grad], axis=1)
     qd = [own] + [shift(own, "x", d) for d in range(1, nx)]
-    kv = spread(jnp.concatenate([keys, values], axis=1), ("y", "zh"), groups)
+    kv_copies = pl.pallas_call(
+        pair_kernel,
+        out_shape=jax.ShapeDtypeStruct((groups, rows, 2 * HD), bf16),
+        in_specs=[vmem, vmem],
+        out_specs=vmem,
+        compiler_params=params,
+    )(keys, values)
+    kv = lax.all_to_all(kv_copies, ("y", "zh"), split_axis=0, concat_axis=0, tiled=True)
     kv = kv.reshape(groups * rows, 2 * HD)
 
     seg_q = lax.dynamic_slice_in_dim(segment_ids, g * span, span, 0)
@@ -213,29 +250,15 @@
     scalars = jnp.stack([g, start[0], start[span - 1], x]).astype(jnp.int32)
     start = start.reshape(1, span)
 
-    smem = pl.BlockSpec(memory_space=pltpu.SMEM)
-    vmem = pl.BlockSpec(memory_space=pltpu.VMEM)
-    params = pltpu.CompilerParams(vmem_limit_bytes=48 * 1024 * 1024)
-
-    wide = features.shape[1] // nx
-    mine = pl.pallas_call(
-        lambda *refs: regroup_kernel(nx, tps, *refs),
-        out_shape=[jax.ShapeDtypeStruct((rows, wide), bf16)] * nx,
-        in_specs=[smem, vmem],
-        out_specs=[vmem] * nx,
-        compiler_params=params,
-    )(scalars, features)
-    from_x = [mine[0]] + [shift(mine[d], "x", d) for d in range(1, nx)]
-
     stats = pl.pallas_call(
         lambda *refs: stats_kernel(nx, *refs),
-        out_shape=jax.ShapeDtypeStruct((3, GROUP, span), f32),
-        in_specs=[smem, vmem] + [vmem] * (nx + 1) + [pl.BlockSpec(memory_space=pl.ANY)] * nx,
+        out_shape=jax.ShapeDtypeStruct((nx, 3, GROUP, span), f32),
+        in_specs=[smem, vmem] + [vmem] * (nx + 1),
         out_specs=vmem,
         scratch_shapes=[pltpu.VMEM((3, GROUP, span), f32)],
         compiler_params=params,
-    )(scalars, start, *qd, kv, *from_x)
-    all_stats = spread(stats, "x", nx)
+    )(scalars, start, *qd, kv)
+    all_stats = lax.all_to_all(stats, "x", split_axis=0, concat_axis=0, tiled=True)
     *dq_parts, dv_part = pl.pallas_call(
         lambda *refs: grad_kernel(nx, *refs),
         out_shape=[jax.ShapeDtypeStruct((rows, GROUP * HD), bf16)] * nx
@@ -249,13 +272,23 @@
     dv = lax.all_to_all(
         dv_part.reshape(groups, rows, HD), ("y", "zh"), split_axis=0, concat_axis=0, tiled=True
     )
-    dq = dq_parts[0].astype(f32)
-    for d in range(1, nx):
-        dq = dq + shift(dq_parts[d], "x", -d).astype(f32)
-    query_grads = dq.astype(bf16)
-
-    value_b = jnp.sum(dv.astype(f32), axis=0).astype(bf16)
-    value_x = spread(value_b, "x", nx)
+    wide = features.shape[1] // nx
+    mine = pl.pallas_call(
+        lambda *refs: regroup_kernel(nx, tps, *refs),
+        out_shape=[jax.ShapeDtypeStruct((rows, wide), bf16)] * nx,
+        in_specs=[smem, vmem, unread],
+        out_specs=[vmem] * nx,
+        compiler_params=params,
+    )(scalars, features, dv_part)
+    from_x = [mine[0]] + [shift(mine[d], "x", d) for d in range(1, nx)]
+    value_copies = pl.pallas_call(
+        sum_kernel,
+        out_shape=jax.ShapeDtypeStruct((nx, rows, HD), bf16),
+        in_specs=[vmem] + [unread] * nx,
+        out_specs=vmem,
+        compiler_params=params,
+    )(dv, *from_x)
+    value_x = lax.all_to_all(value_copies, "x", split_axis=0, concat_axis=0, tiled=True)
     part = wide // (tps * ny)
     term = pl.pallas_call(
         lambda *refs: weight_kernel(nx, *refs),
@@ -265,14 +298,30 @@
         compiler_params=params,
     )(scalars, value_x, *from_x)
     pieces = lax.all_to_all(term, "y", split_axis=0, concat_axis=0, tiled=True)
-    summed = jnp.sum(pieces.astype(f32), axis=0).astype(bf16)
+    row_copies = pl.pallas_call(
+        sum_kernel,
+        out_shape=jax.ShapeDtypeStruct((nzh, tps, part, HD), bf16),
+        in_specs=[vmem],
+        out_specs=vmem,
+        compiler_params=params,
+    )(pieces)
     turned = lax.all_to_all(
-        jnp.broadcast_to(summed[None], (nzh,) + summed.shape).reshape(nzh * tps, part, HD),
+        row_copies.reshape(nzh * tps, part, HD),
         ("zh",) + TP, split_axis=0, concat_axis=0, tiled=True,
-    ).reshape(nzh, tps, part, HD)
-    own_rows = jnp.sum(turned.astype(f32), axis=0) * (1.0 / math.sqrt(tokens))
-    own_rows = own_rows.astype(bf16).transpose(1, 0, 2).reshape(part, tps * HD)
-    weight_grad = spread(own_rows, ("x", "y"), nx * ny)
+    )
+    final_copies = pl.pallas_call(
+        lambda *refs: turn_kernel(nzh, 1.0 / math.sqrt(tokens), *refs),
+        out_shape=jax.ShapeDtypeStruct((nx * ny, part, tps * HD), bf16),
+        in_specs=[vmem],
+        out_specs=vmem,
+        compiler_params=params,
+    )(turned)
+    weight_grad = lax.all_to_all(final_copies, ("x", "y"), split_axis=0, concat_axis=0, tiled=True)
+
+    dq = dq_parts[0].astype(f32)
+    for d in range(1, nx):
+        dq = dq + shift(dq_parts[d], "x", -d).astype(f32)
+    query_grads = dq.astype(bf16)
     return (query_grads, weight_grad.reshape(wide // tps * nx, tps * HD).astype(f32))
 
 

time: 180 us -> 187 us (1.039)
  blocking collectives: 78.5 us -> 48.4 us
  starting transfers between devices: 50.2 us -> 68.3 us
  waiting for transfers between devices: 33.3 us -> 50.9 us
  Pallas kernels: 5.72 us -> 8.72 us
    all_to_all x4 -> x3, blocking collectives: 64 us -> 31.1 us  [the longest x1 14.4 us: per_device(): lax.all_to_all(row_copies.reshape(nzh * tps, part, HD), ('zh',) + TP, spl...]
    all_to_all x2 -> x3, starting transfers between devices: 21.5 us -> 39.6 us  [the longest x1 18.1 us: per_device(): lax.all_to_all(dv_part.reshape(groups, rows, HD), ('y', 'zh'), split_axis...]
    all_to_all x2 -> x3, waiting for transfers between devices: 14.6 us -> 27 us  [the longest x1 19.9 us: per_device(): lax.all_to_all(kv_copies, ('y', 'zh'), split_axis=0, concat_axis=0, tiled...]
    ppermute x9, waiting for transfers between devices: 18.6 us -> 24 us  [shift(): return lax.ppermute(a, axis, [(i, (i + by) % n) for i in range(n)])]
    all_to_all x1, blocking collectives: 14.5 us -> 17.3 us  [per_device(): pieces = lax.all_to_all(term, 'y', split_axis=0, concat_axis=0, tiled=True)]
    pallas_call x0 -> x4, Pallas kernels: none -> 2.31 us  [the longest x1 1.1 us: per_device(): pl.pallas_call(pair_kernel, out_shape=jax.ShapeDtypeStruct((groups, rows,...]
    broadcast_in_dim x5 -> x0, local copies, waits for them, and re-layouts: 2.21 us -> none  [the longest x4 2.2 us: spread(): copies = jnp.broadcast_to(piece[None], (count,) + piece.shape)]
  transfers between devices with their start and end apart: 11 -> 12, of which waited for: 7 -> 8; matrix products, arithmetic and copies ran while one was open for 2% -> 2% of each run, Pallas kernels for 0% -> 0%
where the time goes in v3:
time: 187 us; the launch traced here: 184 us
  starting transfers between devices  68.3 us (37%)
  waiting for transfers between devices  50.9 us (27%)
  blocking collectives  48.4 us (26%)
  Pallas kernels  8.72 us (5%)
  other arithmetic  3.95 us (2%)
  local copies, waits for them, and re-layouts  2.91 us (2%)
    ppermute x9, starting transfers between devices, shift(): return lax.ppermute(a, axis, [(i, (i + by) % n) for i in range(n)])  28.7 us
    ppermute x9, waiting for transfers between devices, shift(): return lax.ppermute(a, axis, [(i, (i + by) % n) for i in range(n)])  24 us
    all_to_all x1, waiting for transfers between devices, per_device(): lax.all_to_all(kv_copies, ('y', 'zh'), split_axis=0, concat_axis=0, tiled...  19.9 us
    all_to_all x1, starting transfers between devices, per_device(): lax.all_to_all(dv_part.reshape(groups, rows, HD), ('y', 'zh'), split_axis...  18.1 us
    all_to_all x1, blocking collectives, per_device(): pieces = lax.all_to_all(term, 'y', split_axis=0, concat_axis=0, tiled=True)  17.3 us
    all_to_all x1, starting transfers between devices, per_device(): lax.all_to_all(kv_copies, ('y', 'zh'), split_axis=0, concat_axis=0, tiled...  15.6 us
    all_to_all x1, blocking collectives, per_device(): lax.all_to_all(row_copies.reshape(nzh * tps, part, HD), ('zh',) + TP, spl...  14.4 us
    all_to_all x1, blocking collectives, per_device(): lax.all_to_all(stats, 'x', split_axis=0, concat_axis=0, tiled=True)  8.44 us
  transfers between devices with their start and end apart: 12, of which 8 were waited for; matrix products, arithmetic and copies ran while one was open for 2% of the time, Pallas kernels for 0%

profile of v3, /device:TPU:6, one launch (start us, length us, event | category | flops | bytes accessed | tf_op | source)
XLA Modules:
  0.0 184.0 jit_solution(11449397978796190502)
XLA Ops:
  3.3 15.6 %all-to-all-start = ((bf16[16,128,256]{2,1,0:T(8,128)(2,1)}), bf16[16,128,256]{2,1,0:T(8,128)(2,1)S(1)}, u32[]{:S(2)}, u32[]{:S(2)}) async-start(bf16[16,128,256]{2,1,0:T(8,128)(2,1)} %shard_map.77), calls=%async_computation | async-start | bytes 2097152 | tf_op jit(solution)/shard_map/all_to_all | solution.py:243
  19.0 2.7 %collective-permute-start.2 = (bf16[128,1024]{1,0:T(8,128)(2,1)S(1)}, bf16[128,1024]{1,0:T(8,128)(2,1)S(1)}, u32[]{:S(2)}, u32[]{:S(2)}) collective-permute-start(bf16[128,1024]{1,0:T(8,128)(2,1)S(1)} %constant_dynamic-update-slice_fusion.refs_2_.refs_3_), channel_id=1, source_target_pairs={{0,24},{8,0},{16,8},{24,16},{1,25},{9,1},{17,9},{25,17},{2,26},{10... | collective-permute-start | bytes 786440 | tf_op jit(solution)/shard_map/ppermute | solution.py:216
  21.7 3.0 %collective-permute-start.1 = (bf16[128,1024]{1,0:T(8,128)(2,1)S(1)}, bf16[128,1024]{1,0:T(8,128)(2,1)S(1)}, u32[]{:S(2)}, u32[]{:S(2)}) collective-permute-start(bf16[128,1024]{1,0:T(8,128)(2,1)S(1)} %constant_dynamic-update-slice_fusion.refs_2_.refs_3_), channel_id=1, source_target_pairs={{0,16},{8,24},{16,0},{24,8},{1,17},{9,25},{17,1},{25,9},{2,18},{10... | collective-permute-start | bytes 786440 | tf_op jit(solution)/shard_map/ppermute | solution.py:216
  24.7 4.0 %collective-permute-start = (bf16[128,1024]{1,0:T(8,128)(2,1)S(1)}, bf16[128,1024]{1,0:T(8,128)(2,1)S(1)}, u32[]{:S(2)}, u32[]{:S(2)}) collective-permute-start(bf16[128,1024]{1,0:T(8,128)(2,1)S(1)} %constant_dynamic-update-slice_fusion.refs_2_.refs_3_), channel_id=1, source_target_pairs={{0,8},{8,16},{16,24},{24,0},{1,9},{9,17},{17,25},{25,1},{2,10},{10... | collective-permute-start | bytes 786440 | tf_op jit(solution)/shard_map/ppermute | solution.py:216
  31.1 4.4 %collective-permute-done.2.refs_5_.refs_6_ = bf16[128,1024]{1,0:T(8,128)(2,1)S(1)} collective-permute-done((bf16[128,1024]{1,0:T(8,128)(2,1)S(1)}, bf16[128,1024]{1,0:T(8,128)(2,1)S(1)}, u32[]{:S(2)}, u32[]{:S(2)}) %collective-permute-start.2) | collective-permute-done | bytes 262176 | tf_op jit(solution)/shard_map/ppermute | solution.py:216
  35.5 2.5 %collective-permute-done.refs_3_.refs_4_ = bf16[128,1024]{1,0:T(8,128)(2,1)S(1)} collective-permute-done((bf16[128,1024]{1,0:T(8,128)(2,1)S(1)}, bf16[128,1024]{1,0:T(8,128)(2,1)S(1)}, u32[]{:S(2)}, u32[]{:S(2)}) %collective-permute-start) | collective-permute-done | bytes 262176 | tf_op jit(solution)/shard_map/ppermute | solution.py:216
  38.0 19.9 %all-to-all-done = bf16[16,128,256]{2,1,0:T(8,128)(2,1)S(1)} async-done(((bf16[16,128,256]{2,1,0:T(8,128)(2,1)}), bf16[16,128,256]{2,1,0:T(8,128)(2,1)S(1)}, u32[]{:S(2)}, u32[]{:S(2)}) %all-to-all-start) | async-done | bytes 1048608 | tf_op jit(solution)/shard_map/all_to_all | solution.py:243
  59.6 8.4 %all_to_all.35.refs_2_ = f32[4,3,4,512]{3,2,1,0:T(4,128)S(1)} all-to-all(f32[4,3,4,512]{3,2,1,0:T(4,128)S(1)} %shard_map.78), channel_id=1, replica_groups=mesh['y'=8,'zh'=2,'x'=4,'zl'=4,'core'=2] {'x'}, dimensions={0} | all-to-all | bytes 196608 | tf_op jit(solution)/shard_map/all_to_all | solution.py:261
  68.0 2.9 %shard_map.79 = (bf16[128,512]{1,0:T(8,128)(2,1)S(1)}, bf16[128,512]{1,0:T(8,128)(2,1)S(1)}, bf16[128,512]{1,0:T(8,128)(2,1)S(1)}, bf16[128,512]{1,0:T(8,128)(2,1)S(1)}, bf16[2048,128]{1,0:T(8,128)(2,1)}) custom-call(s32[4]{0:T(128)S(1)} %pad_add_fusion.refs_0_, s32[1,512]{1,0:T(1,128)S(1)} %bitcast.13, f32[4,3,4,512]{3,2,1,0:T(4,128)S(1)} %all_to_all.35.refs_2_, ...), custom_call_target="tpu_custom_call" | custom-call | tf_op jit(solution)/shard_map/pallas_call | solution.py:262
  71.6 18.1 %all-to-all-start.2 = ((bf16[16,128,128]{2,1,0:T(8,128)(2,1)}), bf16[16,128,128]{2,1,0:T(8,128)(2,1)S(1)}, u32[]{:S(2)}, u32[]{:S(2)}) async-start(bf16[16,128,128]{2,1,0:T(8,128)(2,1)} %bitcast.4), calls=%async_computation.2 | async-start | bytes 1048576 | tf_op jit(solution)/shard_map/all_to_all | solution.py:272
  90.6 4.0 %collective-permute-start.6 = (bf16[128,1024]{1,0:T(8,128)(2,1)S(1)}, bf16[128,1024]{1,0:T(8,128)(2,1)S(1)}, u32[]{:S(2)}, u32[]{:S(2)}) collective-permute-start(bf16[128,1024]{1,0:T(8,128)(2,1)S(1)} %get-tuple-element.17), channel_id=1, source_target_pairs={{0,8},{8,16},{16,24},{24,0},{1,9},{9,17},{17,25},{25,1},{2,10},{10... | collective-permute-start | bytes 786440 | tf_op jit(solution)/shard_map/ppermute | solution.py:216
  96.8 3.0 %collective-permute-start.8 = (bf16[128,1024]{1,0:T(8,128)(2,1)S(1)}, bf16[128,1024]{1,0:T(8,128)(2,1)S(1)}, u32[]{:S(2)}, u32[]{:S(2)}) collective-permute-start(bf16[128,1024]{1,0:T(8,128)(2,1)S(1)} %get-tuple-element.19), channel_id=1, source_target_pairs={{0,24},{8,0},{16,8},{24,16},{1,25},{9,1},{17,9},{25,17},{2,26},{10... | collective-permute-start | bytes 786440 | tf_op jit(solution)/shard_map/ppermute | solution.py:216
  99.9 4.9 %collective-permute-done.7.refs_2_.refs_4_ = bf16[128,1024]{1,0:T(8,128)(2,1)S(1)} collective-permute-done((bf16[128,1024]{1,0:T(8,128)(2,1)S(1)}, bf16[128,1024]{1,0:T(8,128)(2,1)S(1)}, u32[]{:S(2)}, u32[]{:S(2)}) %collective-permute-start.7) | collective-permute-done | bytes 262176 | tf_op jit(solution)/shard_map/ppermute | solution.py:216
  104.7 2.7 %collective-permute-done.8.refs_3_.refs_5_ = bf16[128,1024]{1,0:T(8,128)(2,1)S(1)} collective-permute-done((bf16[128,1024]{1,0:T(8,128)(2,1)S(1)}, bf16[128,1024]{1,0:T(8,128)(2,1)S(1)}, u32[]{:S(2)}, u32[]{:S(2)}) %collective-permute-start.8) | collective-permute-done | bytes 262176 | tf_op jit(solution)/shard_map/ppermute | solution.py:216
  107.5 8.2 %all_to_all.36.refs_1_ = bf16[4,128,128]{2,1,0:T(8,128)(2,1)S(1)} all-to-all(bf16[4,128,128]{2,1,0:T(8,128)(2,1)S(1)} %shard_map.81), channel_id=1, replica_groups=mesh['y'=8,'zh'=2,'x'=4,'zl'=4,'core'=2] {'x'}, dimensions={0} | all-to-all | bytes 262144 | tf_op jit(solution)/shard_map/all_to_all | solution.py:291
  116.7 17.3 %all_to_all.37.in_ref = bf16[8,8,16,128]{3,2,1,0:T(8,128)(2,1)S(1)} all-to-all(bf16[8,8,16,128]{3,2,1,0:T(8,128)(2,1)S(1)} %shard_map.82), channel_id=1, replica_groups=mesh['y'=8,'zh'=2,'x'=4,'zl'=4,'core'=2] {'y'}, dimensions={0} | all-to-all | bytes 524288 | tf_op jit(solution)/shard_map/all_to_all | solution.py:300
  134.0 14.4 %all_to_all.38.refs_0_ = bf16[16,16,128]{2,1,0:T(8,128)(2,1)S(1)} all-to-all(bf16[16,16,128]{2,1,0:T(8,128)(2,1)S(1)} %bitcast.11), channel_id=1, replica_groups=mesh['y'=8,'zh'=2,'x'=4,'zl'=4,'core'=2] {'zh','zl','core'}, dimensions={0} | all-to-all | bytes 131072 | tf_op jit(solution)/shard_map/all_to_all | solution.py:308
  149.5 5.8 %all-to-all-start.6 = ((bf16[32,16,1024]{2,1,0:T(8,128)(2,1)}), bf16[32,16,1024]{2,1,0:T(8,128)(2,1)S(1)}, u32[]{:S(2)}, u32[]{:S(2)}) async-start(bf16[32,16,1024]{2,1,0:T(8,128)(2,1)} %shard_map.84), calls=%async_computation.6 | async-start | bytes 2097152 | tf_op jit(solution)/shard_map/all_to_all | solution.py:319
  155.4 2.7 %collective-permute-start.3 = (bf16[128,512]{1,0:T(8,128)(2,1)S(1)}, bf16[128,512]{1,0:T(8,128)(2,1)S(1)}, u32[]{:S(2)}, u32[]{:S(2)}) collective-permute-start(bf16[128,512]{1,0:T(8,128)(2,1)S(1)} %copy-done.4), channel_id=1, source_target_pairs={{0,24},{8,0},{16,8},{24,16},{1,25},{9,1},{17,9},{25,17},{2,26},{10... | collective-permute-start | bytes 393224 | tf_op jit(solution)/shard_map/ppermute | solution.py:216
  158.1 2.8 %collective-permute-start.4 = (bf16[128,512]{1,0:T(8,128)(2,1)S(1)}, bf16[128,512]{1,0:T(8,128)(2,1)S(1)}, u32[]{:S(2)}, u32[]{:S(2)}) collective-permute-start(bf16[128,512]{1,0:T(8,128)(2,1)S(1)} %get-tuple-element.13), channel_id=1, source_target_pairs={{0,16},{8,24},{16,0},{24,8},{1,17},{9,25},{17,1},{25,9},{2,18},{10... | collective-permute-start | bytes 393224 | tf_op jit(solution)/shard_map/ppermute | solution.py:216
  160.8 4.2 %collective-permute-start.5 = (bf16[128,512]{1,0:T(8,128)(2,1)S(1)}, bf16[128,512]{1,0:T(8,128)(2,1)S(1)}, u32[]{:S(2)}, u32[]{:S(2)}) collective-permute-start(bf16[128,512]{1,0:T(8,128)(2,1)S(1)} %get-tuple-element.14), channel_id=1, source_target_pairs={{0,8},{8,16},{16,24},{24,0},{1,9},{9,17},{17,25},{25,1},{2,10},{10... | collective-permute-start | bytes 393224 | tf_op jit(solution)/shard_map/ppermute | solution.py:216
  165.1 6.2 %collective-permute-done.3 = bf16[128,512]{1,0:T(8,128)(2,1)S(1)} collective-permute-done((bf16[128,512]{1,0:T(8,128)(2,1)S(1)}, bf16[128,512]{1,0:T(8,128)(2,1)S(1)}, u32[]{:S(2)}, u32[]{:S(2)}) %collective-permute-start.3) | collective-permute-done | bytes 131104 | tf_op jit(solution)/shard_map/ppermute | solution.py:216
  171.3 3.3 %collective-permute-done.5 = bf16[128,512]{1,0:T(8,128)(2,1)S(1)} collective-permute-done((bf16[128,512]{1,0:T(8,128)(2,1)S(1)}, bf16[128,512]{1,0:T(8,128)(2,1)S(1)}, u32[]{:S(2)}, u32[]{:S(2)}) %collective-permute-start.5) | collective-permute-done | bytes 131104 | tf_op jit(solution)/shard_map/ppermute | solution.py:216
  175.3 7.0 %all-to-all-done.6 = bf16[32,16,1024]{2,1,0:T(8,128)(2,1)S(1)} async-done(((bf16[32,16,1024]{2,1,0:T(8,128)(2,1)}), bf16[32,16,1024]{2,1,0:T(8,128)(2,1)S(1)}, u32[]{:S(2)}, u32[]{:S(2)}) %all-to-all-start.6) | async-done | bytes 1048608 | tf_op jit(solution)/shard_map/all_to_all | solution.py:319
  (37 shorter events, 14.9 us)
Async XLA Ops:
  0.6 0.8 copy-start.1
  1.4 0.8 copy-start.2
  2.1 16.8 %copy-start.5 = (bf16[128,512]{1,0:T(8,128)(2,1)S(1)}, bf16[128,512]{1,0:T(8,128)(2,1)}, u32[]{:S(2)}) copy-start(bf16[128,512]{1,0:T(8,128)(2,1)} %param.6) | copy-start | bytes 393220
  2.2 16.8 %copy-start.6 = (bf16[128,512]{1,0:T(8,128)(2,1)S(1)}, bf16[128,512]{1,0:T(8,128)(2,1)}, u32[]{:S(2)}) copy-start(bf16[128,512]{1,0:T(8,128)(2,1)} %param.9) | copy-start | bytes 393220
  2.2 26.6 %copy-start.7 = (s32[8192]{0:T(1024)S(1)}, s32[8192]{0:T(1024)}, u32[]{:S(2)}) copy-start(s32[8192]{0:T(1024)} %param.11) | copy-start | bytes 98308
  3.3 54.6 %all-to-all-start = ((bf16[16,128,256]{2,1,0:T(8,128)(2,1)}), bf16[16,128,256]{2,1,0:T(8,128)(2,1)S(1)}, u32[]{:S(2)}, u32[]{:S(2)}) async-start(bf16[16,128,256]{2,1,0:T(8,128)(2,1)} %shard_map.77), calls=%async_computation | async-start | bytes 2097152 | tf_op jit(solution)/shard_map/all_to_all | solution.py:243
  19.0 16.5 %collective-permute-start.2 = (bf16[128,1024]{1,0:T(8,128)(2,1)S(1)}, bf16[128,1024]{1,0:T(8,128)(2,1)S(1)}, u32[]{:S(2)}, u32[]{:S(2)}) collective-permute-start(bf16[128,1024]{1,0:T(8,128)(2,1)S(1)} %constant_dynamic-update-slice_fusion.refs_2_.refs_3_), channel_id=1, source_target_pairs={{0,24},{8,0},{16,8},{24,16},{1,25},{9,1},{17,9},{25,17},{2,26},{10... | collective-permute-start | bytes 786440 | tf_op jit(solution)/shard_map/ppermute | solution.py:216
  21.7 13.7 %collective-permute-start.1 = (bf16[128,1024]{1,0:T(8,128)(2,1)S(1)}, bf16[128,1024]{1,0:T(8,128)(2,1)S(1)}, u32[]{:S(2)}, u32[]{:S(2)}) collective-permute-start(bf16[128,1024]{1,0:T(8,128)(2,1)S(1)} %constant_dynamic-update-slice_fusion.refs_2_.refs_3_), channel_id=1, source_target_pairs={{0,16},{8,24},{16,0},{24,8},{1,17},{9,25},{17,1},{25,9},{2,18},{10... | collective-permute-start | bytes 786440 | tf_op jit(solution)/shard_map/ppermute | solution.py:216
  24.7 13.2 %collective-permute-start = (bf16[128,1024]{1,0:T(8,128)(2,1)S(1)}, bf16[128,1024]{1,0:T(8,128)(2,1)S(1)}, u32[]{:S(2)}, u32[]{:S(2)}) collective-permute-start(bf16[128,1024]{1,0:T(8,128)(2,1)S(1)} %constant_dynamic-update-slice_fusion.refs_2_.refs_3_), channel_id=1, source_target_pairs={{0,8},{8,16},{16,24},{24,0},{1,9},{9,17},{17,25},{25,1},{2,10},{10... | collective-permute-start | bytes 786440 | tf_op jit(solution)/shard_map/ppermute | solution.py:216
  59.6 30.2 %copy-start = (bf16[128,4096]{1,0:T(8,128)(2,1)S(1)}, bf16[128,4096]{1,0:T(8,128)(2,1)}, u32[]{:S(2)}) copy-start(bf16[128,4096]{1,0:T(8,128)(2,1)} %refs_1_.1) | copy-start | bytes 3145732
  71.0 0.7 copy-start.3
  71.6 35.8 %all-to-all-start.2 = ((bf16[16,128,128]{2,1,0:T(8,128)(2,1)}), bf16[16,128,128]{2,1,0:T(8,128)(2,1)S(1)}, u32[]{:S(2)}, u32[]{:S(2)}) async-start(bf16[16,128,128]{2,1,0:T(8,128)(2,1)} %bitcast.4), calls=%async_computation.2 | async-start | bytes 1048576 | tf_op jit(solution)/shard_map/all_to_all | solution.py:272
  90.6 9.2 %collective-permute-start.6 = (bf16[128,1024]{1,0:T(8,128)(2,1)S(1)}, bf16[128,1024]{1,0:T(8,128)(2,1)S(1)}, u32[]{:S(2)}, u32[]{:S(2)}) collective-permute-start(bf16[128,1024]{1,0:T(8,128)(2,1)S(1)} %get-tuple-element.17), channel_id=1, source_target_pairs={{0,8},{8,16},{16,24},{24,0},{1,9},{9,17},{17,25},{25,1},{2,10},{10... | collective-permute-start | bytes 786440 | tf_op jit(solution)/shard_map/ppermute | solution.py:216
  94.6 10.1 %collective-permute-start.7 = (bf16[128,1024]{1,0:T(8,128)(2,1)S(1)}, bf16[128,1024]{1,0:T(8,128)(2,1)S(1)}, u32[]{:S(2)}, u32[]{:S(2)}) collective-permute-start(bf16[128,1024]{1,0:T(8,128)(2,1)S(1)} %get-tuple-element.18), channel_id=1, source_target_pairs={{0,16},{8,24},{16,0},{24,8},{1,17},{9,25},{17,1},{25,9},{2,18},{10... | collective-permute-start | bytes 786440 | tf_op jit(solution)/shard_map/ppermute | solution.py:216
  96.8 10.6 %collective-permute-start.8 = (bf16[128,1024]{1,0:T(8,128)(2,1)S(1)}, bf16[128,1024]{1,0:T(8,128)(2,1)S(1)}, u32[]{:S(2)}, u32[]{:S(2)}) collective-permute-start(bf16[128,1024]{1,0:T(8,128)(2,1)S(1)} %get-tuple-element.19), channel_id=1, source_target_pairs={{0,24},{8,0},{16,8},{24,16},{1,25},{9,1},{17,9},{25,17},{2,26},{10... | collective-permute-start | bytes 786440 | tf_op jit(solution)/shard_map/ppermute | solution.py:216
  116.7 38.7 %copy-start.4 = (bf16[128,512]{1,0:T(8,128)(2,1)S(1)}, bf16[128,512]{1,0:T(8,128)(2,1)}, u32[]{:S(2)}) copy-start(bf16[128,512]{1,0:T(8,128)(2,1)} %copy-done.3) | copy-start | bytes 393220
  149.5 32.8 %all-to-all-start.6 = ((bf16[32,16,1024]{2,1,0:T(8,128)(2,1)}), bf16[32,16,1024]{2,1,0:T(8,128)(2,1)S(1)}, u32[]{:S(2)}, u32[]{:S(2)}) async-start(bf16[32,16,1024]{2,1,0:T(8,128)(2,1)} %shard_map.84), calls=%async_computation.6 | async-start | bytes 2097152 | tf_op jit(solution)/shard_map/all_to_all | solution.py:319
  155.4 15.9 %collective-permute-start.3 = (bf16[128,512]{1,0:T(8,128)(2,1)S(1)}, bf16[128,512]{1,0:T(8,128)(2,1)S(1)}, u32[]{:S(2)}, u32[]{:S(2)}) collective-permute-start(bf16[128,512]{1,0:T(8,128)(2,1)S(1)} %copy-done.4), channel_id=1, source_target_pairs={{0,24},{8,0},{16,8},{24,16},{1,25},{9,1},{17,9},{25,17},{2,26},{10... | collective-permute-start | bytes 393224 | tf_op jit(solution)/shard_map/ppermute | solution.py:216
  158.1 13.2 %collective-permute-start.4 = (bf16[128,512]{1,0:T(8,128)(2,1)S(1)}, bf16[128,512]{1,0:T(8,128)(2,1)S(1)}, u32[]{:S(2)}, u32[]{:S(2)}) collective-permute-start(bf16[128,512]{1,0:T(8,128)(2,1)S(1)} %get-tuple-element.13), channel_id=1, source_target_pairs={{0,16},{8,24},{16,0},{24,8},{1,17},{9,25},{17,1},{25,9},{2,18},{10... | collective-permute-start | bytes 393224 | tf_op jit(solution)/shard_map/ppermute | solution.py:216
  160.8 13.8 %collective-permute-start.5 = (bf16[128,512]{1,0:T(8,128)(2,1)S(1)}, bf16[128,512]{1,0:T(8,128)(2,1)S(1)}, u32[]{:S(2)}, u32[]{:S(2)}) collective-permute-start(bf16[128,512]{1,0:T(8,128)(2,1)S(1)} %get-tuple-element.14), channel_id=1, source_target_pairs={{0,8},{8,16},{16,24},{24,0},{1,9},{9,17},{17,25},{25,1},{2,10},{10... | collective-permute-start | bytes 393224 | tf_op jit(solution)/shard_map/ppermute | solution.py:216

commit v4 on v3

v4 whole, which is shorter than its diff:
```python
import math

import jax
import jax.numpy as jnp
from jax import lax
from jax.experimental import pallas as pl
from jax.experimental.pallas import tpu as pltpu
from jax.sharding import Mesh, PartitionSpec as P

HD = 128
GROUP = 4
DIMS = (4, 2, 2, 4, 4, 2)
AXES = ("yh", "yl", "zh", "x", "zl", "core")
CTX = ("yh", "yl", "zh", "x")
Y = ("yh", "yl")
TP = ("zl", "core")
QUERY = ("yl", "x")
KEY = ("yh", "zh")
BLOCK = 128
LOW = -1e30
FLOOR = -1e29
SCALE = HD ** (-0.5)
SCALE2 = SCALE * math.log2(math.e)
NT = (((1,), (1,)), ((), ()))
TN = (((0,), (0,)), ((), ()))


class Place:
    def __init__(self, sizes, sc_ref):
        self.nyl, self.nzh, self.nx = sizes
        self.yh, self.yl, self.zh, self.x, self.low, self.high = (sc_ref[i] for i in range(6))
        self.pieces = self.nyl * self.nx
        self.run = self.nx * BLOCK
        self.step = self.nyl * self.nzh * self.run
        self.width = self.pieces * BLOCK
        self.origin = [
            (lax.rem(self.yl + self.nyl - e, self.nyl), lax.rem(self.x + self.nx - d, self.nx))
            for e in range(self.nyl)
            for d in range(self.nx)
        ]
        self.lanes = [pl.multiple_of((yl * self.nx + x) * BLOCK, BLOCK) for yl, x in self.origin]

    def gather(self, row_ref):
        return jnp.concatenate([row_ref[:, pl.ds(at, BLOCK)] for at in self.lanes], axis=1)

    def queries(self):
        lane = lax.broadcasted_iota(jnp.int32, (1, BLOCK), 1)
        base = self.yh * self.step + self.zh * self.run
        return jnp.concatenate(
            [base + yl * self.nzh * self.run + x * BLOCK + lane for yl, x in self.origin], axis=1
        )

    def chunk(self):
        return self.nzh * BLOCK

    def keys(self, j):
        r = lax.broadcasted_iota(jnp.int32, (self.chunk(), 1), 0)
        base = j * self.step + self.yl * self.nzh * self.run + self.x * BLOCK
        return base + (r // BLOCK) * self.run + r % BLOCK

    def over_chunks(self, step):
        first, last = self.low // self.step, self.yh
        clear = jnp.minimum((self.high + self.step - 1) // self.step, last)

        def masked(j, carry):
            step(j, True)
            return carry

        def free(j, carry):
            step(j, False)
            return carry

        lax.fori_loop(first, clear, masked, 0)
        lax.fori_loop(clear, last, free, 0)
        step(last, True)


def chunk_of(j, size, kv_ref):
    at = pl.ds(pl.multiple_of(j * size, size), size)
    return at, kv_ref[at, 0:HD], kv_ref[at, HD : 2 * HD]


def head_of(q_refs, n):
    q = jnp.concatenate([r[:, n * HD : (n + 1) * HD] for r in q_refs], axis=0)
    do = jnp.concatenate([r[:, (GROUP + n) * HD : (GROUP + n + 1) * HD] for r in q_refs], axis=0)
    return q, do


def stats_kernel(sizes, sc_ref, start_ref, *refs):
    place = Place(sizes, sc_ref)
    count, span = place.pieces, place.width
    q_refs, kv_ref, out_ref, st_ref = refs[:count], refs[count], refs[-2], refs[-1]
    pos_q, start = place.queries(), place.gather(start_ref)
    st_ref[0] = jnp.full((GROUP, span), FLOOR, jnp.float32)
    st_ref[1] = jnp.zeros((GROUP, span), jnp.float32)
    st_ref[2] = jnp.zeros((GROUP, span), jnp.float32)

    def step(j, masked):
        _, k, v = chunk_of(j, place.chunk(), kv_ref)
        if masked:
            pos_k = place.keys(j)
            allowed = (pos_k <= pos_q) & (pos_k >= start)
        for n in range(GROUP):
            q, do = head_of(q_refs, n)
            s = lax.dot_general(k, q, NT, preferred_element_type=jnp.float32) * SCALE2
            if masked:
                s = jnp.where(allowed, s, LOW)
            dp = lax.dot_general(v, do, NT, preferred_element_type=jnp.float32)
            m_old = st_ref[0, n : n + 1, :]
            m = jnp.maximum(m_old, jnp.max(s, axis=0, keepdims=True))
            alpha = jnp.exp2(m_old - m)
            w = jnp.exp2(s - m)
            st_ref[0, n : n + 1, :] = m
            st_ref[1, n : n + 1, :] = st_ref[1, n : n + 1, :] * alpha + jnp.sum(
                w, axis=0, keepdims=True
            )
            st_ref[2, n : n + 1, :] = st_ref[2, n : n + 1, :] * alpha + jnp.sum(
                w * dp, axis=0, keepdims=True
            )

    place.over_chunks(step)
    for i, at in enumerate(place.lanes):
        for k in range(3):
            row = st_ref[k, :, i * BLOCK : (i + 1) * BLOCK]
            for copy in range(count):
                out_ref[copy, k, :, pl.ds(at, BLOCK)] = row


def grad_kernel(sizes, sc_ref, start_ref, st_ref, *refs):
    place = Place(sizes, sc_ref)
    count, span = place.pieces, place.width
    q_refs, kv_ref, (*dq_refs, dv_ref, acc_ref) = refs[:count], refs[count], refs[count + 1 :]
    pos_q, start = place.queries(), place.gather(start_ref)
    acc_ref[...] = jnp.zeros(acc_ref.shape, jnp.float32)
    dv_ref[...] = jnp.zeros(dv_ref.shape, dv_ref.dtype)
    part = [[place.gather(st_ref.at[i, k]) for k in range(3)] for i in range(count)]
    top = part[0][0]
    for i in range(1, count):
        top = jnp.maximum(top, part[i][0])
    total = jnp.zeros_like(top)
    num = jnp.zeros_like(top)
    for i in range(count):
        f = jnp.exp2(part[i][0] - top)
        total = total + part[i][1] * f
        num = num + part[i][2] * f
    log_total = top + jnp.log2(total)
    delta = num / total

    def step(j, masked):
        at, k, v = chunk_of(j, place.chunk(), kv_ref)
        if masked:
            pos_k = place.keys(j)
            allowed = (pos_k <= pos_q) & (pos_k >= start)
        dv = jnp.zeros((place.chunk(), HD), jnp.float32)
        for n in range(GROUP):
            q, do = head_of(q_refs, n)
            s = lax.dot_general(k, q, NT, preferred_element_type=jnp.float32) * SCALE2
            if masked:
                s = jnp.where(allowed, s, LOW)
            dp = lax.dot_general(v, do, NT, preferred_element_type=jnp.float32)
            p = jnp.exp2(s - log_total[n : n + 1, :])
            ds = (p * (dp - delta[n : n + 1, :])).astype(jnp.bfloat16)
            dv = dv + jnp.dot(p.astype(jnp.bfloat16), do, preferred_element_type=jnp.float32)
            acc_ref[n] += lax.dot_general(k, ds, TN, preferred_element_type=jnp.float32)
        dv_ref[at, :] = dv.astype(dv_ref.dtype)

    place.over_chunks(step)
    nx = place.nx
    for n in range(GROUP):
        dq = (acc_ref[n] * SCALE).T.astype(jnp.bfloat16)
        for i in range(count):
            dq_refs[i % nx][i // nx, :, n * HD : (n + 1) * HD] = dq[i * BLOCK : (i + 1) * BLOCK]


def join_kernel(*refs):
    *in_refs, away_ref, own_ref = refs
    total = in_refs[0][...].astype(jnp.float32)
    for r in in_refs[1:]:
        total = total + r[...].astype(jnp.float32)
    own_ref[...] = total[0]
    away_ref[...] = total[1].astype(away_ref.dtype)


def regroup_kernel(nx, tps, sc_ref, f_ref, _, *out_refs):
    x = sc_ref[3]
    share = f_ref.shape[1] // tps
    wide = share // nx
    for d, out_ref in enumerate(out_refs):
        to = lax.rem(x + d, nx) * wide
        for t in range(tps):
            at = pl.multiple_of(t * share + to, wide)
            out_ref[:, t * wide : (t + 1) * wide] = f_ref[:, pl.ds(at, wide)]


def weight_kernel(nx, sc_ref, v_ref, *refs):
    f_refs, out_ref = refs[:nx], refs[nx]
    ny, tps, part, _ = out_ref.shape
    x = sc_ref[3]
    f = jnp.concatenate([r[...] for r in f_refs], axis=0)
    v = jnp.concatenate([v_ref[lax.rem(x + nx - d, nx)] for d in range(nx)], axis=0)
    term = lax.dot_general(v, f, TN, preferred_element_type=jnp.float32).T
    for t in range(tps):
        for y in range(ny):
            at = (t * ny + y) * part
            out_ref[y, t] = term[at : at + part].astype(out_ref.dtype)


def sum_kernel(in_ref, *refs):
    out_ref = refs[-1]
    total = in_ref[0].astype(jnp.float32)
    for i in range(1, in_ref.shape[0]):
        total = total + in_ref[i].astype(jnp.float32)
    total = total.astype(out_ref.dtype)
    for i in range(out_ref.shape[0]):
        out_ref[i] = total


def turn_kernel(nzh, factor, in_ref, _, out_ref):
    tps = in_ref.shape[0] // nzh
    parts = []
    for t in range(tps):
        total = in_ref[t].astype(jnp.float32)
        for i in range(1, nzh):
            total = total + in_ref[i * tps + t].astype(jnp.float32)
        parts.append((total * factor).astype(out_ref.dtype))
    whole = jnp.concatenate(parts, axis=1)
    for i in range(out_ref.shape[0]):
        out_ref[i] = whole


def shift(a, axis, by):
    n = lax.axis_size(axis)
    return lax.ppermute(a, axis, [(i, (i + by) % n) for i in range(n)])


def per_device(queries, keys, values, out_grad, features, segment_ids):
    nyh, nyl, nzh, nx, nzl, ncore = (lax.axis_size(a) for a in AXES)
    ny, tps = nyh * nyl, nzl * ncore
    sizes = (nyl, nzh, nx)
    tokens = segment_ids.shape[0]
    rows = queries.shape[0]
    bf16, f32 = jnp.bfloat16, jnp.float32
    smem = pl.BlockSpec(memory_space=pltpu.SMEM)
    vmem = pl.BlockSpec(memory_space=pltpu.VMEM)
    unread = pl.BlockSpec(memory_space=pl.ANY)
    params = pltpu.CompilerParams(vmem_limit_bytes=24 * 1024 * 1024)

    kv_copies = jnp.broadcast_to(
        jnp.concatenate([keys, values], axis=1)[None], (nyh * nzh, rows, 2 * HD)
    )
    kv = lax.all_to_all(kv_copies, KEY, split_axis=0, concat_axis=0, tiled=True)
    kv = kv.reshape(nyh * nzh * rows, 2 * HD)
    own = jnp.concatenate([queries, out_grad], axis=1)
    pieces = [own] + [shift(own, "yl", e) for e in range(1, nyl)]
    qd = [shift(p, "x", d) if d else p for p in pieces for d in range(nx)]

    yh, yl, zh, x = (lax.axis_index(a) for a in CTX)
    base = (yh * nyl * nzh + zh) * nx * rows
    seg_q = jnp.concatenate(
        [
            lax.dynamic_slice_in_dim(segment_ids, base + i * nzh * nx * rows, nx * rows, 0)
            for i in range(nyl)
        ]
    )
    ids = jnp.arange(16, dtype=jnp.int32)
    firsts = jnp.sum((segment_ids[None, :] < ids[:, None]).astype(jnp.int32), axis=1)
    start = jnp.sum(jnp.where(seg_q[None, :] == ids[:, None], firsts[:, None], 0), axis=0)
    scalars = jnp.stack([yh, yl, zh, x, start[0], start[-1]]).astype(jnp.int32)
    start = start.reshape(1, nyl * nx * rows)

    count = nyl * nx
    stats = pl.pallas_call(
        lambda *refs: stats_kernel(sizes, *refs),
        out_shape=jax.ShapeDtypeStruct((count, 3, GROUP, count * rows), f32),
        in_specs=[smem, vmem] + [vmem] * (count + 1),
        out_specs=vmem,
        scratch_shapes=[pltpu.VMEM((3, GROUP, count * rows), f32)],
        compiler_params=params,
    )(scalars, start, *qd, kv)
    all_stats = lax.all_to_all(stats, QUERY, split_axis=0, concat_axis=0, tiled=True)
    *dq_parts, dv_part = pl.pallas_call(
        lambda *refs: grad_kernel(sizes, *refs),
        out_shape=[jax.ShapeDtypeStruct((nyl, rows, GROUP * HD), bf16)] * nx
        + [jax.ShapeDtypeStruct((nyh * nzh * rows, HD), bf16)],
        in_specs=[smem, vmem, vmem] + [vmem] * (count + 1),
        out_specs=[vmem] * (nx + 1),
        scratch_shapes=[pltpu.VMEM((GROUP, HD, count * rows), f32)],
        compiler_params=params,
    )(scalars, start, all_stats, *qd, kv)

    dv = lax.all_to_all(
        dv_part.reshape(nyh * nzh, rows, HD), KEY, split_axis=0, concat_axis=0, tiled=True
    )
    wide = features.shape[1] // nx
    mine = pl.pallas_call(
        lambda *refs: regroup_kernel(nx, tps, *refs),
        out_shape=[jax.ShapeDtypeStruct((rows, wide), bf16)] * nx,
        in_specs=[smem, vmem, unread],
        out_specs=[vmem] * nx,
        compiler_params=params,
    )(scalars, features, stats)
    from_x = [mine[0]] + [shift(mine[d], "x", d) for d in range(1, nx)]
    value_copies = pl.pallas_call(
        sum_kernel,
        out_shape=jax.ShapeDtypeStruct((nx, rows, HD), bf16),
        in_specs=[vmem] + [unread] * (nx - 1),
        out_specs=vmem,
        compiler_params=params,
    )(dv, *from_x[1:])
    value_x = lax.all_to_all(value_copies, "x", split_axis=0, concat_axis=0, tiled=True)
    part = wide // (tps * ny)
    term = pl.pallas_call(
        lambda *refs: weight_kernel(nx, *refs),
        out_shape=jax.ShapeDtypeStruct((ny, tps, part, HD), bf16),
        in_specs=[smem] + [vmem] * (nx + 1),
        out_specs=vmem,
        compiler_params=params,
    )(scalars, value_x, *from_x)
    pieces = lax.all_to_all(term, Y, split_axis=0, concat_axis=0, tiled=True)

    dq_x = [dq_parts[0]] + [shift(dq_parts[d], "x", -d) for d in range(1, nx)]
    away, at_home = pl.pallas_call(
        join_kernel,
        out_shape=(
            jax.ShapeDtypeStruct((rows, GROUP * HD), bf16),
            jax.ShapeDtypeStruct((rows, GROUP * HD), f32),
        ),
        in_specs=[vmem] * nx,
        out_specs=(vmem, vmem),
        compiler_params=params,
    )(*dq_x)

    row_copies = pl.pallas_call(
        sum_kernel,
        out_shape=jax.ShapeDtypeStruct((nzh, tps, part, HD), bf16),
        in_specs=[vmem],
        out_specs=vmem,
        compiler_params=params,
    )(pieces)
    turned = lax.all_to_all(
        row_copies.reshape(nzh * tps, part, HD),
        ("zh",) + TP, split_axis=0, concat_axis=0, tiled=True,
    )
    final_copies = pl.pallas_call(
        lambda *refs: turn_kernel(nzh, 1.0 / math.sqrt(tokens), *refs),
        out_shape=jax.ShapeDtypeStruct((nx * ny, part, tps * HD), bf16),
        in_specs=[vmem, unread],
        out_specs=vmem,
        compiler_params=params,
    )(turned, away)
    weight_grad = lax.all_to_all(
        final_copies, ("x",) + Y, split_axis=0, concat_axis=0, tiled=True
    )
    query_grads = (at_home + shift(away, "yl", 1).astype(f32)).astype(bf16)
    return (query_grads, weight_grad.reshape(wide // tps * nx, tps * HD).astype(f32))


def solution(mesh):
    fine = Mesh(mesh.devices.reshape(DIMS), AXES)
    split = P(CTX, TP)
    return jax.shard_map(
        per_device,
        mesh=fine,
        in_specs=(split, split, split, split, P(CTX, None), P()),
        out_specs=(split, P(TP, None)),
        check_vma=False,
    )
```

time: 187 us -> 207 us (1.11)
  starting transfers between devices: 68.3 us -> 110 us
  blocking collectives: 48.4 us -> 19.6 us
  local copies, waits for them, and re-layouts: 2.91 us -> 6.46 us
  Pallas kernels: 8.72 us -> 11.4 us
  waiting for transfers between devices: 50.9 us -> 53.1 us
    all_to_all x3 -> x1, blocking collectives: 40.1 us -> 11.4 us  [per_device(): lax.all_to_all(stats, QUERY, split_axis=0, concat_axis=0, tiled=True)]
    all_to_all x3 -> x5, starting transfers between devices: 39.6 us -> 64.4 us  [the longest x1 24.8 us: per_device(): lax.all_to_all(dv_part.reshape(nyh * nzh, rows, HD), KEY, split_axis=0, c...]
    ppermute x9 -> x14, waiting for transfers between devices: 24 us -> 45.4 us  [shift(): return lax.ppermute(a, axis, [(i, (i + by) % n) for i in range(n)])]
    all_to_all x3 -> x5, waiting for transfers between devices: 27 us -> 7.73 us  [the longest x1 7.7 us: per_device(): lax.all_to_all(row_copies.reshape(nzh * tps, part, HD), ('zh',) + TP, spl...]
    ppermute x9 -> x14, starting transfers between devices: 28.7 us -> 45.1 us  [shift(): return lax.ppermute(a, axis, [(i, (i + by) % n) for i in range(n)])]
  transfers between devices with their start and end apart: 12 -> 19, of which waited for: 8 -> 8; matrix products, arithmetic and copies ran while one was open for 2% -> 2% of each run, Pallas kernels for 0% -> 1%
where the time goes in v4:
time: 207 us; the launch traced here: 205 us
  starting transfers between devices  110 us (53%)
  waiting for transfers between devices  53.1 us (26%)
  blocking collectives  19.6 us (9%)
  Pallas kernels  11.4 us (6%)
  local copies, waits for them, and re-layouts  6.46 us (3%)
  other arithmetic  3.4 us (2%)
    ppermute x14, waiting for transfers between devices, shift(): return lax.ppermute(a, axis, [(i, (i + by) % n) for i in range(n)])  45.4 us
    ppermute x14, starting transfers between devices, shift(): return lax.ppermute(a, axis, [(i, (i + by) % n) for i in range(n)])  45.1 us
    all_to_all x1, starting transfers between devices, per_device(): lax.all_to_all(dv_part.reshape(nyh * nzh, rows, HD), KEY, split_axis=0, c...  24.8 us
    all_to_all x1, starting transfers between devices, per_device(): kv = lax.all_to_all(kv_copies, KEY, split_axis=0, concat_axis=0, tiled=True)  15.5 us
    all_to_all x1, blocking collectives, per_device(): lax.all_to_all(stats, QUERY, split_axis=0, concat_axis=0, tiled=True)  11.4 us
    all_to_all x1, starting transfers between devices, per_device(): lax.all_to_all(final_copies, ('x',) + Y, split_axis=0, concat_axis=0, til...  10.3 us
    all_to_all x1, blocking collectives, per_device(): lax.all_to_all(value_copies, 'x', split_axis=0, concat_axis=0, tiled=True)  8.22 us
    all_to_all x1, waiting for transfers between devices, per_device(): lax.all_to_all(row_copies.reshape(nzh * tps, part, HD), ('zh',) + TP, spl...  7.7 us
  transfers between devices with their start and end apart: 19, of which 8 were waited for; matrix products, arithmetic and copies ran while one was open for 2% of the time, Pallas kernels for 1%

profile of v4, /device:TPU:6, one launch (start us, length us, event | category | flops | bytes accessed | tf_op | source)
XLA Modules:
  0.0 204.5 jit_solution(13461692768898062247)
XLA Ops:
  2.3 15.5 %all-to-all-start = ((bf16[8,128,256]{2,1,0:T(8,128)(2,1)}), bf16[8,128,256]{2,1,0:T(8,128)(2,1)S(1)}, u32[]{:S(2)}, u32[]{:S(2)}) async-start(bf16[8,128,256]{2,1,0:T(8,128)(2,1)} %broadcast_in_dim.12), calls=%async_computation | async-start | bytes 1048576 | tf_op jit(solution)/shard_map/all_to_all | solution.py:251
  24.1 3.0 %collective-permute-start.1 = (bf16[128,1024]{1,0:T(8,128)(2,1)S(1)}, bf16[128,1024]{1,0:T(8,128)(2,1)S(1)}, u32[]{:S(2)}, u32[]{:S(2)}) collective-permute-start(bf16[128,1024]{1,0:T(8,128)(2,1)S(1)} %constant_dynamic-update-slice_fusion.refs_2_.refs_3_), channel_id=1, source_target_pairs={{0,16},{8,24},{16,0},{24,8},{1,17},{9,25},{17,1},{25,9},{2,18},{10... | collective-permute-start | bytes 786440 | tf_op jit(solution)/shard_map/ppermute | solution.py:233
  27.2 4.0 %collective-permute-start = (bf16[128,1024]{1,0:T(8,128)(2,1)S(1)}, bf16[128,1024]{1,0:T(8,128)(2,1)S(1)}, u32[]{:S(2)}, u32[]{:S(2)}) collective-permute-start(bf16[128,1024]{1,0:T(8,128)(2,1)S(1)} %constant_dynamic-update-slice_fusion.refs_2_.refs_3_), channel_id=1, source_target_pairs={{0,8},{8,16},{16,24},{24,0},{1,9},{9,17},{17,25},{25,1},{2,10},{10... | collective-permute-start | bytes 786440 | tf_op jit(solution)/shard_map/ppermute | solution.py:233
  31.4 4.6 %collective-permute-done.3.refs_6_.refs_7_ = bf16[128,1024]{1,0:T(8,128)(2,1)S(1)} collective-permute-done((bf16[128,1024]{1,0:T(8,128)(2,1)S(1)}, bf16[128,1024]{1,0:T(8,128)(2,1)S(1)}, u32[]{:S(2)}, u32[]{:S(2)}) %collective-permute-start.3) | collective-permute-done | bytes 262176 | tf_op jit(solution)/shard_map/ppermute | solution.py:233
  38.8 3.0 %collective-permute-start.5 = (bf16[128,1024]{1,0:T(8,128)(2,1)S(1)}, bf16[128,1024]{1,0:T(8,128)(2,1)S(1)}, u32[]{:S(2)}, u32[]{:S(2)}) collective-permute-start(bf16[128,1024]{1,0:T(8,128)(2,1)S(1)} %collective-permute-done.3.refs_6_.refs_7_), channel_id=1, source_target_pairs={{0,16},{8,24},{16,0},{24,8},{1,17},{9,25},{17,1},{25,9},{2,18},{10... | collective-permute-start | bytes 786440 | tf_op jit(solution)/shard_map/ppermute | solution.py:233
  41.8 4.0 %collective-permute-start.4 = (bf16[128,1024]{1,0:T(8,128)(2,1)S(1)}, bf16[128,1024]{1,0:T(8,128)(2,1)S(1)}, u32[]{:S(2)}, u32[]{:S(2)}) collective-permute-start(bf16[128,1024]{1,0:T(8,128)(2,1)S(1)} %collective-permute-done.3.refs_6_.refs_7_), channel_id=1, source_target_pairs={{0,8},{8,16},{16,24},{24,0},{1,9},{9,17},{17,25},{25,1},{2,10},{10... | collective-permute-start | bytes 786440 | tf_op jit(solution)/shard_map/ppermute | solution.py:233
  47.9 4.1 %collective-permute-done.6.refs_9_.refs_10_ = bf16[128,1024]{1,0:T(8,128)(2,1)S(1)} collective-permute-done((bf16[128,1024]{1,0:T(8,128)(2,1)S(1)}, bf16[128,1024]{1,0:T(8,128)(2,1)S(1)}, u32[]{:S(2)}, u32[]{:S(2)}) %collective-permute-start.6) | collective-permute-done | bytes 262176 | tf_op jit(solution)/shard_map/ppermute | solution.py:233
  57.2 11.4 %all_to_all.35.refs_2_ = f32[8,3,4,1024]{3,2,1,0:T(4,128)S(1)} all-to-all(f32[8,3,4,1024]{3,2,1,0:T(4,128)S(1)} %shard_map.77.refs_2_), channel_id=1, replica_groups=mesh['yh'=4,'yl'=2,'zh'=2,'x'=4,'zl'=4,'core'=2] {'yl','x'}, dimensions={0} | all-to-all | bytes 786432 | tf_op jit(solution)/shard_map/all_to_all | solution.py:280
  68.6 4.3 %shard_map.78 = (bf16[2,128,512]{2,1,0:T(8,128)(2,1)S(1)}, bf16[2,128,512]{2,1,0:T(8,128)(2,1)S(1)}, bf16[2,128,512]{2,1,0:T(8,128)(2,1)S(1)}, bf16[2,128,512]{2,1,0:T(8,128)(2,1)S(1)}, bf16[1024,128]{1,0:T(8,128)(2,1)}) custom-call(s32[6]{0:T(128)S(1)} %stack.19.refs_0_, s32[1,1024]{1,0:T(1,128)S(1)} %bitcast.14, f32[8,3,4,1024]{3,2,1,0:T(4,128)S(1)} %all_to_all.35.refs_2_, ...), custom_call_target="tpu_custom_call" | custom-call | tf_op jit(solution)/shard_map/pallas_call | solution.py:281
  74.3 24.8 %all-to-all-start.2 = ((bf16[8,128,128]{2,1,0:T(8,128)(2,1)}), bf16[8,128,128]{2,1,0:T(8,128)(2,1)S(1)}, u32[]{:S(2)}, u32[]{:S(2)}) async-start(bf16[8,128,128]{2,1,0:T(8,128)(2,1)} %bitcast.6), calls=%async_computation.2 | async-start | bytes 524288 | tf_op jit(solution)/shard_map/all_to_all | solution.py:291
  101.2 4.0 %collective-permute-start.11 = (bf16[128,1024]{1,0:T(8,128)(2,1)S(1)}, bf16[128,1024]{1,0:T(8,128)(2,1)S(1)}, u32[]{:S(2)}, u32[]{:S(2)}) collective-permute-start(bf16[128,1024]{1,0:T(8,128)(2,1)S(1)} %get-tuple-element.20), channel_id=1, source_target_pairs={{0,8},{8,16},{16,24},{24,0},{1,9},{9,17},{17,25},{25,1},{2,10},{10... | collective-permute-start | bytes 786440 | tf_op jit(solution)/shard_map/ppermute | solution.py:233
  107.5 2.9 %collective-permute-start.13 = (bf16[128,1024]{1,0:T(8,128)(2,1)S(1)}, bf16[128,1024]{1,0:T(8,128)(2,1)S(1)}, u32[]{:S(2)}, u32[]{:S(2)}) collective-permute-start(bf16[128,1024]{1,0:T(8,128)(2,1)S(1)} %get-tuple-element.22), channel_id=1, source_target_pairs={{0,24},{8,0},{16,8},{24,16},{1,25},{9,1},{17,9},{25,17},{2,26},{10... | collective-permute-start | bytes 786440 | tf_op jit(solution)/shard_map/ppermute | solution.py:233
  110.4 4.5 %collective-permute-done.11.refs_0_.refs_3_ = bf16[128,1024]{1,0:T(8,128)(2,1)S(1)} collective-permute-done((bf16[128,1024]{1,0:T(8,128)(2,1)S(1)}, bf16[128,1024]{1,0:T(8,128)(2,1)S(1)}, u32[]{:S(2)}, u32[]{:S(2)}) %collective-permute-start.11) | collective-permute-done | bytes 262176 | tf_op jit(solution)/shard_map/ppermute | solution.py:233
  115.0 2.8 %collective-permute-done.12.refs_1_.refs_4_ = bf16[128,1024]{1,0:T(8,128)(2,1)S(1)} collective-permute-done((bf16[128,1024]{1,0:T(8,128)(2,1)S(1)}, bf16[128,1024]{1,0:T(8,128)(2,1)S(1)}, u32[]{:S(2)}, u32[]{:S(2)}) %collective-permute-start.12) | collective-permute-done | bytes 262176 | tf_op jit(solution)/shard_map/ppermute | solution.py:233
  117.8 2.8 %collective-permute-done.13.refs_2_.refs_5_ = bf16[128,1024]{1,0:T(8,128)(2,1)S(1)} collective-permute-done((bf16[128,1024]{1,0:T(8,128)(2,1)S(1)}, bf16[128,1024]{1,0:T(8,128)(2,1)S(1)}, u32[]{:S(2)}, u32[]{:S(2)}) %collective-permute-start.13) | collective-permute-done | bytes 262176 | tf_op jit(solution)/shard_map/ppermute | solution.py:233
  120.6 8.2 %all_to_all.36.refs_1_ = bf16[4,128,128]{2,1,0:T(8,128)(2,1)S(1)} all-to-all(bf16[4,128,128]{2,1,0:T(8,128)(2,1)S(1)} %shard_map.81), channel_id=1, replica_groups=mesh['yh'=4,'yl'=2,'zh'=2,'x'=4,'zl'=4,'core'=2] {'x'}, dimensions={0} | all-to-all | bytes 262144 | tf_op jit(solution)/shard_map/all_to_all | solution.py:310
  130.5 6.9 %all-to-all-start.4 = ((bf16[8,8,16,128]{3,2,1,0:T(8,128)(2,1)}), bf16[8,8,16,128]{3,2,1,0:T(8,128)(2,1)S(1)}, u32[]{:S(2)}, u32[]{:S(2)}) async-start(bf16[8,8,16,128]{3,2,1,0:T(8,128)(2,1)} %shard_map.82), calls=%async_computation.4 | async-start | bytes 524288 | tf_op jit(solution)/shard_map/all_to_all | solution.py:319
  139.5 5.2 %collective-permute-start.8 = (bf16[2,128,512]{2,1,0:T(8,128)(2,1)S(1)}, bf16[2,128,512]{2,1,0:T(8,128)(2,1)S(1)}, u32[]{:S(2)}, u32[]{:S(2)}) collective-permute-start(bf16[2,128,512]{2,1,0:T(8,128)(2,1)S(1)} %copy-done.2), channel_id=1, source_target_pairs={{0,16},{8,24},{16,0},{24,8},{1,17},{9,25},{17,1},{25,9},{2,18},{10... | collective-permute-start | bytes 786440 | tf_op jit(solution)/shard_map/ppermute | solution.py:233
  144.8 3.1 %collective-permute-start.9 = (bf16[2,128,512]{2,1,0:T(8,128)(2,1)S(1)}, bf16[2,128,512]{2,1,0:T(8,128)(2,1)S(1)}, u32[]{:S(2)}, u32[]{:S(2)}) collective-permute-start(bf16[2,128,512]{2,1,0:T(8,128)(2,1)S(1)} %get-tuple-element.16), channel_id=1, source_target_pairs={{0,8},{8,16},{16,24},{24,0},{1,9},{9,17},{17,25},{25,1},{2,10},{10... | collective-permute-start | bytes 786440 | tf_op jit(solution)/shard_map/ppermute | solution.py:233
  148.5 6.8 %all-to-all-start.5 = ((bf16[16,16,128]{2,1,0:T(8,128)(2,1)}), bf16[16,16,128]{2,1,0:T(8,128)(2,1)S(1)}, u32[]{:S(2)}, u32[]{:S(2)}) async-start(bf16[16,16,128]{2,1,0:T(8,128)(2,1)} %bitcast.7), calls=%async_computation.5 | async-start | bytes 131072 | tf_op jit(solution)/shard_map/all_to_all | solution.py:340
  155.5 7.7 %all-to-all-done.5.refs_0_ = bf16[16,16,128]{2,1,0:T(8,128)(2,1)S(1)} async-done(((bf16[16,16,128]{2,1,0:T(8,128)(2,1)}), bf16[16,16,128]{2,1,0:T(8,128)(2,1)S(1)}, u32[]{:S(2)}, u32[]{:S(2)}) %all-to-all-start.5) | async-done | bytes 65568 | tf_op jit(solution)/shard_map/all_to_all | solution.py:340
  164.3 10.3 %all-to-all-start.6 = ((bf16[32,16,1024]{2,1,0:T(8,128)(2,1)}), bf16[32,16,1024]{2,1,0:T(8,128)(2,1)S(1)}, u32[]{:S(2)}, u32[]{:S(2)}) async-start(bf16[32,16,1024]{2,1,0:T(8,128)(2,1)} %shard_map.84), calls=%async_computation.6 | async-start | bytes 2097152 | tf_op jit(solution)/shard_map/all_to_all | solution.py:351
  174.7 3.4 %collective-permute-start.10 = (bf16[128,512]{1,0:T(8,128)(2,1)S(1)}, bf16[128,512]{1,0:T(8,128)(2,1)S(1)}, u32[]{:S(2)}, u32[]{:S(2)}) collective-permute-start(bf16[128,512]{1,0:T(8,128)(2,1)S(1)} %get-tuple-element.18.refs_1_), channel_id=1, source_target_pairs={{0,64},{64,0},{1,65},{65,1},{2,66},{66,2},{3,67},{67,3},{4,68},{68... | collective-permute-start | bytes 393224 | tf_op jit(solution)/shard_map/ppermute | solution.py:233
  178.1 24.1 %collective-permute-done.10 = bf16[128,512]{1,0:T(8,128)(2,1)S(1)} collective-permute-done((bf16[128,512]{1,0:T(8,128)(2,1)S(1)}, bf16[128,512]{1,0:T(8,128)(2,1)S(1)}, u32[]{:S(2)}, u32[]{:S(2)}) %collective-permute-start.10) | collective-permute-done | bytes 131104 | tf_op jit(solution)/shard_map/ppermute | solution.py:233
  (50 shorter events, 31.9 us)
Async XLA Ops:
  0.6 18.1 %copy-start.5 = (bf16[128,512]{1,0:T(8,128)(2,1)S(1)}, bf16[128,512]{1,0:T(8,128)(2,1)}, u32[]{:S(2)}) copy-start(bf16[128,512]{1,0:T(8,128)(2,1)} %param.9) | copy-start | bytes 393220
  0.6 30.5 %copy-start.6 = (s32[8192]{0:T(1024)S(1)}, s32[8192]{0:T(1024)}, u32[]{:S(2)}) copy-start(s32[8192]{0:T(1024)} %param.11) | copy-start | bytes 98308
  2.3 52.2 %all-to-all-start = ((bf16[8,128,256]{2,1,0:T(8,128)(2,1)}), bf16[8,128,256]{2,1,0:T(8,128)(2,1)S(1)}, u32[]{:S(2)}, u32[]{:S(2)}) async-start(bf16[8,128,256]{2,1,0:T(8,128)(2,1)} %broadcast_in_dim.12), calls=%async_computation | async-start | bytes 1048576 | tf_op jit(solution)/shard_map/all_to_all | solution.py:251
  18.8 17.2 %collective-permute-start.3 = (bf16[128,1024]{1,0:T(8,128)(2,1)S(1)}, bf16[128,1024]{1,0:T(8,128)(2,1)S(1)}, u32[]{:S(2)}, u32[]{:S(2)}) collective-permute-start(bf16[128,1024]{1,0:T(8,128)(2,1)S(1)} %constant_dynamic-update-slice_fusion.refs_2_.refs_3_), channel_id=1, source_target_pairs={{0,64},{64,0},{1,65},{65,1},{2,66},{66,2},{3,67},{67,3},{4,68},{68... | collective-permute-start | bytes 786440 | tf_op jit(solution)/shard_map/ppermute | solution.py:233
  21.4 20.4 %collective-permute-start.2 = (bf16[128,1024]{1,0:T(8,128)(2,1)S(1)}, bf16[128,1024]{1,0:T(8,128)(2,1)S(1)}, u32[]{:S(2)}, u32[]{:S(2)}) collective-permute-start(bf16[128,1024]{1,0:T(8,128)(2,1)S(1)} %constant_dynamic-update-slice_fusion.refs_2_.refs_3_), channel_id=1, source_target_pairs={{0,24},{8,0},{16,8},{24,16},{1,25},{9,1},{17,9},{25,17},{2,26},{10... | collective-permute-start | bytes 786440 | tf_op jit(solution)/shard_map/ppermute | solution.py:233
  24.1 23.8 %collective-permute-start.1 = (bf16[128,1024]{1,0:T(8,128)(2,1)S(1)}, bf16[128,1024]{1,0:T(8,128)(2,1)S(1)}, u32[]{:S(2)}, u32[]{:S(2)}) collective-permute-start(bf16[128,1024]{1,0:T(8,128)(2,1)S(1)} %constant_dynamic-update-slice_fusion.refs_2_.refs_3_), channel_id=1, source_target_pairs={{0,16},{8,24},{16,0},{24,8},{1,17},{9,25},{17,1},{25,9},{2,18},{10... | collective-permute-start | bytes 786440 | tf_op jit(solution)/shard_map/ppermute | solution.py:233
  27.2 20.7 %collective-permute-start = (bf16[128,1024]{1,0:T(8,128)(2,1)S(1)}, bf16[128,1024]{1,0:T(8,128)(2,1)S(1)}, u32[]{:S(2)}, u32[]{:S(2)}) collective-permute-start(bf16[128,1024]{1,0:T(8,128)(2,1)S(1)} %constant_dynamic-update-slice_fusion.refs_2_.refs_3_), channel_id=1, source_target_pairs={{0,8},{8,16},{16,24},{24,0},{1,9},{9,17},{17,25},{25,1},{2,10},{10... | collective-permute-start | bytes 786440 | tf_op jit(solution)/shard_map/ppermute | solution.py:233
  36.0 15.9 %collective-permute-start.6 = (bf16[128,1024]{1,0:T(8,128)(2,1)S(1)}, bf16[128,1024]{1,0:T(8,128)(2,1)S(1)}, u32[]{:S(2)}, u32[]{:S(2)}) collective-permute-start(bf16[128,1024]{1,0:T(8,128)(2,1)S(1)} %collective-permute-done.3.refs_6_.refs_7_), channel_id=1, source_target_pairs={{0,24},{8,0},{16,8},{24,16},{1,25},{9,1},{17,9},{25,17},{2,26},{10... | collective-permute-start | bytes 786440 | tf_op jit(solution)/shard_map/ppermute | solution.py:233
  38.8 13.2 %collective-permute-start.5 = (bf16[128,1024]{1,0:T(8,128)(2,1)S(1)}, bf16[128,1024]{1,0:T(8,128)(2,1)S(1)}, u32[]{:S(2)}, u32[]{:S(2)}) collective-permute-start(bf16[128,1024]{1,0:T(8,128)(2,1)S(1)} %collective-permute-done.3.refs_6_.refs_7_), channel_id=1, source_target_pairs={{0,16},{8,24},{16,0},{24,8},{1,17},{9,25},{17,1},{25,9},{2,18},{10... | collective-permute-start | bytes 786440 | tf_op jit(solution)/shard_map/ppermute | solution.py:233
  41.8 12.7 %collective-permute-start.4 = (bf16[128,1024]{1,0:T(8,128)(2,1)S(1)}, bf16[128,1024]{1,0:T(8,128)(2,1)S(1)}, u32[]{:S(2)}, u32[]{:S(2)}) collective-permute-start(bf16[128,1024]{1,0:T(8,128)(2,1)S(1)} %collective-permute-done.3.refs_6_.refs_7_), channel_id=1, source_target_pairs={{0,8},{8,16},{16,24},{24,0},{1,9},{9,17},{17,25},{25,1},{2,10},{10... | collective-permute-start | bytes 786440 | tf_op jit(solution)/shard_map/ppermute | solution.py:233
  74.3 46.2 %all-to-all-start.2 = ((bf16[8,128,128]{2,1,0:T(8,128)(2,1)}), bf16[8,128,128]{2,1,0:T(8,128)(2,1)S(1)}, u32[]{:S(2)}, u32[]{:S(2)}) async-start(bf16[8,128,128]{2,1,0:T(8,128)(2,1)} %bitcast.6), calls=%async_computation.2 | async-start | bytes 524288 | tf_op jit(solution)/shard_map/all_to_all | solution.py:291
  99.1 1.2 copy-start
  100.4 37.0 %copy-start.4 = (bf16[2,128,512]{2,1,0:T(8,128)(2,1)S(1)}, bf16[2,128,512]{2,1,0:T(8,128)(2,1)}, u32[]{:S(2)}) copy-start(bf16[2,128,512]{2,1,0:T(8,128)(2,1)} %copy-done.3) | copy-start | bytes 786436
  100.4 39.2 %copy-start.2 = (bf16[2,128,512]{2,1,0:T(8,128)(2,1)S(1)}, bf16[2,128,512]{2,1,0:T(8,128)(2,1)}, u32[]{:S(2)}) copy-start(bf16[2,128,512]{2,1,0:T(8,128)(2,1)} %copy-done.1) | copy-start | bytes 786436
  101.2 13.8 %collective-permute-start.11 = (bf16[128,1024]{1,0:T(8,128)(2,1)S(1)}, bf16[128,1024]{1,0:T(8,128)(2,1)S(1)}, u32[]{:S(2)}, u32[]{:S(2)}) collective-permute-start(bf16[128,1024]{1,0:T(8,128)(2,1)S(1)} %get-tuple-element.20), channel_id=1, source_target_pairs={{0,8},{8,16},{16,24},{24,0},{1,9},{9,17},{17,25},{25,1},{2,10},{10... | collective-permute-start | bytes 786440 | tf_op jit(solution)/shard_map/ppermute | solution.py:233
  105.2 12.5 %collective-permute-start.12 = (bf16[128,1024]{1,0:T(8,128)(2,1)S(1)}, bf16[128,1024]{1,0:T(8,128)(2,1)S(1)}, u32[]{:S(2)}, u32[]{:S(2)}) collective-permute-start(bf16[128,1024]{1,0:T(8,128)(2,1)S(1)} %get-tuple-element.21), channel_id=1, source_target_pairs={{0,16},{8,24},{16,0},{24,8},{1,17},{9,25},{17,1},{25,9},{2,18},{10... | collective-permute-start | bytes 786440 | tf_op jit(solution)/shard_map/ppermute | solution.py:233
  107.5 13.1 %collective-permute-start.13 = (bf16[128,1024]{1,0:T(8,128)(2,1)S(1)}, bf16[128,1024]{1,0:T(8,128)(2,1)S(1)}, u32[]{:S(2)}, u32[]{:S(2)}) collective-permute-start(bf16[128,1024]{1,0:T(8,128)(2,1)S(1)} %get-tuple-element.22), channel_id=1, source_target_pairs={{0,24},{8,0},{16,8},{24,16},{1,25},{9,1},{17,9},{25,17},{2,26},{10... | collective-permute-start | bytes 786440 | tf_op jit(solution)/shard_map/ppermute | solution.py:233
  130.5 17.4 %all-to-all-start.4 = ((bf16[8,8,16,128]{3,2,1,0:T(8,128)(2,1)}), bf16[8,8,16,128]{3,2,1,0:T(8,128)(2,1)S(1)}, u32[]{:S(2)}, u32[]{:S(2)}) async-start(bf16[8,8,16,128]{3,2,1,0:T(8,128)(2,1)} %shard_map.82), calls=%async_computation.4 | async-start | bytes 524288 | tf_op jit(solution)/shard_map/all_to_all | solution.py:319
  137.4 17.9 %collective-permute-start.7 = (bf16[2,128,512]{2,1,0:T(8,128)(2,1)S(1)}, bf16[2,128,512]{2,1,0:T(8,128)(2,1)S(1)}, u32[]{:S(2)}, u32[]{:S(2)}) collective-permute-start(bf16[2,128,512]{2,1,0:T(8,128)(2,1)S(1)} %copy-done.4), channel_id=1, source_target_pairs={{0,24},{8,0},{16,8},{24,16},{1,25},{9,1},{17,9},{25,17},{2,26},{10... | collective-permute-start | bytes 786440 | tf_op jit(solution)/shard_map/ppermute | solution.py:233
  139.5 15.8 %collective-permute-start.8 = (bf16[2,128,512]{2,1,0:T(8,128)(2,1)S(1)}, bf16[2,128,512]{2,1,0:T(8,128)(2,1)S(1)}, u32[]{:S(2)}, u32[]{:S(2)}) collective-permute-start(bf16[2,128,512]{2,1,0:T(8,128)(2,1)S(1)} %copy-done.2), channel_id=1, source_target_pairs={{0,16},{8,24},{16,0},{24,8},{1,17},{9,25},{17,1},{25,9},{2,18},{10... | collective-permute-start | bytes 786440 | tf_op jit(solution)/shard_map/ppermute | solution.py:233
  144.8 10.6 %collective-permute-start.9 = (bf16[2,128,512]{2,1,0:T(8,128)(2,1)S(1)}, bf16[2,128,512]{2,1,0:T(8,128)(2,1)S(1)}, u32[]{:S(2)}, u32[]{:S(2)}) collective-permute-start(bf16[2,128,512]{2,1,0:T(8,128)(2,1)S(1)} %get-tuple-element.16), channel_id=1, source_target_pairs={{0,8},{8,16},{16,24},{24,0},{1,9},{9,17},{17,25},{25,1},{2,10},{10... | collective-permute-start | bytes 786440 | tf_op jit(solution)/shard_map/ppermute | solution.py:233
  148.5 14.7 %all-to-all-start.5 = ((bf16[16,16,128]{2,1,0:T(8,128)(2,1)}), bf16[16,16,128]{2,1,0:T(8,128)(2,1)S(1)}, u32[]{:S(2)}, u32[]{:S(2)}) async-start(bf16[16,16,128]{2,1,0:T(8,128)(2,1)} %bitcast.7), calls=%async_computation.5 | async-start | bytes 131072 | tf_op jit(solution)/shard_map/all_to_all | solution.py:340
  164.3 38.6 %all-to-all-start.6 = ((bf16[32,16,1024]{2,1,0:T(8,128)(2,1)}), bf16[32,16,1024]{2,1,0:T(8,128)(2,1)S(1)}, u32[]{:S(2)}, u32[]{:S(2)}) async-start(bf16[32,16,1024]{2,1,0:T(8,128)(2,1)} %shard_map.84), calls=%async_computation.6 | async-start | bytes 2097152 | tf_op jit(solution)/shard_map/all_to_all | solution.py:351
  174.7 27.5 %collective-permute-start.10 = (bf16[128,512]{1,0:T(8,128)(2,1)S(1)}, bf16[128,512]{1,0:T(8,128)(2,1)S(1)}, u32[]{:S(2)}, u32[]{:S(2)}) collective-permute-start(bf16[128,512]{1,0:T(8,128)(2,1)S(1)} %get-tuple-element.18.refs_1_), channel_id=1, source_target_pairs={{0,64},{64,0},{1,65},{65,1},{2,66},{66,2},{3,67},{67,3},{4,68},{68... | collective-permute-start | bytes 393224 | tf_op jit(solution)/shard_map/ppermute | solution.py:233
  (2 other events, 1.4 us)

commit v5 on v2

--- a/solution.py
+++ b/solution.py
@@ -111,15 +111,8 @@
             out_ref[k, :, pl.ds(p, BLOCK)] = st_ref[k, :, d * BLOCK : (d + 1) * BLOCK]
 
 
-def grad_kernel(nx, sc_ref, start_ref, st_ref, *refs):
-    q_refs, kv_ref = refs[:nx], refs[nx]
-    dq_refs, dv_ref, acc_ref = refs[nx + 1 : 2 * nx + 1], refs[2 * nx + 1], refs[2 * nx + 2]
-    g, low, high, x = sc_ref[0], sc_ref[1], sc_ref[2], sc_ref[3]
-    places = places_of(x, nx)
-    pos_q = positions_of(g, x, nx)
-    start = lanes_of(start_ref, places)
-    acc_ref[...] = jnp.zeros(acc_ref.shape, jnp.float32)
-    dv_ref[...] = jnp.zeros(dv_ref.shape, dv_ref.dtype)
+def combined(st_ref, places):
+    nx = len(places)
     part = [[lanes_of(st_ref.at[i, k], places) for k in range(3)] for i in range(nx)]
     top = part[0][0]
     for i in range(1, nx):
@@ -130,11 +123,20 @@
         f = jnp.exp2(part[i][0] - top)
         total = total + part[i][1] * f
         num = num + part[i][2] * f
-    log_total = top + jnp.log2(total)
-    delta = num / total
+    return top + jnp.log2(total), num / total
+
+
+def value_kernel(nx, sc_ref, start_ref, st_ref, *refs):
+    q_refs, kv_ref, dv_ref = refs[:nx], refs[nx], refs[nx + 1]
+    g, low, high, x = sc_ref[0], sc_ref[1], sc_ref[2], sc_ref[3]
+    places = places_of(x, nx)
+    pos_q = positions_of(g, x, nx)
+    start = lanes_of(start_ref, places)
+    dv_ref[...] = jnp.zeros(dv_ref.shape, dv_ref.dtype)
+    log_total, _ = combined(st_ref, places)
 
     def step(j, masked):
-        at, k, v = chunk_of(j, kv_ref)
+        at, k, _ = chunk_of(j, kv_ref)
         if masked:
             allowed = allowed_in(j, x, nx, pos_q, start)
         dv = jnp.zeros((CHUNK, HD), jnp.float32)
@@ -143,12 +145,36 @@
             s = lax.dot_general(k, q, NT, preferred_element_type=jnp.float32) * SCALE2
             if masked:
                 s = jnp.where(allowed, s, LOW)
+            p = jnp.exp2(s - log_total[n : n + 1, :])
+            dv = dv + jnp.dot(p.astype(jnp.bfloat16), do, preferred_element_type=jnp.float32)
+        dv_ref[at, :] = dv.astype(dv_ref.dtype)
+
+    over_chunks(g, low, high, nx, step)
+
+
+def query_kernel(nx, sc_ref, start_ref, st_ref, *refs):
+    q_refs, kv_ref, (*dq_refs, done_ref, acc_ref) = refs[:nx], refs[nx], refs[nx + 2 :]
+    done_ref[...] = jnp.zeros(done_ref.shape, done_ref.dtype)
+    g, low, high, x = sc_ref[0], sc_ref[1], sc_ref[2], sc_ref[3]
+    places = places_of(x, nx)
+    pos_q = positions_of(g, x, nx)
+    start = lanes_of(start_ref, places)
+    acc_ref[...] = jnp.zeros(acc_ref.shape, jnp.float32)
+    log_total, delta = combined(st_ref, places)
+
+    def step(j, masked):
+        _, k, v = chunk_of(j, kv_ref)
+        if masked:
+            allowed = allowed_in(j, x, nx, pos_q, start)
+        for n in range(GROUP):
+            q, do = head_of(q_refs, n)
+            s = lax.dot_general(k, q, NT, preferred_element_type=jnp.float32) * SCALE2
+            if masked:
+                s = jnp.where(allowed, s, LOW)
             dp = lax.dot_general(v, do, NT, preferred_element_type=jnp.float32)
             p = jnp.exp2(s - log_total[n : n + 1, :])
             ds = (p * (dp - delta[n : n + 1, :])).astype(jnp.bfloat16)
-            dv = dv + jnp.dot(p.astype(jnp.bfloat16), do, preferred_element_type=jnp.float32)
             acc_ref[n] += lax.dot_general(k, ds, TN, preferred_element_type=jnp.float32)
-        dv_ref[at, :] = dv.astype(dv_ref.dtype)
 
     over_chunks(g, low, high, nx, step)
     for n in range(GROUP):
@@ -166,6 +192,16 @@
         for t in range(tps):
             at = pl.multiple_of(t * share + to, wide)
             out_ref[:, t * wide : (t + 1) * wide] = f_ref[:, pl.ds(at, wide)]
+
+
+def sum_kernel(in_ref, *refs):
+    out_ref = refs[-1]
+    total = in_ref[0].astype(jnp.float32)
+    for i in range(1, in_ref.shape[0]):
+        total = total + in_ref[i].astype(jnp.float32)
+    total = total.astype(out_ref.dtype)
+    for i in range(out_ref.shape[0]):
+        out_ref[i] = total
 
 
 def weight_kernel(nx, sc_ref, v_ref, *refs):
@@ -215,7 +251,8 @@
 
     smem = pl.BlockSpec(memory_space=pltpu.SMEM)
     vmem = pl.BlockSpec(memory_space=pltpu.VMEM)
-    params = pltpu.CompilerParams(vmem_limit_bytes=48 * 1024 * 1024)
+    unread = pl.BlockSpec(memory_space=pl.ANY)
+    params = pltpu.CompilerParams(vmem_limit_bytes=24 * 1024 * 1024)
 
     wide = features.shape[1] // nx
     mine = pl.pallas_call(
@@ -230,32 +267,40 @@
     stats = pl.pallas_call(
         lambda *refs: stats_kernel(nx, *refs),
         out_shape=jax.ShapeDtypeStruct((3, GROUP, span), f32),
-        in_specs=[smem, vmem] + [vmem] * (nx + 1) + [pl.BlockSpec(memory_space=pl.ANY)] * nx,
+        in_specs=[smem, vmem] + [vmem] * (nx + 1) + [unread] * (nx - 1),
         out_specs=vmem,
         scratch_shapes=[pltpu.VMEM((3, GROUP, span), f32)],
         compiler_params=params,
-    )(scalars, start, *qd, kv, *from_x)
+    )(scalars, start, *qd, kv, *from_x[1:])
     all_stats = spread(stats, "x", nx)
-    *dq_parts, dv_part = pl.pallas_call(
-        lambda *refs: grad_kernel(nx, *refs),
+    dv_part = pl.pallas_call(
+        lambda *refs: value_kernel(nx, *refs),
+        out_shape=jax.ShapeDtypeStruct((groups * rows, HD), bf16),
+        in_specs=[smem, vmem, vmem] + [vmem] * (nx + 1),
+        out_specs=vmem,
+        compiler_params=params,
+    )(scalars, start, all_stats, *qd, kv)
+    *dq_parts, done = pl.pallas_call(
+        lambda *refs: query_kernel(nx, *refs),
         out_shape=[jax.ShapeDtypeStruct((rows, GROUP * HD), bf16)] * nx
-        + [jax.ShapeDtypeStruct((groups * rows, HD), bf16)],
-        in_specs=[smem, vmem, vmem] + [vmem] * (nx + 1),
+        + [jax.ShapeDtypeStruct((8, BLOCK), f32)],
+        in_specs=[smem, vmem, vmem] + [vmem] * (nx + 1) + [unread],
         out_specs=[vmem] * (nx + 1),
         scratch_shapes=[pltpu.VMEM((GROUP, HD, span), f32)],
         compiler_params=params,
-    )(scalars, start, all_stats, *qd, kv)
+    )(scalars, start, all_stats, *qd, kv, dv_part)
 
     dv = lax.all_to_all(
         dv_part.reshape(groups, rows, HD), ("y", "zh"), split_axis=0, concat_axis=0, tiled=True
     )
-    dq = dq_parts[0].astype(f32)
-    for d in range(1, nx):
-        dq = dq + shift(dq_parts[d], "x", -d).astype(f32)
-    query_grads = dq.astype(bf16)
-
-    value_b = jnp.sum(dv.astype(f32), axis=0).astype(bf16)
-    value_x = spread(value_b, "x", nx)
+    value_copies = pl.pallas_call(
+        sum_kernel,
+        out_shape=jax.ShapeDtypeStruct((nx, rows, HD), bf16),
+        in_specs=[vmem, vmem],
+        out_specs=vmem,
+        compiler_params=params,
+    )(dv, done)
+    value_x = lax.all_to_all(value_copies, "x", split_axis=0, concat_axis=0, tiled=True)
     part = wide // (tps * ny)
     term = pl.pallas_call(
         lambda *refs: weight_kernel(nx, *refs),
@@ -273,6 +318,10 @@
     own_rows = jnp.sum(turned.astype(f32), axis=0) * (1.0 / math.sqrt(tokens))
     own_rows = own_rows.astype(bf16).transpose(1, 0, 2).reshape(part, tps * HD)
     weight_grad = spread(own_rows, ("x", "y"), nx * ny)
+    dq = dq_parts[0].astype(f32)
+    for d in range(1, nx):
+        dq = dq + shift(dq_parts[d], "x", -d).astype(f32)
+    query_grads = dq.astype(bf16)
     return (query_grads, weight_grad.reshape(wide // tps * nx, tps * HD).astype(f32))
 
 

time: 180 us -> 179 us (level)
  blocking collectives: 78.5 us -> 42.5 us
  starting transfers between devices: 50.2 us -> 65.8 us
  waiting for transfers between devices: 33.3 us -> 46.5 us
  local copies, waits for them, and re-layouts: 4.22 us -> 7.19 us
  Pallas kernels: 5.72 us -> 8.26 us
    all_to_all x1, blocking collectives: 36.6 us -> 8.35 us  [per_device(): lax.all_to_all(value_copies, 'x', split_axis=0, concat_axis=0, tiled=True)]
    all_to_all x0 -> x1, starting transfers between devices: none -> 15.6 us  [per_device(): lax.all_to_all(dv_part.reshape(groups, rows, HD), ('y', 'zh'), split_axis...]
    all_to_all x0 -> x1, waiting for transfers between devices: none -> 14 us  [per_device(): lax.all_to_all(dv_part.reshape(groups, rows, HD), ('y', 'zh'), split_axis...]
    all_to_all x2 -> x1, blocking collectives: 16.7 us -> 8.31 us  [spread(): return lax.all_to_all(copies, axes, split_axis=0, concat_axis=0, tiled=True)]
    unnamed x21 -> x29, local copies, waits for them, and re-layouts: 1.32 us -> 4.28 us
    pallas_call x1 -> x3, Pallas kernels: 2.27 us -> 4.8 us  [the longest x1 2.53 us: per_device(): pl.pallas_call(lambda *refs: value_kernel(nx, *refs), out_shape=jax.Shape...]
  transfers between devices with their start and end apart: 11 -> 12, of which waited for: 7 -> 8; matrix products, arithmetic and copies ran while one was open for 2% -> 2% of each run, Pallas kernels for 0% -> 2%
where the time goes in v5:
time: 179 us; the launch traced here: 176 us
  starting transfers between devices  65.8 us (37%)
  waiting for transfers between devices  46.5 us (26%)
  blocking collectives  42.5 us (24%)
  Pallas kernels  8.26 us (5%)
  local copies, waits for them, and re-layouts  7.19 us (4%)
  other arithmetic  4.89 us (3%)
    ppermute x9, starting transfers between devices, shift(): return lax.ppermute(a, axis, [(i, (i + by) % n) for i in range(n)])  28.7 us
    all_to_all x2, starting transfers between devices, spread(): return lax.all_to_all(copies, axes, split_axis=0, concat_axis=0, tiled=True)  21.5 us
    ppermute x9, waiting for transfers between devices, shift(): return lax.ppermute(a, axis, [(i, (i + by) % n) for i in range(n)])  18.6 us
    all_to_all x1, starting transfers between devices, per_device(): lax.all_to_all(dv_part.reshape(groups, rows, HD), ('y', 'zh'), split_axis...  15.6 us
    all_to_all x1, blocking collectives, per_device(): pieces = lax.all_to_all(term, 'y', split_axis=0, concat_axis=0, tiled=True)  14.4 us
    all_to_all x1, waiting for transfers between devices, per_device(): lax.all_to_all(dv_part.reshape(groups, rows, HD), ('y', 'zh'), split_axis...  14 us
    all_to_all x2, waiting for transfers between devices, spread(): return lax.all_to_all(copies, axes, split_axis=0, concat_axis=0, tiled=True)  13.9 us
    all_to_all x1, blocking collectives, per_device(): lax.all_to_all(jnp.broadcast_to(summed[None], (nzh,) + summed.shape).resh...  11.5 us
  transfers between devices with their start and end apart: 12, of which 8 were waited for; matrix products, arithmetic and copies ran while one was open for 2% of the time, Pallas kernels for 2%

profile of v5, /device:TPU:6, one launch (start us, length us, event | category | flops | bytes accessed | tf_op | source)
XLA Modules:
  0.0 176.1 jit_solution(6363790755291083130)
XLA Ops:
  2.6 15.6 %all-to-all-start = ((bf16[16,128,256]{2,1,0:T(8,128)(2,1)}), bf16[16,128,256]{2,1,0:T(8,128)(2,1)S(1)}, u32[]{:S(2)}, u32[]{:S(2)}) async-start(bf16[16,128,256]{2,1,0:T(8,128)(2,1)} %broadcast_in_dim.24), calls=%async_computation | async-start | bytes 2097152 | tf_op jit(solution)/shard_map/all_to_all | solution.py:222
  18.3 2.7 %collective-permute-start.2 = (bf16[128,1024]{1,0:T(8,128)(2,1)S(1)}, bf16[128,1024]{1,0:T(8,128)(2,1)S(1)}, u32[]{:S(2)}, u32[]{:S(2)}) collective-permute-start(bf16[128,1024]{1,0:T(8,128)(2,1)S(1)} %constant_dynamic-update-slice_fusion.refs_2_.refs_3_), channel_id=1, source_target_pairs={{0,24},{8,0},{16,8},{24,16},{1,25},{9,1},{17,9},{25,17},{2,26},{10... | collective-permute-start | bytes 786440 | tf_op jit(solution)/shard_map/ppermute | solution.py:227
  21.1 3.0 %collective-permute-start.1 = (bf16[128,1024]{1,0:T(8,128)(2,1)S(1)}, bf16[128,1024]{1,0:T(8,128)(2,1)S(1)}, u32[]{:S(2)}, u32[]{:S(2)}) collective-permute-start(bf16[128,1024]{1,0:T(8,128)(2,1)S(1)} %constant_dynamic-update-slice_fusion.refs_2_.refs_3_), channel_id=1, source_target_pairs={{0,16},{8,24},{16,0},{24,8},{1,17},{9,25},{17,1},{25,9},{2,18},{10... | collective-permute-start | bytes 786440 | tf_op jit(solution)/shard_map/ppermute | solution.py:227
  24.1 4.0 %collective-permute-start = (bf16[128,1024]{1,0:T(8,128)(2,1)S(1)}, bf16[128,1024]{1,0:T(8,128)(2,1)S(1)}, u32[]{:S(2)}, u32[]{:S(2)}) collective-permute-start(bf16[128,1024]{1,0:T(8,128)(2,1)S(1)} %constant_dynamic-update-slice_fusion.refs_2_.refs_3_), channel_id=1, source_target_pairs={{0,8},{8,16},{16,24},{24,0},{1,9},{9,17},{17,25},{25,1},{2,10},{10... | collective-permute-start | bytes 786440 | tf_op jit(solution)/shard_map/ppermute | solution.py:227
  32.0 2.8 %collective-permute-start.3 = (bf16[128,1024]{1,0:T(8,128)(2,1)S(1)}, bf16[128,1024]{1,0:T(8,128)(2,1)S(1)}, u32[]{:S(2)}, u32[]{:S(2)}) collective-permute-start(bf16[128,1024]{1,0:T(8,128)(2,1)S(1)} %get-tuple-element.11), channel_id=1, source_target_pairs={{0,8},{8,16},{16,24},{24,0},{1,9},{9,17},{17,25},{25,1},{2,10},{10... | collective-permute-start | bytes 786440 | tf_op jit(solution)/shard_map/ppermute | solution.py:227
  34.8 3.2 %collective-permute-start.4 = (bf16[128,1024]{1,0:T(8,128)(2,1)S(1)}, bf16[128,1024]{1,0:T(8,128)(2,1)S(1)}, u32[]{:S(2)}, u32[]{:S(2)}) collective-permute-start(bf16[128,1024]{1,0:T(8,128)(2,1)S(1)} %get-tuple-element.12), channel_id=1, source_target_pairs={{0,16},{8,24},{16,0},{24,8},{1,17},{9,25},{17,1},{25,9},{2,18},{10... | collective-permute-start | bytes 786440 | tf_op jit(solution)/shard_map/ppermute | solution.py:227
  37.9 3.3 %collective-permute-start.5 = (bf16[128,1024]{1,0:T(8,128)(2,1)S(1)}, bf16[128,1024]{1,0:T(8,128)(2,1)S(1)}, u32[]{:S(2)}, u32[]{:S(2)}) collective-permute-start(bf16[128,1024]{1,0:T(8,128)(2,1)S(1)} %get-tuple-element.13), channel_id=1, source_target_pairs={{0,24},{8,0},{16,8},{24,16},{1,25},{9,1},{17,9},{25,17},{2,26},{10... | collective-permute-start | bytes 786440 | tf_op jit(solution)/shard_map/ppermute | solution.py:227
  41.3 3.4 %collective-permute-done.3.refs_7_.refs_3_ = bf16[128,1024]{1,0:T(8,128)(2,1)S(1)} collective-permute-done((bf16[128,1024]{1,0:T(8,128)(2,1)S(1)}, bf16[128,1024]{1,0:T(8,128)(2,1)S(1)}, u32[]{:S(2)}, u32[]{:S(2)}) %collective-permute-start.3) | collective-permute-done | bytes 262176 | tf_op jit(solution)/shard_map/ppermute | solution.py:227
  47.1 3.4 %collective-permute-done.5.refs_9_.refs_5_ = bf16[128,1024]{1,0:T(8,128)(2,1)S(1)} collective-permute-done((bf16[128,1024]{1,0:T(8,128)(2,1)S(1)}, bf16[128,1024]{1,0:T(8,128)(2,1)S(1)}, u32[]{:S(2)}, u32[]{:S(2)}) %collective-permute-start.5) | collective-permute-done | bytes 262176 | tf_op jit(solution)/shard_map/ppermute | solution.py:227
  50.4 6.8 %all-to-all-done = bf16[16,128,256]{2,1,0:T(8,128)(2,1)S(1)} async-done(((bf16[16,128,256]{2,1,0:T(8,128)(2,1)}), bf16[16,128,256]{2,1,0:T(8,128)(2,1)S(1)}, u32[]{:S(2)}, u32[]{:S(2)}) %all-to-all-start) | async-done | bytes 1048608 | tf_op jit(solution)/shard_map/all_to_all | solution.py:222
  59.0 8.3 %all_to_all.35.refs_2_ = f32[4,3,4,512]{3,2,1,0:T(4,128)S(1)} all-to-all(f32[4,3,4,512]{3,2,1,0:T(4,128)S(1)} %broadcast_in_dim.25), channel_id=1, replica_groups=mesh['y'=8,'zh'=2,'x'=4,'zl'=4,'core'=2] {'x'}, dimensions={0} | all-to-all | bytes 196608 | tf_op jit(solution)/shard_map/all_to_all | solution.py:222
  67.3 2.5 %shard_map.79.refs_8_ = bf16[2048,128]{1,0:T(8,128)(2,1)} custom-call(s32[4]{0:T(128)S(1)} %pad_add_fusion.refs_0_, s32[1,512]{1,0:T(1,128)S(1)} %bitcast.21, f32[4,3,4,512]{3,2,1,0:T(4,128)S(1)} %all_to_all.35.refs_2_, bf16[128,1024]{1,0:T(8,128)(2,1)S(1)} %constant_dynamic-update-slice_fusion.refs_2_.refs_3_, ...), custom_call_target="tpu_custom_call" | custom-call | tf_op jit(solution)/shard_map/pallas_call | solution.py:276
  69.8 15.6 %all-to-all-start.2 = ((bf16[16,128,128]{2,1,0:T(8,128)(2,1)}), bf16[16,128,128]{2,1,0:T(8,128)(2,1)S(1)}, u32[]{:S(2)}, u32[]{:S(2)}) async-start(bf16[16,128,128]{2,1,0:T(8,128)(2,1)} %bitcast.4), calls=%async_computation.2 | async-start | bytes 1048576 | tf_op jit(solution)/shard_map/all_to_all | solution.py:293
  90.2 14.0 %all-to-all-done.2.in_ref = bf16[16,128,128]{2,1,0:T(8,128)(2,1)S(1)} async-done(((bf16[16,128,128]{2,1,0:T(8,128)(2,1)}), bf16[16,128,128]{2,1,0:T(8,128)(2,1)S(1)}, u32[]{:S(2)}, u32[]{:S(2)}) %all-to-all-start.2) | async-done | bytes 524320 | tf_op jit(solution)/shard_map/all_to_all | solution.py:293
  104.3 8.4 %all_to_all.36.refs_1_ = bf16[4,128,128]{2,1,0:T(8,128)(2,1)S(1)} all-to-all(bf16[4,128,128]{2,1,0:T(8,128)(2,1)S(1)} %shard_map.81), channel_id=1, replica_groups=mesh['y'=8,'zh'=2,'x'=4,'zl'=4,'core'=2] {'x'}, dimensions={0} | all-to-all | bytes 262144 | tf_op jit(solution)/shard_map/all_to_all | solution.py:303
  114.5 14.4 %all_to_all.37 = bf16[8,8,16,128]{3,2,1,0:T(8,128)(2,1)S(1)} all-to-all(bf16[8,8,16,128]{3,2,1,0:T(8,128)(2,1)S(1)} %shard_map.82), channel_id=1, replica_groups=mesh['y'=8,'zh'=2,'x'=4,'zl'=4,'core'=2] {'y'}, dimensions={0} | all-to-all | bytes 524288 | tf_op jit(solution)/shard_map/all_to_all | solution.py:312
  129.0 11.5 %all_to_all.38 = bf16[16,16,128]{2,1,0:T(8,128)(2,1)S(1)} all-to-all(bf16[16,16,128]{2,1,0:T(8,128)(2,1)S(1)} %bitcast.23), channel_id=1, replica_groups=mesh['y'=8,'zh'=2,'x'=4,'zl'=4,'core'=2] {'zh','zl','core'}, dimensions={0} | all-to-all | bytes 131072 | tf_op jit(solution)/shard_map/all_to_all | solution.py:314
  141.6 5.8 %all-to-all-start.6 = ((bf16[32,16,1024]{2,1,0:T(8,128)(2,1)}), bf16[32,16,1024]{2,1,0:T(8,128)(2,1)S(1)}, u32[]{:S(2)}, u32[]{:S(2)}) async-start(bf16[32,16,1024]{2,1,0:T(8,128)(2,1)} %broadcast_in_dim.48), calls=%async_computation.6 | async-start | bytes 2097152 | tf_op jit(solution)/shard_map/all_to_all | solution.py:222
  147.4 2.7 %collective-permute-start.6 = (bf16[128,512]{1,0:T(8,128)(2,1)S(1)}, bf16[128,512]{1,0:T(8,128)(2,1)S(1)}, u32[]{:S(2)}, u32[]{:S(2)}) collective-permute-start(bf16[128,512]{1,0:T(8,128)(2,1)S(1)} %copy-done.10), channel_id=1, source_target_pairs={{0,24},{8,0},{16,8},{24,16},{1,25},{9,1},{17,9},{25,17},{2,26},{10... | collective-permute-start | bytes 393224 | tf_op jit(solution)/shard_map/ppermute | solution.py:227
  150.2 2.8 %collective-permute-start.7 = (bf16[128,512]{1,0:T(8,128)(2,1)S(1)}, bf16[128,512]{1,0:T(8,128)(2,1)S(1)}, u32[]{:S(2)}, u32[]{:S(2)}) collective-permute-start(bf16[128,512]{1,0:T(8,128)(2,1)S(1)} %copy-done.8), channel_id=1, source_target_pairs={{0,16},{8,24},{16,0},{24,8},{1,17},{9,25},{17,1},{25,9},{2,18},{10... | collective-permute-start | bytes 393224 | tf_op jit(solution)/shard_map/ppermute | solution.py:227
  152.9 4.2 %collective-permute-start.8 = (bf16[128,512]{1,0:T(8,128)(2,1)S(1)}, bf16[128,512]{1,0:T(8,128)(2,1)S(1)}, u32[]{:S(2)}, u32[]{:S(2)}) collective-permute-start(bf16[128,512]{1,0:T(8,128)(2,1)S(1)} %copy-done.6), channel_id=1, source_target_pairs={{0,8},{8,16},{16,24},{24,0},{1,9},{9,17},{17,25},{25,1},{2,10},{10... | collective-permute-start | bytes 393224 | tf_op jit(solution)/shard_map/ppermute | solution.py:227
  157.2 6.2 %collective-permute-done.6 = bf16[128,512]{1,0:T(8,128)(2,1)S(1)} collective-permute-done((bf16[128,512]{1,0:T(8,128)(2,1)S(1)}, bf16[128,512]{1,0:T(8,128)(2,1)S(1)}, u32[]{:S(2)}, u32[]{:S(2)}) %collective-permute-start.6) | collective-permute-done | bytes 131104 | tf_op jit(solution)/shard_map/ppermute | solution.py:227
  163.3 3.3 %collective-permute-done.8 = bf16[128,512]{1,0:T(8,128)(2,1)S(1)} collective-permute-done((bf16[128,512]{1,0:T(8,128)(2,1)S(1)}, bf16[128,512]{1,0:T(8,128)(2,1)S(1)}, u32[]{:S(2)}, u32[]{:S(2)}) %collective-permute-start.8) | collective-permute-done | bytes 131104 | tf_op jit(solution)/shard_map/ppermute | solution.py:227
  167.4 7.0 %all-to-all-done.6 = bf16[32,16,1024]{2,1,0:T(8,128)(2,1)S(1)} async-done(((bf16[32,16,1024]{2,1,0:T(8,128)(2,1)}), bf16[32,16,1024]{2,1,0:T(8,128)(2,1)S(1)}, u32[]{:S(2)}, u32[]{:S(2)}) %all-to-all-start.6) | async-done | bytes 1048608 | tf_op jit(solution)/shard_map/all_to_all | solution.py:222
  (55 shorter events, 20.1 us)
Async XLA Ops:
  0.6 17.7 %copy-start.11 = (bf16[128,512]{1,0:T(8,128)(2,1)S(1)}, bf16[128,512]{1,0:T(8,128)(2,1)}, u32[]{:S(2)}) copy-start(bf16[128,512]{1,0:T(8,128)(2,1)} %param.6) | copy-start | bytes 393220
  0.6 17.7 %copy-start.12 = (bf16[128,512]{1,0:T(8,128)(2,1)S(1)}, bf16[128,512]{1,0:T(8,128)(2,1)}, u32[]{:S(2)}) copy-start(bf16[128,512]{1,0:T(8,128)(2,1)} %param.9) | copy-start | bytes 393220
  0.7 27.5 %copy-start.13 = (s32[8192]{0:T(1024)S(1)}, s32[8192]{0:T(1024)}, u32[]{:S(2)}) copy-start(s32[8192]{0:T(1024)} %param.11) | copy-start | bytes 98308
  0.7 29.8 %copy-start = (bf16[128,4096]{1,0:T(8,128)(2,1)S(1)}, bf16[128,4096]{1,0:T(8,128)(2,1)}, u32[]{:S(2)}) copy-start(bf16[128,4096]{1,0:T(8,128)(2,1)} %refs_1_.1) | copy-start | bytes 3145732
  2.6 54.6 %all-to-all-start = ((bf16[16,128,256]{2,1,0:T(8,128)(2,1)}), bf16[16,128,256]{2,1,0:T(8,128)(2,1)S(1)}, u32[]{:S(2)}, u32[]{:S(2)}) async-start(bf16[16,128,256]{2,1,0:T(8,128)(2,1)} %broadcast_in_dim.24), calls=%async_computation | async-start | bytes 2097152 | tf_op jit(solution)/shard_map/all_to_all | solution.py:222
  18.3 19.6 %collective-permute-start.2 = (bf16[128,1024]{1,0:T(8,128)(2,1)S(1)}, bf16[128,1024]{1,0:T(8,128)(2,1)S(1)}, u32[]{:S(2)}, u32[]{:S(2)}) collective-permute-start(bf16[128,1024]{1,0:T(8,128)(2,1)S(1)} %constant_dynamic-update-slice_fusion.refs_2_.refs_3_), channel_id=1, source_target_pairs={{0,24},{8,0},{16,8},{24,16},{1,25},{9,1},{17,9},{25,17},{2,26},{10... | collective-permute-start | bytes 786440 | tf_op jit(solution)/shard_map/ppermute | solution.py:227
  21.1 20.2 %collective-permute-start.1 = (bf16[128,1024]{1,0:T(8,128)(2,1)S(1)}, bf16[128,1024]{1,0:T(8,128)(2,1)S(1)}, u32[]{:S(2)}, u32[]{:S(2)}) collective-permute-start(bf16[128,1024]{1,0:T(8,128)(2,1)S(1)} %constant_dynamic-update-slice_fusion.refs_2_.refs_3_), channel_id=1, source_target_pairs={{0,16},{8,24},{16,0},{24,8},{1,17},{9,25},{17,1},{25,9},{2,18},{10... | collective-permute-start | bytes 786440 | tf_op jit(solution)/shard_map/ppermute | solution.py:227
  24.1 17.2 %collective-permute-start = (bf16[128,1024]{1,0:T(8,128)(2,1)S(1)}, bf16[128,1024]{1,0:T(8,128)(2,1)S(1)}, u32[]{:S(2)}, u32[]{:S(2)}) collective-permute-start(bf16[128,1024]{1,0:T(8,128)(2,1)S(1)} %constant_dynamic-update-slice_fusion.refs_2_.refs_3_), channel_id=1, source_target_pairs={{0,8},{8,16},{16,24},{24,0},{1,9},{9,17},{17,25},{25,1},{2,10},{10... | collective-permute-start | bytes 786440 | tf_op jit(solution)/shard_map/ppermute | solution.py:227
  31.3 0.7 copy-start.1
  32.0 12.7 %collective-permute-start.3 = (bf16[128,1024]{1,0:T(8,128)(2,1)S(1)}, bf16[128,1024]{1,0:T(8,128)(2,1)S(1)}, u32[]{:S(2)}, u32[]{:S(2)}) collective-permute-start(bf16[128,1024]{1,0:T(8,128)(2,1)S(1)} %get-tuple-element.11), channel_id=1, source_target_pairs={{0,8},{8,16},{16,24},{24,0},{1,9},{9,17},{17,25},{25,1},{2,10},{10... | collective-permute-start | bytes 786440 | tf_op jit(solution)/shard_map/ppermute | solution.py:227
  34.8 12.3 %collective-permute-start.4 = (bf16[128,1024]{1,0:T(8,128)(2,1)S(1)}, bf16[128,1024]{1,0:T(8,128)(2,1)S(1)}, u32[]{:S(2)}, u32[]{:S(2)}) collective-permute-start(bf16[128,1024]{1,0:T(8,128)(2,1)S(1)} %get-tuple-element.12), channel_id=1, source_target_pairs={{0,16},{8,24},{16,0},{24,8},{1,17},{9,25},{17,1},{25,9},{2,18},{10... | collective-permute-start | bytes 786440 | tf_op jit(solution)/shard_map/ppermute | solution.py:227
  37.9 12.5 %collective-permute-start.5 = (bf16[128,1024]{1,0:T(8,128)(2,1)S(1)}, bf16[128,1024]{1,0:T(8,128)(2,1)S(1)}, u32[]{:S(2)}, u32[]{:S(2)}) collective-permute-start(bf16[128,1024]{1,0:T(8,128)(2,1)S(1)} %get-tuple-element.13), channel_id=1, source_target_pairs={{0,24},{8,0},{16,8},{24,16},{1,25},{9,1},{17,9},{25,17},{2,26},{10... | collective-permute-start | bytes 786440 | tf_op jit(solution)/shard_map/ppermute | solution.py:227
  69.8 34.4 %all-to-all-start.2 = ((bf16[16,128,128]{2,1,0:T(8,128)(2,1)}), bf16[16,128,128]{2,1,0:T(8,128)(2,1)S(1)}, u32[]{:S(2)}, u32[]{:S(2)}) async-start(bf16[16,128,128]{2,1,0:T(8,128)(2,1)} %bitcast.4), calls=%async_computation.2 | async-start | bytes 1048576 | tf_op jit(solution)/shard_map/all_to_all | solution.py:293
  88.3 0.7 copy-start.5
  88.9 0.7 copy-start.7
  112.6 1.0 copy-start.2
  128.9 18.5 %copy-start.10 = (bf16[128,512]{1,0:T(8,128)(2,1)S(1)}, bf16[128,512]{1,0:T(8,128)(2,1)}, u32[]{:S(2)}) copy-start(bf16[128,512]{1,0:T(8,128)(2,1)} %copy-done.9) | copy-start | bytes 393220
  128.9 21.2 %copy-start.8 = (bf16[128,512]{1,0:T(8,128)(2,1)S(1)}, bf16[128,512]{1,0:T(8,128)(2,1)}, u32[]{:S(2)}) copy-start(bf16[128,512]{1,0:T(8,128)(2,1)} %copy-done.7) | copy-start | bytes 393220
  128.9 24.0 %copy-start.6 = (bf16[128,512]{1,0:T(8,128)(2,1)S(1)}, bf16[128,512]{1,0:T(8,128)(2,1)}, u32[]{:S(2)}) copy-start(bf16[128,512]{1,0:T(8,128)(2,1)} %copy-done.5) | copy-start | bytes 393220
  128.9 37.7 %copy-start.4 = (bf16[128,512]{1,0:T(8,128)(2,1)S(1)}, bf16[128,512]{1,0:T(8,128)(2,1)}, u32[]{:S(2)}) copy-start(bf16[128,512]{1,0:T(8,128)(2,1)} %copy-done.3) | copy-start | bytes 393220
  141.6 32.8 %all-to-all-start.6 = ((bf16[32,16,1024]{2,1,0:T(8,128)(2,1)}), bf16[32,16,1024]{2,1,0:T(8,128)(2,1)S(1)}, u32[]{:S(2)}, u32[]{:S(2)}) async-start(bf16[32,16,1024]{2,1,0:T(8,128)(2,1)} %broadcast_in_dim.48), calls=%async_computation.6 | async-start | bytes 2097152 | tf_op jit(solution)/shard_map/all_to_all | solution.py:222
  147.4 15.9 %collective-permute-start.6 = (bf16[128,512]{1,0:T(8,128)(2,1)S(1)}, bf16[128,512]{1,0:T(8,128)(2,1)S(1)}, u32[]{:S(2)}, u32[]{:S(2)}) collective-permute-start(bf16[128,512]{1,0:T(8,128)(2,1)S(1)} %copy-done.10), channel_id=1, source_target_pairs={{0,24},{8,0},{16,8},{24,16},{1,25},{9,1},{17,9},{25,17},{2,26},{10... | collective-permute-start | bytes 393224 | tf_op jit(solution)/shard_map/ppermute | solution.py:227
  150.2 13.2 %collective-permute-start.7 = (bf16[128,512]{1,0:T(8,128)(2,1)S(1)}, bf16[128,512]{1,0:T(8,128)(2,1)S(1)}, u32[]{:S(2)}, u32[]{:S(2)}) collective-permute-start(bf16[128,512]{1,0:T(8,128)(2,1)S(1)} %copy-done.8), channel_id=1, source_target_pairs={{0,16},{8,24},{16,0},{24,8},{1,17},{9,25},{17,1},{25,9},{2,18},{10... | collective-permute-start | bytes 393224 | tf_op jit(solution)/shard_map/ppermute | solution.py:227
  152.9 13.8 %collective-permute-start.8 = (bf16[128,512]{1,0:T(8,128)(2,1)S(1)}, bf16[128,512]{1,0:T(8,128)(2,1)S(1)}, u32[]{:S(2)}, u32[]{:S(2)}) collective-permute-start(bf16[128,512]{1,0:T(8,128)(2,1)S(1)} %copy-done.6), channel_id=1, source_target_pairs={{0,8},{8,16},{16,24},{24,0},{1,9},{9,17},{17,25},{25,1},{2,10},{10... | collective-permute-start | bytes 393224 | tf_op jit(solution)/shard_map/ppermute | solution.py:227
  (2 other events, 1.3 us)

commit v6 on v5

--- a/solution.py
+++ b/solution.py
@@ -14,6 +14,7 @@
 CTX = ("y", "zh", "x")
 TP = ("zl", "core")
 BLOCK = 128
+VM = 16
 CHUNK = 256
 PER = CHUNK // BLOCK
 LOW = -1e30
@@ -38,8 +39,8 @@
     return jnp.concatenate([g * span + p + lane for p in places_of(x, nx)], axis=1)
 
 
-def chunk_of(j, kv_ref):
-    at = pl.ds(pl.multiple_of(j * CHUNK, CHUNK), CHUNK)
+def chunk_of(j, wide, kv_ref):
+    at = pl.ds(pl.multiple_of(j * CHUNK, CHUNK), wide * CHUNK)
     return at, kv_ref[at, 0:HD], kv_ref[at, HD : 2 * HD]
 
 
@@ -59,18 +60,24 @@
     width = PER * nx * BLOCK
     first, last = low // width, g // PER
     clear = jnp.minimum((high + width - 1) // width, last)
+    pairs = (last - clear) // 2
 
     def masked(j, carry):
-        step(j, True)
+        step(j, 1, True)
         return carry
 
-    def free(j, carry):
-        step(j, False)
+    def pair(i, carry):
+        step(clear + 2 * i, 2, False)
         return carry
 
+    def single(j, carry):
+        step(j, 1, False)
+        return carry
+
     lax.fori_loop(first, clear, masked, 0)
-    lax.fori_loop(clear, last, free, 0)
-    step(last, True)
+    lax.fori_loop(0, pairs, pair, 0)
+    lax.fori_loop(clear + 2 * pairs, last, single, 0)
+    step(last, 1, True)
 
 
 def stats_kernel(nx, sc_ref, start_ref, *refs):
@@ -83,27 +90,27 @@
     st_ref[1] = jnp.zeros((GROUP, span), jnp.float32)
     st_ref[2] = jnp.zeros((GROUP, span), jnp.float32)
 
-    def step(j, masked):
-        _, k, v = chunk_of(j, kv_ref)
+    def step(j, wide, masked):
+        _, k, v = chunk_of(j, wide, kv_ref)
         if masked:
             allowed = allowed_in(j, x, nx, pos_q, start)
+        old = [[st_ref[k, n : n + 1, :] for k in range(3)] for n in range(GROUP)]
+        new = []
         for n in range(GROUP):
             q, do = head_of(q_refs, n)
             s = lax.dot_general(k, q, NT, preferred_element_type=jnp.float32) * SCALE2
             if masked:
                 s = jnp.where(allowed, s, LOW)
             dp = lax.dot_general(v, do, NT, preferred_element_type=jnp.float32)
-            m_old = st_ref[0, n : n + 1, :]
+            m_old, l_old, d_old = old[n]
             m = jnp.maximum(m_old, jnp.max(s, axis=0, keepdims=True))
             alpha = jnp.exp2(m_old - m)
             w = jnp.exp2(s - m)
-            st_ref[0, n : n + 1, :] = m
-            st_ref[1, n : n + 1, :] = st_ref[1, n : n + 1, :] * alpha + jnp.sum(
-                w, axis=0, keepdims=True
-            )
-            st_ref[2, n : n + 1, :] = st_ref[2, n : n + 1, :] * alpha + jnp.sum(
-                w * dp, axis=0, keepdims=True
-            )
+            l = l_old * alpha + jnp.sum(w, axis=0, keepdims=True)
+            new.append((m, l, d_old * alpha + jnp.sum(w * dp, axis=0, keepdims=True)))
+        for n in range(GROUP):
+            for k in range(3):
+                st_ref[k, n : n + 1, :] = new[n][k]
 
     over_chunks(g, low, high, nx, step)
     for d, p in enumerate(places_of(x, nx)):
@@ -135,18 +142,22 @@
     dv_ref[...] = jnp.zeros(dv_ref.shape, dv_ref.dtype)
     log_total, _ = combined(st_ref, places)
 
-    def step(j, masked):
-        at, k, _ = chunk_of(j, kv_ref)
+    def step(j, wide, masked):
+        at, k, _ = chunk_of(j, wide, kv_ref)
         if masked:
             allowed = allowed_in(j, x, nx, pos_q, start)
-        dv = jnp.zeros((CHUNK, HD), jnp.float32)
+        heads = [head_of(q_refs, n) for n in range(GROUP)]
+        ps = []
         for n in range(GROUP):
-            q, do = head_of(q_refs, n)
-            s = lax.dot_general(k, q, NT, preferred_element_type=jnp.float32) * SCALE2
+            s = lax.dot_general(k, heads[n][0], NT, preferred_element_type=jnp.float32) * SCALE2
             if masked:
                 s = jnp.where(allowed, s, LOW)
-            p = jnp.exp2(s - log_total[n : n + 1, :])
-            dv = dv + jnp.dot(p.astype(jnp.bfloat16), do, preferred_element_type=jnp.float32)
+            ps.append(jnp.exp2(s - log_total[n : n + 1, :]).astype(jnp.bfloat16))
+        dv = jnp.dot(
+            jnp.concatenate(ps, axis=1),
+            jnp.concatenate([do for _, do in heads], axis=0),
+            preferred_element_type=jnp.float32,
+        )
         dv_ref[at, :] = dv.astype(dv_ref.dtype)
 
     over_chunks(g, low, high, nx, step)
@@ -162,8 +173,8 @@
     acc_ref[...] = jnp.zeros(acc_ref.shape, jnp.float32)
     log_total, delta = combined(st_ref, places)
 
-    def step(j, masked):
-        _, k, v = chunk_of(j, kv_ref)
+    def step(j, wide, masked):
+        _, k, v = chunk_of(j, wide, kv_ref)
         if masked:
             allowed = allowed_in(j, x, nx, pos_q, start)
         for n in range(GROUP):
@@ -252,7 +263,7 @@
     smem = pl.BlockSpec(memory_space=pltpu.SMEM)
     vmem = pl.BlockSpec(memory_space=pltpu.VMEM)
     unread = pl.BlockSpec(memory_space=pl.ANY)
-    params = pltpu.CompilerParams(vmem_limit_bytes=24 * 1024 * 1024)
+    params = pltpu.CompilerParams(vmem_limit_bytes=VM * 1024 * 1024)
 
     wide = features.shape[1] // nx
     mine = pl.pallas_call(

time: 179 us -> 177 us (0.989)
  no operation moved by 1% of the time
where the time goes in v6:
time: 177 us; the launch traced here: 175 us
  starting transfers between devices  64.7 us (37%)
  waiting for transfers between devices  46.3 us (26%)
  blocking collectives  42.5 us (24%)
  Pallas kernels  8.29 us (5%)
  local copies, waits for them, and re-layouts  7.19 us (4%)
  other arithmetic  4.89 us (3%)
    ppermute x9, starting transfers between devices, shift(): return lax.ppermute(a, axis, [(i, (i + by) % n) for i in range(n)])  28.7 us
    all_to_all x2, starting transfers between devices, spread(): return lax.all_to_all(copies, axes, split_axis=0, concat_axis=0, tiled=True)  21.5 us
    ppermute x9, waiting for transfers between devices, shift(): return lax.ppermute(a, axis, [(i, (i + by) % n) for i in range(n)])  18.6 us
    all_to_all x1, starting transfers between devices, per_device(): lax.all_to_all(dv_part.reshape(groups, rows, HD), ('y', 'zh'), split_axis...  14.5 us
    all_to_all x1, blocking collectives, per_device(): pieces = lax.all_to_all(term, 'y', split_axis=0, concat_axis=0, tiled=True)  14.5 us
    all_to_all x2, waiting for transfers between devices, spread(): return lax.all_to_all(copies, axes, split_axis=0, concat_axis=0, tiled=True)  13.9 us
    all_to_all x1, waiting for transfers between devices, per_device(): lax.all_to_all(dv_part.reshape(groups, rows, HD), ('y', 'zh'), split_axis...  13.8 us
    all_to_all x1, blocking collectives, per_device(): lax.all_to_all(jnp.broadcast_to(summed[None], (nzh,) + summed.shape).resh...  11.4 us
  transfers between devices with their start and end apart: 12, of which 8 were waited for; matrix products, arithmetic and copies ran while one was open for 2% of the time, Pallas kernels for 2%

profile of v6, /device:TPU:6, one launch (start us, length us, event | category | flops | bytes accessed | tf_op | source)
XLA Modules:
  0.0 174.8 jit_solution(15677889156678605281)
XLA Ops:
  2.6 15.6 %all-to-all-start = ((bf16[16,128,256]{2,1,0:T(8,128)(2,1)}), bf16[16,128,256]{2,1,0:T(8,128)(2,1)S(1)}, u32[]{:S(2)}, u32[]{:S(2)}) async-start(bf16[16,128,256]{2,1,0:T(8,128)(2,1)} %broadcast_in_dim.24), calls=%async_computation | async-start | bytes 2097152 | tf_op jit(solution)/shard_map/all_to_all | solution.py:233
  18.3 2.7 %collective-permute-start.2 = (bf16[128,1024]{1,0:T(8,128)(2,1)S(1)}, bf16[128,1024]{1,0:T(8,128)(2,1)S(1)}, u32[]{:S(2)}, u32[]{:S(2)}) collective-permute-start(bf16[128,1024]{1,0:T(8,128)(2,1)S(1)} %constant_dynamic-update-slice_fusion.refs_2_.refs_3_), channel_id=1, source_target_pairs={{0,24},{8,0},{16,8},{24,16},{1,25},{9,1},{17,9},{25,17},{2,26},{10... | collective-permute-start | bytes 786440 | tf_op jit(solution)/shard_map/ppermute | solution.py:238
  21.1 3.0 %collective-permute-start.1 = (bf16[128,1024]{1,0:T(8,128)(2,1)S(1)}, bf16[128,1024]{1,0:T(8,128)(2,1)S(1)}, u32[]{:S(2)}, u32[]{:S(2)}) collective-permute-start(bf16[128,1024]{1,0:T(8,128)(2,1)S(1)} %constant_dynamic-update-slice_fusion.refs_2_.refs_3_), channel_id=1, source_target_pairs={{0,16},{8,24},{16,0},{24,8},{1,17},{9,25},{17,1},{25,9},{2,18},{10... | collective-permute-start | bytes 786440 | tf_op jit(solution)/shard_map/ppermute | solution.py:238
  24.1 4.0 %collective-permute-start = (bf16[128,1024]{1,0:T(8,128)(2,1)S(1)}, bf16[128,1024]{1,0:T(8,128)(2,1)S(1)}, u32[]{:S(2)}, u32[]{:S(2)}) collective-permute-start(bf16[128,1024]{1,0:T(8,128)(2,1)S(1)} %constant_dynamic-update-slice_fusion.refs_2_.refs_3_), channel_id=1, source_target_pairs={{0,8},{8,16},{16,24},{24,0},{1,9},{9,17},{17,25},{25,1},{2,10},{10... | collective-permute-start | bytes 786440 | tf_op jit(solution)/shard_map/ppermute | solution.py:238
  32.0 2.8 %collective-permute-start.3 = (bf16[128,1024]{1,0:T(8,128)(2,1)S(1)}, bf16[128,1024]{1,0:T(8,128)(2,1)S(1)}, u32[]{:S(2)}, u32[]{:S(2)}) collective-permute-start(bf16[128,1024]{1,0:T(8,128)(2,1)S(1)} %get-tuple-element.11), channel_id=1, source_target_pairs={{0,8},{8,16},{16,24},{24,0},{1,9},{9,17},{17,25},{25,1},{2,10},{10... | collective-permute-start | bytes 786440 | tf_op jit(solution)/shard_map/ppermute | solution.py:238
  34.8 3.2 %collective-permute-start.4 = (bf16[128,1024]{1,0:T(8,128)(2,1)S(1)}, bf16[128,1024]{1,0:T(8,128)(2,1)S(1)}, u32[]{:S(2)}, u32[]{:S(2)}) collective-permute-start(bf16[128,1024]{1,0:T(8,128)(2,1)S(1)} %get-tuple-element.12), channel_id=1, source_target_pairs={{0,16},{8,24},{16,0},{24,8},{1,17},{9,25},{17,1},{25,9},{2,18},{10... | collective-permute-start | bytes 786440 | tf_op jit(solution)/shard_map/ppermute | solution.py:238
  37.9 3.3 %collective-permute-start.5 = (bf16[128,1024]{1,0:T(8,128)(2,1)S(1)}, bf16[128,1024]{1,0:T(8,128)(2,1)S(1)}, u32[]{:S(2)}, u32[]{:S(2)}) collective-permute-start(bf16[128,1024]{1,0:T(8,128)(2,1)S(1)} %get-tuple-element.13), channel_id=1, source_target_pairs={{0,24},{8,0},{16,8},{24,16},{1,25},{9,1},{17,9},{25,17},{2,26},{10... | collective-permute-start | bytes 786440 | tf_op jit(solution)/shard_map/ppermute | solution.py:238
  41.3 3.4 %collective-permute-done.3.refs_7_.refs_3_ = bf16[128,1024]{1,0:T(8,128)(2,1)S(1)} collective-permute-done((bf16[128,1024]{1,0:T(8,128)(2,1)S(1)}, bf16[128,1024]{1,0:T(8,128)(2,1)S(1)}, u32[]{:S(2)}, u32[]{:S(2)}) %collective-permute-start.3) | collective-permute-done | bytes 262176 | tf_op jit(solution)/shard_map/ppermute | solution.py:238
  47.1 3.4 %collective-permute-done.5.refs_9_.refs_5_ = bf16[128,1024]{1,0:T(8,128)(2,1)S(1)} collective-permute-done((bf16[128,1024]{1,0:T(8,128)(2,1)S(1)}, bf16[128,1024]{1,0:T(8,128)(2,1)S(1)}, u32[]{:S(2)}, u32[]{:S(2)}) %collective-permute-start.5) | collective-permute-done | bytes 262176 | tf_op jit(solution)/shard_map/ppermute | solution.py:238
  50.4 6.8 %all-to-all-done = bf16[16,128,256]{2,1,0:T(8,128)(2,1)S(1)} async-done(((bf16[16,128,256]{2,1,0:T(8,128)(2,1)}), bf16[16,128,256]{2,1,0:T(8,128)(2,1)S(1)}, u32[]{:S(2)}, u32[]{:S(2)}) %all-to-all-start) | async-done | bytes 1048608 | tf_op jit(solution)/shard_map/all_to_all | solution.py:233
  59.0 8.3 %all_to_all.35.refs_2_ = f32[4,3,4,512]{3,2,1,0:T(4,128)S(1)} all-to-all(f32[4,3,4,512]{3,2,1,0:T(4,128)S(1)} %broadcast_in_dim.25), channel_id=1, replica_groups=mesh['y'=8,'zh'=2,'x'=4,'zl'=4,'core'=2] {'x'}, dimensions={0} | all-to-all | bytes 196608 | tf_op jit(solution)/shard_map/all_to_all | solution.py:233
  69.7 14.5 %all-to-all-start.2 = ((bf16[16,128,128]{2,1,0:T(8,128)(2,1)}), bf16[16,128,128]{2,1,0:T(8,128)(2,1)S(1)}, u32[]{:S(2)}, u32[]{:S(2)}) async-start(bf16[16,128,128]{2,1,0:T(8,128)(2,1)} %bitcast.4), calls=%async_computation.2 | async-start | bytes 1048576 | tf_op jit(solution)/shard_map/all_to_all | solution.py:304
  84.2 2.4 %shard_map.80 = (bf16[128,512]{1,0:T(8,128)(2,1)S(1)}, bf16[128,512]{1,0:T(8,128)(2,1)S(1)}, bf16[128,512]{1,0:T(8,128)(2,1)S(1)}, bf16[128,512]{1,0:T(8,128)(2,1)S(1)}, f32[8,128]{1,0:T(8,128)S(1)}) custom-call(s32[4]{0:T(128)S(1)} %pad_add_fusion.refs_0_, s32[1,512]{1,0:T(1,128)S(1)} %bitcast.22, f32[4,3,4,512]{3,2,1,0:T(4,128)S(1)} %all_to_all.35.refs_2_, ...), custom_call_target="tpu_custom_call" | custom-call | tf_op jit(solution)/shard_map/pallas_call | solution.py:294
  89.2 13.8 %all-to-all-done.2.in_ref = bf16[16,128,128]{2,1,0:T(8,128)(2,1)S(1)} async-done(((bf16[16,128,128]{2,1,0:T(8,128)(2,1)}), bf16[16,128,128]{2,1,0:T(8,128)(2,1)S(1)}, u32[]{:S(2)}, u32[]{:S(2)}) %all-to-all-start.2) | async-done | bytes 524320 | tf_op jit(solution)/shard_map/all_to_all | solution.py:304
  103.0 8.4 %all_to_all.36.refs_1_ = bf16[4,128,128]{2,1,0:T(8,128)(2,1)S(1)} all-to-all(bf16[4,128,128]{2,1,0:T(8,128)(2,1)S(1)} %shard_map.81), channel_id=1, replica_groups=mesh['y'=8,'zh'=2,'x'=4,'zl'=4,'core'=2] {'x'}, dimensions={0} | all-to-all | bytes 262144 | tf_op jit(solution)/shard_map/all_to_all | solution.py:314
  113.3 14.5 %all_to_all.37 = bf16[8,8,16,128]{3,2,1,0:T(8,128)(2,1)S(1)} all-to-all(bf16[8,8,16,128]{3,2,1,0:T(8,128)(2,1)S(1)} %shard_map.82), channel_id=1, replica_groups=mesh['y'=8,'zh'=2,'x'=4,'zl'=4,'core'=2] {'y'}, dimensions={0} | all-to-all | bytes 524288 | tf_op jit(solution)/shard_map/all_to_all | solution.py:323
  127.8 11.4 %all_to_all.38 = bf16[16,16,128]{2,1,0:T(8,128)(2,1)S(1)} all-to-all(bf16[16,16,128]{2,1,0:T(8,128)(2,1)S(1)} %bitcast.23), channel_id=1, replica_groups=mesh['y'=8,'zh'=2,'x'=4,'zl'=4,'core'=2] {'zh','zl','core'}, dimensions={0} | all-to-all | bytes 131072 | tf_op jit(solution)/shard_map/all_to_all | solution.py:325
  140.4 5.8 %all-to-all-start.6 = ((bf16[32,16,1024]{2,1,0:T(8,128)(2,1)}), bf16[32,16,1024]{2,1,0:T(8,128)(2,1)S(1)}, u32[]{:S(2)}, u32[]{:S(2)}) async-start(bf16[32,16,1024]{2,1,0:T(8,128)(2,1)} %broadcast_in_dim.48), calls=%async_computation.6 | async-start | bytes 2097152 | tf_op jit(solution)/shard_map/all_to_all | solution.py:233
  146.2 2.7 %collective-permute-start.6 = (bf16[128,512]{1,0:T(8,128)(2,1)S(1)}, bf16[128,512]{1,0:T(8,128)(2,1)S(1)}, u32[]{:S(2)}, u32[]{:S(2)}) collective-permute-start(bf16[128,512]{1,0:T(8,128)(2,1)S(1)} %copy-done.10), channel_id=1, source_target_pairs={{0,24},{8,0},{16,8},{24,16},{1,25},{9,1},{17,9},{25,17},{2,26},{10... | collective-permute-start | bytes 393224 | tf_op jit(solution)/shard_map/ppermute | solution.py:238
  148.9 2.8 %collective-permute-start.7 = (bf16[128,512]{1,0:T(8,128)(2,1)S(1)}, bf16[128,512]{1,0:T(8,128)(2,1)S(1)}, u32[]{:S(2)}, u32[]{:S(2)}) collective-permute-start(bf16[128,512]{1,0:T(8,128)(2,1)S(1)} %copy-done.8), channel_id=1, source_target_pairs={{0,16},{8,24},{16,0},{24,8},{1,17},{9,25},{17,1},{25,9},{2,18},{10... | collective-permute-start | bytes 393224 | tf_op jit(solution)/shard_map/ppermute | solution.py:238
  151.7 4.2 %collective-permute-start.8 = (bf16[128,512]{1,0:T(8,128)(2,1)S(1)}, bf16[128,512]{1,0:T(8,128)(2,1)S(1)}, u32[]{:S(2)}, u32[]{:S(2)}) collective-permute-start(bf16[128,512]{1,0:T(8,128)(2,1)S(1)} %copy-done.6), channel_id=1, source_target_pairs={{0,8},{8,16},{16,24},{24,0},{1,9},{9,17},{17,25},{25,1},{2,10},{10... | collective-permute-start | bytes 393224 | tf_op jit(solution)/shard_map/ppermute | solution.py:238
  155.9 6.2 %collective-permute-done.6 = bf16[128,512]{1,0:T(8,128)(2,1)S(1)} collective-permute-done((bf16[128,512]{1,0:T(8,128)(2,1)S(1)}, bf16[128,512]{1,0:T(8,128)(2,1)S(1)}, u32[]{:S(2)}, u32[]{:S(2)}) %collective-permute-start.6) | collective-permute-done | bytes 131104 | tf_op jit(solution)/shard_map/ppermute | solution.py:238
  162.1 3.3 %collective-permute-done.8 = bf16[128,512]{1,0:T(8,128)(2,1)S(1)} collective-permute-done((bf16[128,512]{1,0:T(8,128)(2,1)S(1)}, bf16[128,512]{1,0:T(8,128)(2,1)S(1)}, u32[]{:S(2)}, u32[]{:S(2)}) %collective-permute-start.8) | collective-permute-done | bytes 131104 | tf_op jit(solution)/shard_map/ppermute | solution.py:238
  166.2 7.0 %all-to-all-done.6 = bf16[32,16,1024]{2,1,0:T(8,128)(2,1)S(1)} async-done(((bf16[32,16,1024]{2,1,0:T(8,128)(2,1)}), bf16[32,16,1024]{2,1,0:T(8,128)(2,1)S(1)}, u32[]{:S(2)}, u32[]{:S(2)}) %all-to-all-start.6) | async-done | bytes 1048608 | tf_op jit(solution)/shard_map/all_to_all | solution.py:233
  (55 shorter events, 20.3 us)
Async XLA Ops:
  0.6 17.7 %copy-start.11 = (bf16[128,512]{1,0:T(8,128)(2,1)S(1)}, bf16[128,512]{1,0:T(8,128)(2,1)}, u32[]{:S(2)}) copy-start(bf16[128,512]{1,0:T(8,128)(2,1)} %param.6) | copy-start | bytes 393220
  0.6 17.7 %copy-start.12 = (bf16[128,512]{1,0:T(8,128)(2,1)S(1)}, bf16[128,512]{1,0:T(8,128)(2,1)}, u32[]{:S(2)}) copy-start(bf16[128,512]{1,0:T(8,128)(2,1)} %param.9) | copy-start | bytes 393220
  0.7 27.5 %copy-start.13 = (s32[8192]{0:T(1024)S(1)}, s32[8192]{0:T(1024)}, u32[]{:S(2)}) copy-start(s32[8192]{0:T(1024)} %param.11) | copy-start | bytes 98308
  0.7 29.8 %copy-start = (bf16[128,4096]{1,0:T(8,128)(2,1)S(1)}, bf16[128,4096]{1,0:T(8,128)(2,1)}, u32[]{:S(2)}) copy-start(bf16[128,4096]{1,0:T(8,128)(2,1)} %refs_1_.1) | copy-start | bytes 3145732
  2.6 54.6 %all-to-all-start = ((bf16[16,128,256]{2,1,0:T(8,128)(2,1)}), bf16[16,128,256]{2,1,0:T(8,128)(2,1)S(1)}, u32[]{:S(2)}, u32[]{:S(2)}) async-start(bf16[16,128,256]{2,1,0:T(8,128)(2,1)} %broadcast_in_dim.24), calls=%async_computation | async-start | bytes 2097152 | tf_op jit(solution)/shard_map/all_to_all | solution.py:233
  18.3 19.6 %collective-permute-start.2 = (bf16[128,1024]{1,0:T(8,128)(2,1)S(1)}, bf16[128,1024]{1,0:T(8,128)(2,1)S(1)}, u32[]{:S(2)}, u32[]{:S(2)}) collective-permute-start(bf16[128,1024]{1,0:T(8,128)(2,1)S(1)} %constant_dynamic-update-slice_fusion.refs_2_.refs_3_), channel_id=1, source_target_pairs={{0,24},{8,0},{16,8},{24,16},{1,25},{9,1},{17,9},{25,17},{2,26},{10... | collective-permute-start | bytes 786440 | tf_op jit(solution)/shard_map/ppermute | solution.py:238
  21.1 20.2 %collective-permute-start.1 = (bf16[128,1024]{1,0:T(8,128)(2,1)S(1)}, bf16[128,1024]{1,0:T(8,128)(2,1)S(1)}, u32[]{:S(2)}, u32[]{:S(2)}) collective-permute-start(bf16[128,1024]{1,0:T(8,128)(2,1)S(1)} %constant_dynamic-update-slice_fusion.refs_2_.refs_3_), channel_id=1, source_target_pairs={{0,16},{8,24},{16,0},{24,8},{1,17},{9,25},{17,1},{25,9},{2,18},{10... | collective-permute-start | bytes 786440 | tf_op jit(solution)/shard_map/ppermute | solution.py:238
  24.1 17.2 %collective-permute-start = (bf16[128,1024]{1,0:T(8,128)(2,1)S(1)}, bf16[128,1024]{1,0:T(8,128)(2,1)S(1)}, u32[]{:S(2)}, u32[]{:S(2)}) collective-permute-start(bf16[128,1024]{1,0:T(8,128)(2,1)S(1)} %constant_dynamic-update-slice_fusion.refs_2_.refs_3_), channel_id=1, source_target_pairs={{0,8},{8,16},{16,24},{24,0},{1,9},{9,17},{17,25},{25,1},{2,10},{10... | collective-permute-start | bytes 786440 | tf_op jit(solution)/shard_map/ppermute | solution.py:238
  31.3 0.7 copy-start.1
  32.0 12.7 %collective-permute-start.3 = (bf16[128,1024]{1,0:T(8,128)(2,1)S(1)}, bf16[128,1024]{1,0:T(8,128)(2,1)S(1)}, u32[]{:S(2)}, u32[]{:S(2)}) collective-permute-start(bf16[128,1024]{1,0:T(8,128)(2,1)S(1)} %get-tuple-element.11), channel_id=1, source_target_pairs={{0,8},{8,16},{16,24},{24,0},{1,9},{9,17},{17,25},{25,1},{2,10},{10... | collective-permute-start | bytes 786440 | tf_op jit(solution)/shard_map/ppermute | solution.py:238
  34.8 12.3 %collective-permute-start.4 = (bf16[128,1024]{1,0:T(8,128)(2,1)S(1)}, bf16[128,1024]{1,0:T(8,128)(2,1)S(1)}, u32[]{:S(2)}, u32[]{:S(2)}) collective-permute-start(bf16[128,1024]{1,0:T(8,128)(2,1)S(1)} %get-tuple-element.12), channel_id=1, source_target_pairs={{0,16},{8,24},{16,0},{24,8},{1,17},{9,25},{17,1},{25,9},{2,18},{10... | collective-permute-start | bytes 786440 | tf_op jit(solution)/shard_map/ppermute | solution.py:238
  37.9 12.5 %collective-permute-start.5 = (bf16[128,1024]{1,0:T(8,128)(2,1)S(1)}, bf16[128,1024]{1,0:T(8,128)(2,1)S(1)}, u32[]{:S(2)}, u32[]{:S(2)}) collective-permute-start(bf16[128,1024]{1,0:T(8,128)(2,1)S(1)} %get-tuple-element.13), channel_id=1, source_target_pairs={{0,24},{8,0},{16,8},{24,16},{1,25},{9,1},{17,9},{25,17},{2,26},{10... | collective-permute-start | bytes 786440 | tf_op jit(solution)/shard_map/ppermute | solution.py:238
  69.7 33.3 %all-to-all-start.2 = ((bf16[16,128,128]{2,1,0:T(8,128)(2,1)}), bf16[16,128,128]{2,1,0:T(8,128)(2,1)S(1)}, u32[]{:S(2)}, u32[]{:S(2)}) async-start(bf16[16,128,128]{2,1,0:T(8,128)(2,1)} %bitcast.4), calls=%async_computation.2 | async-start | bytes 1048576 | tf_op jit(solution)/shard_map/all_to_all | solution.py:304
  87.2 0.7 copy-start.5
  87.9 0.7 copy-start.7
  111.4 1.0 copy-start.2
  127.7 18.4 %copy-start.10 = (bf16[128,512]{1,0:T(8,128)(2,1)S(1)}, bf16[128,512]{1,0:T(8,128)(2,1)}, u32[]{:S(2)}) copy-start(bf16[128,512]{1,0:T(8,128)(2,1)} %copy-done.9) | copy-start | bytes 393220
  127.7 21.2 %copy-start.8 = (bf16[128,512]{1,0:T(8,128)(2,1)S(1)}, bf16[128,512]{1,0:T(8,128)(2,1)}, u32[]{:S(2)}) copy-start(bf16[128,512]{1,0:T(8,128)(2,1)} %copy-done.7) | copy-start | bytes 393220
  127.7 23.9 %copy-start.6 = (bf16[128,512]{1,0:T(8,128)(2,1)S(1)}, bf16[128,512]{1,0:T(8,128)(2,1)}, u32[]{:S(2)}) copy-start(bf16[128,512]{1,0:T(8,128)(2,1)} %copy-done.5) | copy-start | bytes 393220
  127.7 37.7 %copy-start.4 = (bf16[128,512]{1,0:T(8,128)(2,1)S(1)}, bf16[128,512]{1,0:T(8,128)(2,1)}, u32[]{:S(2)}) copy-start(bf16[128,512]{1,0:T(8,128)(2,1)} %copy-done.3) | copy-start | bytes 393220
  140.4 32.8 %all-to-all-start.6 = ((bf16[32,16,1024]{2,1,0:T(8,128)(2,1)}), bf16[32,16,1024]{2,1,0:T(8,128)(2,1)S(1)}, u32[]{:S(2)}, u32[]{:S(2)}) async-start(bf16[32,16,1024]{2,1,0:T(8,128)(2,1)} %broadcast_in_dim.48), calls=%async_computation.6 | async-start | bytes 2097152 | tf_op jit(solution)/shard_map/all_to_all | solution.py:233
  146.2 15.9 %collective-permute-start.6 = (bf16[128,512]{1,0:T(8,128)(2,1)S(1)}, bf16[128,512]{1,0:T(8,128)(2,1)S(1)}, u32[]{:S(2)}, u32[]{:S(2)}) collective-permute-start(bf16[128,512]{1,0:T(8,128)(2,1)S(1)} %copy-done.10), channel_id=1, source_target_pairs={{0,24},{8,0},{16,8},{24,16},{1,25},{9,1},{17,9},{25,17},{2,26},{10... | collective-permute-start | bytes 393224 | tf_op jit(solution)/shard_map/ppermute | solution.py:238
  148.9 13.2 %collective-permute-start.7 = (bf16[128,512]{1,0:T(8,128)(2,1)S(1)}, bf16[128,512]{1,0:T(8,128)(2,1)S(1)}, u32[]{:S(2)}, u32[]{:S(2)}) collective-permute-start(bf16[128,512]{1,0:T(8,128)(2,1)S(1)} %copy-done.8), channel_id=1, source_target_pairs={{0,16},{8,24},{16,0},{24,8},{1,17},{9,25},{17,1},{25,9},{2,18},{10... | collective-permute-start | bytes 393224 | tf_op jit(solution)/shard_map/ppermute | solution.py:238
  151.7 13.8 %collective-permute-start.8 = (bf16[128,512]{1,0:T(8,128)(2,1)S(1)}, bf16[128,512]{1,0:T(8,128)(2,1)S(1)}, u32[]{:S(2)}, u32[]{:S(2)}) collective-permute-start(bf16[128,512]{1,0:T(8,128)(2,1)S(1)} %copy-done.6), channel_id=1, source_target_pairs={{0,8},{8,16},{16,24},{24,0},{1,9},{9,17},{17,25},{25,1},{2,10},{10... | collective-permute-start | bytes 393224 | tf_op jit(solution)/shard_map/ppermute | solution.py:238
  (2 other events, 1.3 us)

commit v7 on v6

--- a/solution.py
+++ b/solution.py
@@ -163,9 +163,8 @@
     over_chunks(g, low, high, nx, step)
 
 
-def query_kernel(nx, sc_ref, start_ref, st_ref, *refs):
-    q_refs, kv_ref, (*dq_refs, done_ref, acc_ref) = refs[:nx], refs[nx], refs[nx + 2 :]
-    done_ref[...] = jnp.zeros(done_ref.shape, done_ref.dtype)
+def query_kernel(nx, heads, sc_ref, start_ref, st_ref, *refs):
+    q_refs, kv_ref, acc_ref = refs[:nx], refs[nx], refs[-1]
     g, low, high, x = sc_ref[0], sc_ref[1], sc_ref[2], sc_ref[3]
     places = places_of(x, nx)
     pos_q = positions_of(g, x, nx)
@@ -177,7 +176,7 @@
         _, k, v = chunk_of(j, wide, kv_ref)
         if masked:
             allowed = allowed_in(j, x, nx, pos_q, start)
-        for n in range(GROUP):
+        for i, n in enumerate(heads):
             q, do = head_of(q_refs, n)
             s = lax.dot_general(k, q, NT, preferred_element_type=jnp.float32) * SCALE2
             if masked:
@@ -185,13 +184,28 @@
             dp = lax.dot_general(v, do, NT, preferred_element_type=jnp.float32)
             p = jnp.exp2(s - log_total[n : n + 1, :])
             ds = (p * (dp - delta[n : n + 1, :])).astype(jnp.bfloat16)
-            acc_ref[n] += lax.dot_general(k, ds, TN, preferred_element_type=jnp.float32)
+            acc_ref[i] += lax.dot_general(k, ds, TN, preferred_element_type=jnp.float32)
 
     over_chunks(g, low, high, nx, step)
-    for n in range(GROUP):
-        dq = (acc_ref[n] * SCALE).T.astype(jnp.bfloat16)
+    return [(acc_ref[i] * SCALE).T.astype(jnp.bfloat16) for i in range(len(heads))]
+
+
+def first_query_kernel(nx, heads, *refs):
+    out_ref = refs[-2]
+    for i, dq in enumerate(query_kernel(nx, heads, *refs)):
         for d in range(nx):
-            dq_refs[d][:, n * HD : (n + 1) * HD] = dq[d * BLOCK : (d + 1) * BLOCK]
+            out_ref[d, :, i * HD : (i + 1) * HD] = dq[d * BLOCK : (d + 1) * BLOCK]
+
+
+def last_query_kernel(nx, heads, *refs):
+    before_ref, dq_refs, done_ref = refs[nx + 4], refs[-2 - nx : -2], refs[-2]
+    done_ref[...] = jnp.zeros(done_ref.shape, done_ref.dtype)
+    wide = before_ref.shape[2]
+    for d in range(nx):
+        dq_refs[d][:, 0:wide] = before_ref[d]
+    for i, dq in enumerate(query_kernel(nx, heads, *refs)):
+        for d in range(nx):
+            dq_refs[d][:, wide + i * HD : wide + (i + 1) * HD] = dq[d * BLOCK : (d + 1) * BLOCK]
 
 
 def regroup_kernel(nx, tps, sc_ref, f_ref, *out_refs):
@@ -215,11 +229,16 @@
         out_ref[i] = total
 
 
-def weight_kernel(nx, sc_ref, v_ref, *refs):
-    f_refs, out_ref = refs[:nx], refs[nx]
+def stack_kernel(*refs):
+    *in_refs, _, out_ref = refs
+    for i, r in enumerate(in_refs):
+        out_ref[i] = r[...]
+
+
+def weight_kernel(nx, sc_ref, v_ref, f_ref, out_ref):
     ny, tps, part, _ = out_ref.shape
     x = sc_ref[3]
-    f = jnp.concatenate([r[...] for r in f_refs], axis=0)
+    f = jnp.concatenate([f_ref[d] for d in range(nx)], axis=0)
     v = jnp.concatenate([v_ref[lax.rem(x + nx - d, nx)] for d in range(nx)], axis=0)
     term = lax.dot_general(v, f, TN, preferred_element_type=jnp.float32).T
     for t in range(tps):
@@ -262,7 +281,7 @@
 
     smem = pl.BlockSpec(memory_space=pltpu.SMEM)
     vmem = pl.BlockSpec(memory_space=pltpu.VMEM)
-    unread = pl.BlockSpec(memory_space=pl.ANY)
+    held = pl.BlockSpec(memory_space=pl.ANY)
     params = pltpu.CompilerParams(vmem_limit_bytes=VM * 1024 * 1024)
 
     wide = features.shape[1] // nx
@@ -278,11 +297,11 @@
     stats = pl.pallas_call(
         lambda *refs: stats_kernel(nx, *refs),
         out_shape=jax.ShapeDtypeStruct((3, GROUP, span), f32),
-        in_specs=[smem, vmem] + [vmem] * (nx + 1) + [unread] * (nx - 1),
+        in_specs=[smem, vmem] + [vmem] * (nx + 1) + [held] * nx,
         out_specs=vmem,
         scratch_shapes=[pltpu.VMEM((3, GROUP, span), f32)],
         compiler_params=params,
-    )(scalars, start, *qd, kv, *from_x[1:])
+    )(scalars, start, *qd, kv, *from_x)
     all_stats = spread(stats, "x", nx)
     dv_part = pl.pallas_call(
         lambda *refs: value_kernel(nx, *refs),
@@ -291,15 +310,23 @@
         out_specs=vmem,
         compiler_params=params,
     )(scalars, start, all_stats, *qd, kv)
-    *dq_parts, done = pl.pallas_call(
-        lambda *refs: query_kernel(nx, *refs),
-        out_shape=[jax.ShapeDtypeStruct((rows, GROUP * HD), bf16)] * nx
-        + [jax.ShapeDtypeStruct((8, BLOCK), f32)],
-        in_specs=[smem, vmem, vmem] + [vmem] * (nx + 1) + [unread],
-        out_specs=[vmem] * (nx + 1),
-        scratch_shapes=[pltpu.VMEM((GROUP, HD, span), f32)],
+    half = GROUP // 2
+    dq_first = pl.pallas_call(
+        lambda *refs: first_query_kernel(nx, range(half), *refs),
+        out_shape=jax.ShapeDtypeStruct((nx, rows, half * HD), bf16),
+        in_specs=[smem, vmem, vmem] + [vmem] * (nx + 1) + [held],
+        out_specs=vmem,
+        scratch_shapes=[pltpu.VMEM((half, HD, span), f32)],
         compiler_params=params,
     )(scalars, start, all_stats, *qd, kv, dv_part)
+
+    f_all = pl.pallas_call(
+        stack_kernel,
+        out_shape=jax.ShapeDtypeStruct((nx, rows, wide), bf16),
+        in_specs=[vmem] * nx + [held],
+        out_specs=vmem,
+        compiler_params=params,
+    )(*from_x, dq_first)
 
     dv = lax.all_to_all(
         dv_part.reshape(groups, rows, HD), ("y", "zh"), split_axis=0, concat_axis=0, tiled=True
@@ -307,23 +334,38 @@
     value_copies = pl.pallas_call(
         sum_kernel,
         out_shape=jax.ShapeDtypeStruct((nx, rows, HD), bf16),
-        in_specs=[vmem, vmem],
-        out_specs=vmem,
-        compiler_params=params,
-    )(dv, done)
+        in_specs=[vmem, held],
+        out_specs=vmem,
+        compiler_params=params,
+    )(dv, f_all)
     value_x = lax.all_to_all(value_copies, "x", split_axis=0, concat_axis=0, tiled=True)
     part = wide // (tps * ny)
     term = pl.pallas_call(
         lambda *refs: weight_kernel(nx, *refs),
         out_shape=jax.ShapeDtypeStruct((ny, tps, part, HD), bf16),
-        in_specs=[smem] + [vmem] * (nx + 1),
-        out_specs=vmem,
-        compiler_params=params,
-    )(scalars, value_x, *from_x)
+        in_specs=[smem, vmem, vmem],
+        out_specs=vmem,
+        compiler_params=params,
+    )(scalars, value_x, f_all)
     pieces = lax.all_to_all(term, "y", split_axis=0, concat_axis=0, tiled=True)
-    summed = jnp.sum(pieces.astype(f32), axis=0).astype(bf16)
+    *dq_parts, done = pl.pallas_call(
+        lambda *refs: last_query_kernel(nx, range(half, GROUP), *refs),
+        out_shape=[jax.ShapeDtypeStruct((rows, GROUP * HD), bf16)] * nx
+        + [jax.ShapeDtypeStruct((8, BLOCK), f32)],
+        in_specs=[smem, vmem, vmem] + [vmem] * (nx + 2) + [held],
+        out_specs=[vmem] * (nx + 1),
+        scratch_shapes=[pltpu.VMEM((GROUP - half, HD, span), f32)],
+        compiler_params=params,
+    )(scalars, start, all_stats, *qd, kv, dq_first, term)
+    row_copies = pl.pallas_call(
+        sum_kernel,
+        out_shape=jax.ShapeDtypeStruct((nzh, tps, part, HD), bf16),
+        in_specs=[vmem, vmem],
+        out_specs=vmem,
+        compiler_params=params,
+    )(pieces, done)
     turned = lax.all_to_all(
-        jnp.broadcast_to(summed[None], (nzh,) + summed.shape).reshape(nzh * tps, part, HD),
+        row_copies.reshape(nzh * tps, part, HD),
         ("zh",) + TP, split_axis=0, concat_axis=0, tiled=True,
     ).reshape(nzh, tps, part, HD)
     own_rows = jnp.sum(turned.astype(f32), axis=0) * (1.0 / math.sqrt(tokens))

time: 177 us -> 180 us (1.017)
  blocking collectives: 42.5 us -> 27.7 us
  waiting for transfers between devices: 46.3 us -> 58.2 us
  starting transfers between devices: 64.7 us -> 70.4 us
  local copies, waits for them, and re-layouts: 7.19 us -> 4.22 us
  Pallas kernels: 8.29 us -> 11 us
    all_to_all x2 -> x1, blocking collectives: 25.9 us -> 11 us  [per_device(): lax.all_to_all(row_copies.reshape(nzh * tps, part, HD), ('zh',) + TP, spl...]
    all_to_all x0 -> x1, waiting for transfers between devices: none -> 8.94 us  [per_device(): pieces = lax.all_to_all(term, 'y', split_axis=0, concat_axis=0, tiled=True)]
    all_to_all x0 -> x1, starting transfers between devices: none -> 4.36 us  [per_device(): pieces = lax.all_to_all(term, 'y', split_axis=0, concat_axis=0, tiled=True)]
    all_to_all x1, waiting for transfers between devices: 13.8 us -> 17.4 us  [per_device(): lax.all_to_all(dv_part.reshape(groups, rows, HD), ('y', 'zh'), split_axis...]
    unnamed x29 -> x25, local copies, waits for them, and re-layouts: 4.28 us -> 1.28 us
  transfers between devices with their start and end apart: 12 -> 13, of which waited for: 8 -> 9; matrix products, arithmetic and copies ran while one was open for 2% -> 2% of each run, Pallas kernels for 2% -> 2%
where the time goes in v7:
time: 180 us; the launch traced here: 177 us
  starting transfers between devices  70.4 us (39%)
  waiting for transfers between devices  58.2 us (32%)
  blocking collectives  27.7 us (15%)
  Pallas kernels  11 us (6%)
  other arithmetic  4.86 us (3%)
  local copies, waits for them, and re-layouts  4.22 us (2%)
    ppermute x9, starting transfers between devices, shift(): return lax.ppermute(a, axis, [(i, (i + by) % n) for i in range(n)])  28.7 us
    all_to_all x2, starting transfers between devices, spread(): return lax.all_to_all(copies, axes, split_axis=0, concat_axis=0, tiled=True)  21.5 us
    ppermute x9, waiting for transfers between devices, shift(): return lax.ppermute(a, axis, [(i, (i + by) % n) for i in range(n)])  18.6 us
    all_to_all x1, waiting for transfers between devices, per_device(): lax.all_to_all(dv_part.reshape(groups, rows, HD), ('y', 'zh'), split_axis...  17.4 us
    all_to_all x1, starting transfers between devices, per_device(): lax.all_to_all(dv_part.reshape(groups, rows, HD), ('y', 'zh'), split_axis...  15.8 us
    all_to_all x2, waiting for transfers between devices, spread(): return lax.all_to_all(copies, axes, split_axis=0, concat_axis=0, tiled=True)  13.2 us
    all_to_all x1, blocking collectives, per_device(): lax.all_to_all(row_copies.reshape(nzh * tps, part, HD), ('zh',) + TP, spl...  11 us
    all_to_all x1, waiting for transfers between devices, per_device(): pieces = lax.all_to_all(term, 'y', split_axis=0, concat_axis=0, tiled=True)  8.94 us
  transfers between devices with their start and end apart: 13, of which 9 were waited for; matrix products, arithmetic and copies ran while one was open for 2% of the time, Pallas kernels for 2%

profile of v7, /device:TPU:6, one launch (start us, length us, event | category | flops | bytes accessed | tf_op | source)
XLA Modules:
  0.0 177.3 jit_solution(1848924311046473692)
XLA Ops:
  2.6 15.6 %all-to-all-start = ((bf16[16,128,256]{2,1,0:T(8,128)(2,1)}), bf16[16,128,256]{2,1,0:T(8,128)(2,1)S(1)}, u32[]{:S(2)}, u32[]{:S(2)}) async-start(bf16[16,128,256]{2,1,0:T(8,128)(2,1)} %broadcast_in_dim.22), calls=%async_computation | async-start | bytes 2097152 | tf_op jit(solution)/shard_map/all_to_all | solution.py:252
  18.3 2.7 %collective-permute-start.2 = (bf16[128,1024]{1,0:T(8,128)(2,1)S(1)}, bf16[128,1024]{1,0:T(8,128)(2,1)S(1)}, u32[]{:S(2)}, u32[]{:S(2)}) collective-permute-start(bf16[128,1024]{1,0:T(8,128)(2,1)S(1)} %constant_dynamic-update-slice_fusion.refs_2_.refs_3_), channel_id=1, source_target_pairs={{0,24},{8,0},{16,8},{24,16},{1,25},{9,1},{17,9},{25,17},{2,26},{10... | collective-permute-start | bytes 786440 | tf_op jit(solution)/shard_map/ppermute | solution.py:257
  21.0 3.0 %collective-permute-start.1 = (bf16[128,1024]{1,0:T(8,128)(2,1)S(1)}, bf16[128,1024]{1,0:T(8,128)(2,1)S(1)}, u32[]{:S(2)}, u32[]{:S(2)}) collective-permute-start(bf16[128,1024]{1,0:T(8,128)(2,1)S(1)} %constant_dynamic-update-slice_fusion.refs_2_.refs_3_), channel_id=1, source_target_pairs={{0,16},{8,24},{16,0},{24,8},{1,17},{9,25},{17,1},{25,9},{2,18},{10... | collective-permute-start | bytes 786440 | tf_op jit(solution)/shard_map/ppermute | solution.py:257
  24.0 4.0 %collective-permute-start = (bf16[128,1024]{1,0:T(8,128)(2,1)S(1)}, bf16[128,1024]{1,0:T(8,128)(2,1)S(1)}, u32[]{:S(2)}, u32[]{:S(2)}) collective-permute-start(bf16[128,1024]{1,0:T(8,128)(2,1)S(1)} %constant_dynamic-update-slice_fusion.refs_2_.refs_3_), channel_id=1, source_target_pairs={{0,8},{8,16},{16,24},{24,0},{1,9},{9,17},{17,25},{25,1},{2,10},{10... | collective-permute-start | bytes 786440 | tf_op jit(solution)/shard_map/ppermute | solution.py:257
  32.6 2.8 %collective-permute-start.3 = (bf16[128,1024]{1,0:T(8,128)(2,1)S(1)}, bf16[128,1024]{1,0:T(8,128)(2,1)S(1)}, u32[]{:S(2)}, u32[]{:S(2)}) collective-permute-start(bf16[128,1024]{1,0:T(8,128)(2,1)S(1)} %get-tuple-element.12), channel_id=1, source_target_pairs={{0,8},{8,16},{16,24},{24,0},{1,9},{9,17},{17,25},{25,1},{2,10},{10... | collective-permute-start | bytes 786440 | tf_op jit(solution)/shard_map/ppermute | solution.py:257
  35.4 3.2 %collective-permute-start.4 = (bf16[128,1024]{1,0:T(8,128)(2,1)S(1)}, bf16[128,1024]{1,0:T(8,128)(2,1)S(1)}, u32[]{:S(2)}, u32[]{:S(2)}) collective-permute-start(bf16[128,1024]{1,0:T(8,128)(2,1)S(1)} %get-tuple-element.13), channel_id=1, source_target_pairs={{0,16},{8,24},{16,0},{24,8},{1,17},{9,25},{17,1},{25,9},{2,18},{10... | collective-permute-start | bytes 786440 | tf_op jit(solution)/shard_map/ppermute | solution.py:257
  38.5 3.3 %collective-permute-start.5 = (bf16[128,1024]{1,0:T(8,128)(2,1)S(1)}, bf16[128,1024]{1,0:T(8,128)(2,1)S(1)}, u32[]{:S(2)}, u32[]{:S(2)}) collective-permute-start(bf16[128,1024]{1,0:T(8,128)(2,1)S(1)} %get-tuple-element.14), channel_id=1, source_target_pairs={{0,24},{8,0},{16,8},{24,16},{1,25},{9,1},{17,9},{25,17},{2,26},{10... | collective-permute-start | bytes 786440 | tf_op jit(solution)/shard_map/ppermute | solution.py:257
  44.4 3.3 %collective-permute-done.4.refs_9_.refs_2_ = bf16[128,1024]{1,0:T(8,128)(2,1)S(1)} collective-permute-done((bf16[128,1024]{1,0:T(8,128)(2,1)S(1)}, bf16[128,1024]{1,0:T(8,128)(2,1)S(1)}, u32[]{:S(2)}, u32[]{:S(2)}) %collective-permute-start.4) | collective-permute-done | bytes 262176 | tf_op jit(solution)/shard_map/ppermute | solution.py:257
  47.6 3.4 %collective-permute-done.5.refs_10_.refs_3_ = bf16[128,1024]{1,0:T(8,128)(2,1)S(1)} collective-permute-done((bf16[128,1024]{1,0:T(8,128)(2,1)S(1)}, bf16[128,1024]{1,0:T(8,128)(2,1)S(1)}, u32[]{:S(2)}, u32[]{:S(2)}) %collective-permute-start.5) | collective-permute-done | bytes 262176 | tf_op jit(solution)/shard_map/ppermute | solution.py:257
  51.0 6.2 %all-to-all-done = bf16[16,128,256]{2,1,0:T(8,128)(2,1)S(1)} async-done(((bf16[16,128,256]{2,1,0:T(8,128)(2,1)}), bf16[16,128,256]{2,1,0:T(8,128)(2,1)S(1)}, u32[]{:S(2)}, u32[]{:S(2)}) %all-to-all-start) | async-done | bytes 1048608 | tf_op jit(solution)/shard_map/all_to_all | solution.py:252
  58.9 8.3 %all_to_all.35.refs_2_ = f32[4,3,4,512]{3,2,1,0:T(4,128)S(1)} all-to-all(f32[4,3,4,512]{3,2,1,0:T(4,128)S(1)} %broadcast_in_dim.23), channel_id=1, replica_groups=mesh['y'=8,'zh'=2,'x'=4,'zl'=4,'core'=2] {'x'}, dimensions={0} | all-to-all | bytes 196608 | tf_op jit(solution)/shard_map/all_to_all | solution.py:252
  69.6 15.8 %all-to-all-start.2 = ((bf16[16,128,128]{2,1,0:T(8,128)(2,1)}), bf16[16,128,128]{2,1,0:T(8,128)(2,1)}, u32[]{:S(2)}, u32[]{:S(2)}) async-start(bf16[16,128,128]{2,1,0:T(8,128)(2,1)} %bitcast.4), calls=%async_computation.2 | async-start | bytes 1048576 | tf_op jit(solution)/shard_map/all_to_all | solution.py:331
  87.3 17.4 %all-to-all-done.2.in_ref = bf16[16,128,128]{2,1,0:T(8,128)(2,1)} async-done(((bf16[16,128,128]{2,1,0:T(8,128)(2,1)}), bf16[16,128,128]{2,1,0:T(8,128)(2,1)}, u32[]{:S(2)}, u32[]{:S(2)}) %all-to-all-start.2) | async-done | bytes 524320 | tf_op jit(solution)/shard_map/all_to_all | solution.py:331
  105.8 8.4 %all_to_all.36.refs_1_ = bf16[4,128,128]{2,1,0:T(8,128)(2,1)S(1)} all-to-all(bf16[4,128,128]{2,1,0:T(8,128)(2,1)S(1)} %shard_map.82), channel_id=1, replica_groups=mesh['y'=8,'zh'=2,'x'=4,'zl'=4,'core'=2] {'x'}, dimensions={0} | all-to-all | bytes 262144 | tf_op jit(solution)/shard_map/all_to_all | solution.py:341
  115.8 4.4 %all-to-all-start.4 = ((bf16[8,8,16,128]{3,2,1,0:T(8,128)(2,1)}), bf16[8,8,16,128]{3,2,1,0:T(8,128)(2,1)S(1)}, u32[]{:S(2)}, u32[]{:S(2)}) async-start(bf16[8,8,16,128]{3,2,1,0:T(8,128)(2,1)} %shard_map.83.refs_9_), calls=%async_computation.4 | async-start | bytes 524288 | tf_op jit(solution)/shard_map/all_to_all | solution.py:350
  121.7 8.9 %all-to-all-done.4.in_ref = bf16[8,8,16,128]{3,2,1,0:T(8,128)(2,1)S(1)} async-done(((bf16[8,8,16,128]{3,2,1,0:T(8,128)(2,1)}), bf16[8,8,16,128]{3,2,1,0:T(8,128)(2,1)S(1)}, u32[]{:S(2)}, u32[]{:S(2)}) %all-to-all-start.4) | async-done | bytes 262176 | tf_op jit(solution)/shard_map/all_to_all | solution.py:350
  130.7 11.0 %all_to_all.37 = bf16[16,16,128]{2,1,0:T(8,128)(2,1)S(1)} all-to-all(bf16[16,16,128]{2,1,0:T(8,128)(2,1)S(1)} %bitcast.21), channel_id=1, replica_groups=mesh['y'=8,'zh'=2,'x'=4,'zl'=4,'core'=2] {'zh','zl','core'}, dimensions={0} | all-to-all | bytes 131072 | tf_op jit(solution)/shard_map/all_to_all | solution.py:367
  142.8 5.8 %all-to-all-start.6 = ((bf16[32,16,1024]{2,1,0:T(8,128)(2,1)}), bf16[32,16,1024]{2,1,0:T(8,128)(2,1)S(1)}, u32[]{:S(2)}, u32[]{:S(2)}) async-start(bf16[32,16,1024]{2,1,0:T(8,128)(2,1)} %broadcast_in_dim.41), calls=%async_computation.6 | async-start | bytes 2097152 | tf_op jit(solution)/shard_map/all_to_all | solution.py:252
  148.7 2.7 %collective-permute-start.6 = (bf16[128,512]{1,0:T(8,128)(2,1)S(1)}, bf16[128,512]{1,0:T(8,128)(2,1)S(1)}, u32[]{:S(2)}, u32[]{:S(2)}) collective-permute-start(bf16[128,512]{1,0:T(8,128)(2,1)S(1)} %get-tuple-element.16), channel_id=1, source_target_pairs={{0,24},{8,0},{16,8},{24,16},{1,25},{9,1},{17,9},{25,17},{2,26},{10... | collective-permute-start | bytes 393224 | tf_op jit(solution)/shard_map/ppermute | solution.py:257
  151.4 2.8 %collective-permute-start.7 = (bf16[128,512]{1,0:T(8,128)(2,1)S(1)}, bf16[128,512]{1,0:T(8,128)(2,1)S(1)}, u32[]{:S(2)}, u32[]{:S(2)}) collective-permute-start(bf16[128,512]{1,0:T(8,128)(2,1)S(1)} %get-tuple-element.17), channel_id=1, source_target_pairs={{0,16},{8,24},{16,0},{24,8},{1,17},{9,25},{17,1},{25,9},{2,18},{10... | collective-permute-start | bytes 393224 | tf_op jit(solution)/shard_map/ppermute | solution.py:257
  154.2 4.2 %collective-permute-start.8 = (bf16[128,512]{1,0:T(8,128)(2,1)S(1)}, bf16[128,512]{1,0:T(8,128)(2,1)S(1)}, u32[]{:S(2)}, u32[]{:S(2)}) collective-permute-start(bf16[128,512]{1,0:T(8,128)(2,1)S(1)} %get-tuple-element.18), channel_id=1, source_target_pairs={{0,8},{8,16},{16,24},{24,0},{1,9},{9,17},{17,25},{25,1},{2,10},{10... | collective-permute-start | bytes 393224 | tf_op jit(solution)/shard_map/ppermute | solution.py:257
  158.4 6.2 %collective-permute-done.6 = bf16[128,512]{1,0:T(8,128)(2,1)S(1)} collective-permute-done((bf16[128,512]{1,0:T(8,128)(2,1)S(1)}, bf16[128,512]{1,0:T(8,128)(2,1)S(1)}, u32[]{:S(2)}, u32[]{:S(2)}) %collective-permute-start.6) | collective-permute-done | bytes 131104 | tf_op jit(solution)/shard_map/ppermute | solution.py:257
  164.6 3.3 %collective-permute-done.8 = bf16[128,512]{1,0:T(8,128)(2,1)S(1)} collective-permute-done((bf16[128,512]{1,0:T(8,128)(2,1)S(1)}, bf16[128,512]{1,0:T(8,128)(2,1)S(1)}, u32[]{:S(2)}, u32[]{:S(2)}) %collective-permute-start.8) | collective-permute-done | bytes 131104 | tf_op jit(solution)/shard_map/ppermute | solution.py:257
  168.6 7.1 %all-to-all-done.6 = bf16[32,16,1024]{2,1,0:T(8,128)(2,1)S(1)} async-done(((bf16[32,16,1024]{2,1,0:T(8,128)(2,1)}), bf16[32,16,1024]{2,1,0:T(8,128)(2,1)S(1)}, u32[]{:S(2)}, u32[]{:S(2)}) %all-to-all-start.6) | async-done | bytes 1048608 | tf_op jit(solution)/shard_map/all_to_all | solution.py:252
  (53 shorter events, 22.6 us)
Async XLA Ops:
  0.6 17.6 %copy-start.9 = (bf16[128,512]{1,0:T(8,128)(2,1)S(1)}, bf16[128,512]{1,0:T(8,128)(2,1)}, u32[]{:S(2)}) copy-start(bf16[128,512]{1,0:T(8,128)(2,1)} %param.6) | copy-start | bytes 393220
  0.6 17.6 %copy-start.10 = (bf16[128,512]{1,0:T(8,128)(2,1)S(1)}, bf16[128,512]{1,0:T(8,128)(2,1)}, u32[]{:S(2)}) copy-start(bf16[128,512]{1,0:T(8,128)(2,1)} %param.9) | copy-start | bytes 393220
  0.7 27.4 %copy-start.11 = (s32[8192]{0:T(1024)S(1)}, s32[8192]{0:T(1024)}, u32[]{:S(2)}) copy-start(s32[8192]{0:T(1024)} %param.11) | copy-start | bytes 98308
  2.6 54.6 %all-to-all-start = ((bf16[16,128,256]{2,1,0:T(8,128)(2,1)}), bf16[16,128,256]{2,1,0:T(8,128)(2,1)S(1)}, u32[]{:S(2)}, u32[]{:S(2)}) async-start(bf16[16,128,256]{2,1,0:T(8,128)(2,1)} %broadcast_in_dim.22), calls=%async_computation | async-start | bytes 2097152 | tf_op jit(solution)/shard_map/all_to_all | solution.py:252
  18.3 20.2 %collective-permute-start.2 = (bf16[128,1024]{1,0:T(8,128)(2,1)S(1)}, bf16[128,1024]{1,0:T(8,128)(2,1)S(1)}, u32[]{:S(2)}, u32[]{:S(2)}) collective-permute-start(bf16[128,1024]{1,0:T(8,128)(2,1)S(1)} %constant_dynamic-update-slice_fusion.refs_2_.refs_3_), channel_id=1, source_target_pairs={{0,24},{8,0},{16,8},{24,16},{1,25},{9,1},{17,9},{25,17},{2,26},{10... | collective-permute-start | bytes 786440 | tf_op jit(solution)/shard_map/ppermute | solution.py:257
  21.0 20.8 %collective-permute-start.1 = (bf16[128,1024]{1,0:T(8,128)(2,1)S(1)}, bf16[128,1024]{1,0:T(8,128)(2,1)S(1)}, u32[]{:S(2)}, u32[]{:S(2)}) collective-permute-start(bf16[128,1024]{1,0:T(8,128)(2,1)S(1)} %constant_dynamic-update-slice_fusion.refs_2_.refs_3_), channel_id=1, source_target_pairs={{0,16},{8,24},{16,0},{24,8},{1,17},{9,25},{17,1},{25,9},{2,18},{10... | collective-permute-start | bytes 786440 | tf_op jit(solution)/shard_map/ppermute | solution.py:257
  24.0 17.8 %collective-permute-start = (bf16[128,1024]{1,0:T(8,128)(2,1)S(1)}, bf16[128,1024]{1,0:T(8,128)(2,1)S(1)}, u32[]{:S(2)}, u32[]{:S(2)}) collective-permute-start(bf16[128,1024]{1,0:T(8,128)(2,1)S(1)} %constant_dynamic-update-slice_fusion.refs_2_.refs_3_), channel_id=1, source_target_pairs={{0,8},{8,16},{16,24},{24,0},{1,9},{9,17},{17,25},{25,1},{2,10},{10... | collective-permute-start | bytes 786440 | tf_op jit(solution)/shard_map/ppermute | solution.py:257
  32.5 37.0 %copy-start = (bf16[128,1024]{1,0:T(8,128)(2,1)}, bf16[128,1024]{1,0:T(8,128)(2,1)S(1)}, u32[]{:S(2)}) copy-start(bf16[128,1024]{1,0:T(8,128)(2,1)S(1)} %get-tuple-element.11.refs_7_.refs_0_) | copy-start | bytes 786436
  32.6 11.8 %collective-permute-start.3 = (bf16[128,1024]{1,0:T(8,128)(2,1)S(1)}, bf16[128,1024]{1,0:T(8,128)(2,1)S(1)}, u32[]{:S(2)}, u32[]{:S(2)}) collective-permute-start(bf16[128,1024]{1,0:T(8,128)(2,1)S(1)} %get-tuple-element.12), channel_id=1, source_target_pairs={{0,8},{8,16},{16,24},{24,0},{1,9},{9,17},{17,25},{25,1},{2,10},{10... | collective-permute-start | bytes 786440 | tf_op jit(solution)/shard_map/ppermute | solution.py:257
  35.4 12.3 %collective-permute-start.4 = (bf16[128,1024]{1,0:T(8,128)(2,1)S(1)}, bf16[128,1024]{1,0:T(8,128)(2,1)S(1)}, u32[]{:S(2)}, u32[]{:S(2)}) collective-permute-start(bf16[128,1024]{1,0:T(8,128)(2,1)S(1)} %get-tuple-element.13), channel_id=1, source_target_pairs={{0,16},{8,24},{16,0},{24,8},{1,17},{9,25},{17,1},{25,9},{2,18},{10... | collective-permute-start | bytes 786440 | tf_op jit(solution)/shard_map/ppermute | solution.py:257
  38.5 12.5 %collective-permute-start.5 = (bf16[128,1024]{1,0:T(8,128)(2,1)S(1)}, bf16[128,1024]{1,0:T(8,128)(2,1)S(1)}, u32[]{:S(2)}, u32[]{:S(2)}) collective-permute-start(bf16[128,1024]{1,0:T(8,128)(2,1)S(1)} %get-tuple-element.14), channel_id=1, source_target_pairs={{0,24},{8,0},{16,8},{24,16},{1,25},{9,1},{17,9},{25,17},{2,26},{10... | collective-permute-start | bytes 786440 | tf_op jit(solution)/shard_map/ppermute | solution.py:257
  44.4 25.2 %copy-start.2 = (bf16[128,1024]{1,0:T(8,128)(2,1)}, bf16[128,1024]{1,0:T(8,128)(2,1)S(1)}, u32[]{:S(2)}) copy-start(bf16[128,1024]{1,0:T(8,128)(2,1)S(1)} %collective-permute-done.3.refs_8_.refs_1_) | copy-start | bytes 786436
  47.6 22.0 %copy-start.4 = (bf16[128,1024]{1,0:T(8,128)(2,1)}, bf16[128,1024]{1,0:T(8,128)(2,1)S(1)}, u32[]{:S(2)}) copy-start(bf16[128,1024]{1,0:T(8,128)(2,1)S(1)} %collective-permute-done.4.refs_9_.refs_2_) | copy-start | bytes 786436
  51.0 18.6 %copy-start.6 = (bf16[128,1024]{1,0:T(8,128)(2,1)}, bf16[128,1024]{1,0:T(8,128)(2,1)S(1)}, u32[]{:S(2)}) copy-start(bf16[128,1024]{1,0:T(8,128)(2,1)S(1)} %collective-permute-done.5.refs_10_.refs_3_) | copy-start | bytes 786436
  69.6 35.0 %all-to-all-start.2 = ((bf16[16,128,128]{2,1,0:T(8,128)(2,1)}), bf16[16,128,128]{2,1,0:T(8,128)(2,1)}, u32[]{:S(2)}, u32[]{:S(2)}) async-start(bf16[16,128,128]{2,1,0:T(8,128)(2,1)} %bitcast.4), calls=%async_computation.2 | async-start | bytes 1048576 | tf_op jit(solution)/shard_map/all_to_all | solution.py:331
  85.4 1.7 copy-start.1
  85.4 1.7 copy-start.3
  85.4 1.7 copy-start.5
  85.4 1.7 copy-start.7
  115.8 14.8 %all-to-all-start.4 = ((bf16[8,8,16,128]{3,2,1,0:T(8,128)(2,1)}), bf16[8,8,16,128]{3,2,1,0:T(8,128)(2,1)S(1)}, u32[]{:S(2)}, u32[]{:S(2)}) async-start(bf16[8,8,16,128]{3,2,1,0:T(8,128)(2,1)} %shard_map.83.refs_9_), calls=%async_computation.4 | async-start | bytes 524288 | tf_op jit(solution)/shard_map/all_to_all | solution.py:350
  142.8 32.8 %all-to-all-start.6 = ((bf16[32,16,1024]{2,1,0:T(8,128)(2,1)}), bf16[32,16,1024]{2,1,0:T(8,128)(2,1)S(1)}, u32[]{:S(2)}, u32[]{:S(2)}) async-start(bf16[32,16,1024]{2,1,0:T(8,128)(2,1)} %broadcast_in_dim.41), calls=%async_computation.6 | async-start | bytes 2097152 | tf_op jit(solution)/shard_map/all_to_all | solution.py:252
  148.7 15.9 %collective-permute-start.6 = (bf16[128,512]{1,0:T(8,128)(2,1)S(1)}, bf16[128,512]{1,0:T(8,128)(2,1)S(1)}, u32[]{:S(2)}, u32[]{:S(2)}) collective-permute-start(bf16[128,512]{1,0:T(8,128)(2,1)S(1)} %get-tuple-element.16), channel_id=1, source_target_pairs={{0,24},{8,0},{16,8},{24,16},{1,25},{9,1},{17,9},{25,17},{2,26},{10... | collective-permute-start | bytes 393224 | tf_op jit(solution)/shard_map/ppermute | solution.py:257
  151.4 13.2 %collective-permute-start.7 = (bf16[128,512]{1,0:T(8,128)(2,1)S(1)}, bf16[128,512]{1,0:T(8,128)(2,1)S(1)}, u32[]{:S(2)}, u32[]{:S(2)}) collective-permute-start(bf16[128,512]{1,0:T(8,128)(2,1)S(1)} %get-tuple-element.17), channel_id=1, source_target_pairs={{0,16},{8,24},{16,0},{24,8},{1,17},{9,25},{17,1},{25,9},{2,18},{10... | collective-permute-start | bytes 393224 | tf_op jit(solution)/shard_map/ppermute | solution.py:257
  154.2 13.8 %collective-permute-start.8 = (bf16[128,512]{1,0:T(8,128)(2,1)S(1)}, bf16[128,512]{1,0:T(8,128)(2,1)S(1)}, u32[]{:S(2)}, u32[]{:S(2)}) collective-permute-start(bf16[128,512]{1,0:T(8,128)(2,1)S(1)} %get-tuple-element.18), channel_id=1, source_target_pairs={{0,8},{8,16},{16,24},{24,0},{1,9},{9,17},{17,25},{25,1},{2,10},{10... | collective-permute-start | bytes 393224 | tf_op jit(solution)/shard_map/ppermute | solution.py:257
  (1 other events, 1.2 us)

commit v8 on v6

--- a/solution.py
+++ b/solution.py
@@ -134,7 +134,7 @@
 
 
 def value_kernel(nx, sc_ref, start_ref, st_ref, *refs):
-    q_refs, kv_ref, dv_ref = refs[:nx], refs[nx], refs[nx + 1]
+    q_refs, kv_ref, dv_ref = refs[:nx], refs[nx], refs[-1]
     g, low, high, x = sc_ref[0], sc_ref[1], sc_ref[2], sc_ref[3]
     places = places_of(x, nx)
     pos_q = positions_of(g, x, nx)
@@ -194,15 +194,16 @@
             dq_refs[d][:, n * HD : (n + 1) * HD] = dq[d * BLOCK : (d + 1) * BLOCK]
 
 
-def regroup_kernel(nx, tps, sc_ref, f_ref, *out_refs):
-    x = sc_ref[3]
+def columns_for(to, nx, tps, f_ref):
     share = f_ref.shape[1] // tps
     wide = share // nx
-    for d, out_ref in enumerate(out_refs):
-        to = lax.rem(x + d, nx) * wide
-        for t in range(tps):
-            at = pl.multiple_of(t * share + to, wide)
-            out_ref[:, t * wide : (t + 1) * wide] = f_ref[:, pl.ds(at, wide)]
+    at = [pl.multiple_of(t * share + to * wide, wide) for t in range(tps)]
+    return jnp.concatenate([f_ref[:, pl.ds(a, wide)] for a in at], axis=1)
+
+
+def regroup_kernel(nx, tps, sc_ref, f_ref, *out_refs):
+    for d, out_ref in enumerate(out_refs, 1):
+        out_ref[...] = columns_for(lax.rem(sc_ref[3] + d, nx), nx, tps, f_ref)
 
 
 def sum_kernel(in_ref, *refs):
@@ -215,11 +216,11 @@
         out_ref[i] = total
 
 
-def weight_kernel(nx, sc_ref, v_ref, *refs):
-    f_refs, out_ref = refs[:nx], refs[nx]
+def weight_kernel(nx, sc_ref, v_ref, own_ref, *refs):
+    *f_refs, out_ref = refs
     ny, tps, part, _ = out_ref.shape
     x = sc_ref[3]
-    f = jnp.concatenate([r[...] for r in f_refs], axis=0)
+    f = jnp.concatenate([columns_for(x, nx, tps, own_ref)] + [r[...] for r in f_refs], axis=0)
     v = jnp.concatenate([v_ref[lax.rem(x + nx - d, nx)] for d in range(nx)], axis=0)
     term = lax.dot_general(v, f, TN, preferred_element_type=jnp.float32).T
     for t in range(tps):
@@ -268,29 +269,29 @@
     wide = features.shape[1] // nx
     mine = pl.pallas_call(
         lambda *refs: regroup_kernel(nx, tps, *refs),
-        out_shape=[jax.ShapeDtypeStruct((rows, wide), bf16)] * nx,
+        out_shape=[jax.ShapeDtypeStruct((rows, wide), bf16)] * (nx - 1),
         in_specs=[smem, vmem],
-        out_specs=[vmem] * nx,
+        out_specs=[vmem] * (nx - 1),
         compiler_params=params,
     )(scalars, features)
-    from_x = [mine[0]] + [shift(mine[d], "x", d) for d in range(1, nx)]
+    from_x = [shift(mine[d - 1], "x", d) for d in range(1, nx)]
 
     stats = pl.pallas_call(
         lambda *refs: stats_kernel(nx, *refs),
         out_shape=jax.ShapeDtypeStruct((3, GROUP, span), f32),
-        in_specs=[smem, vmem] + [vmem] * (nx + 1) + [unread] * (nx - 1),
+        in_specs=[smem, vmem] + [vmem] * (nx + 1),
         out_specs=vmem,
         scratch_shapes=[pltpu.VMEM((3, GROUP, span), f32)],
         compiler_params=params,
-    )(scalars, start, *qd, kv, *from_x[1:])
+    )(scalars, start, *qd, kv)
     all_stats = spread(stats, "x", nx)
     dv_part = pl.pallas_call(
         lambda *refs: value_kernel(nx, *refs),
         out_shape=jax.ShapeDtypeStruct((groups * rows, HD), bf16),
-        in_specs=[smem, vmem, vmem] + [vmem] * (nx + 1),
+        in_specs=[smem, vmem, vmem] + [vmem] * (nx + 1) + [unread] * (nx - 1),
         out_specs=vmem,
         compiler_params=params,
-    )(scalars, start, all_stats, *qd, kv)
+    )(scalars, start, all_stats, *qd, kv, *from_x)
     *dq_parts, done = pl.pallas_call(
         lambda *refs: query_kernel(nx, *refs),
         out_shape=[jax.ShapeDtypeStruct((rows, GROUP * HD), bf16)] * nx
@@ -319,7 +320,7 @@
         in_specs=[smem] + [vmem] * (nx + 1),
         out_specs=vmem,
         compiler_params=params,
-    )(scalars, value_x, *from_x)
+    )(scalars, value_x, features, *from_x)
     pieces = lax.all_to_all(term, "y", split_axis=0, concat_axis=0, tiled=True)
     summed = jnp.sum(pieces.astype(f32), axis=0).astype(bf16)
     turned = lax.all_to_all(

time: 177 us -> 182 us (1.028)
  blocking collectives: 42.5 us -> 34.4 us
  starting transfers between devices: 64.7 us -> 71 us
  waiting for transfers between devices: 46.3 us -> 50.9 us
  Pallas kernels: 8.29 us -> 10.7 us
    all_to_all x2 -> x3, waiting for transfers between devices: 13.9 us -> 26.6 us  [spread(): return lax.all_to_all(copies, axes, split_axis=0, concat_axis=0, tiled=True)]
    ppermute x9, waiting for transfers between devices: 18.6 us -> 9.52 us  [shift(): return lax.ppermute(a, axis, [(i, (i + by) % n) for i in range(n)])]
    all_to_all x1 -> x0, blocking collectives: 8.3 us -> none  [spread(): return lax.all_to_all(copies, axes, split_axis=0, concat_axis=0, tiled=True)]
    all_to_all x2 -> x3, starting transfers between devices: 21.5 us -> 26.2 us  [spread(): return lax.all_to_all(copies, axes, split_axis=0, concat_axis=0, tiled=True)]
    unnamed x29 -> x25, local copies, waits for them, and re-layouts: 4.28 us -> 2.64 us
  transfers between devices with their start and end apart: 12 -> 13, of which waited for: 8 -> 6; matrix products, arithmetic and copies ran while one was open for 2% -> 2% of each run, Pallas kernels for 2% -> 3%
where the time goes in v8:
time: 182 us; the launch traced here: 179 us
  starting transfers between devices  71 us (39%)
  waiting for transfers between devices  50.9 us (28%)
  blocking collectives  34.4 us (19%)
  Pallas kernels  10.7 us (6%)
  local copies, waits for them, and re-layouts  6.19 us (3%)
  other arithmetic  4.89 us (3%)
    ppermute x9, starting transfers between devices, shift(): return lax.ppermute(a, axis, [(i, (i + by) % n) for i in range(n)])  28.7 us
    all_to_all x3, waiting for transfers between devices, spread(): return lax.all_to_all(copies, axes, split_axis=0, concat_axis=0, tiled=True)  26.6 us
    all_to_all x3, starting transfers between devices, spread(): return lax.all_to_all(copies, axes, split_axis=0, concat_axis=0, tiled=True)  26.2 us
    all_to_all x1, starting transfers between devices, per_device(): lax.all_to_all(dv_part.reshape(groups, rows, HD), ('y', 'zh'), split_axis...  16 us
    all_to_all x1, blocking collectives, per_device(): pieces = lax.all_to_all(term, 'y', split_axis=0, concat_axis=0, tiled=True)  15.4 us
    all_to_all x1, waiting for transfers between devices, per_device(): lax.all_to_all(dv_part.reshape(groups, rows, HD), ('y', 'zh'), split_axis...  14.8 us
    all_to_all x1, blocking collectives, per_device(): lax.all_to_all(jnp.broadcast_to(summed[None], (nzh,) + summed.shape).resh...  10.8 us
    ppermute x9, waiting for transfers between devices, shift(): return lax.ppermute(a, axis, [(i, (i + by) % n) for i in range(n)])  9.52 us
  transfers between devices with their start and end apart: 13, of which 6 were waited for; matrix products, arithmetic and copies ran while one was open for 2% of the time, Pallas kernels for 3%

profile of v8, /device:TPU:6, one launch (start us, length us, event | category | flops | bytes accessed | tf_op | source)
XLA Modules:
  0.0 179.0 jit_solution(15847055204905092163)
XLA Ops:
  2.6 15.6 %all-to-all-start = ((bf16[16,128,256]{2,1,0:T(8,128)(2,1)}), bf16[16,128,256]{2,1,0:T(8,128)(2,1)S(1)}, u32[]{:S(2)}, u32[]{:S(2)}) async-start(bf16[16,128,256]{2,1,0:T(8,128)(2,1)} %broadcast_in_dim.24), calls=%async_computation | async-start | bytes 2097152 | tf_op jit(solution)/shard_map/all_to_all | solution.py:234
  18.3 2.7 %collective-permute-start.2 = (bf16[128,1024]{1,0:T(8,128)(2,1)S(1)}, bf16[128,1024]{1,0:T(8,128)(2,1)S(1)}, u32[]{:S(2)}, u32[]{:S(2)}) collective-permute-start(bf16[128,1024]{1,0:T(8,128)(2,1)S(1)} %constant_dynamic-update-slice_fusion.refs_2_.refs_3_), channel_id=1, source_target_pairs={{0,24},{8,0},{16,8},{24,16},{1,25},{9,1},{17,9},{25,17},{2,26},{10... | collective-permute-start | bytes 786440 | tf_op jit(solution)/shard_map/ppermute | solution.py:239
  21.1 3.0 %collective-permute-start.1 = (bf16[128,1024]{1,0:T(8,128)(2,1)S(1)}, bf16[128,1024]{1,0:T(8,128)(2,1)S(1)}, u32[]{:S(2)}, u32[]{:S(2)}) collective-permute-start(bf16[128,1024]{1,0:T(8,128)(2,1)S(1)} %constant_dynamic-update-slice_fusion.refs_2_.refs_3_), channel_id=1, source_target_pairs={{0,16},{8,24},{16,0},{24,8},{1,17},{9,25},{17,1},{25,9},{2,18},{10... | collective-permute-start | bytes 786440 | tf_op jit(solution)/shard_map/ppermute | solution.py:239
  24.1 4.0 %collective-permute-start = (bf16[128,1024]{1,0:T(8,128)(2,1)S(1)}, bf16[128,1024]{1,0:T(8,128)(2,1)S(1)}, u32[]{:S(2)}, u32[]{:S(2)}) collective-permute-start(bf16[128,1024]{1,0:T(8,128)(2,1)S(1)} %constant_dynamic-update-slice_fusion.refs_2_.refs_3_), channel_id=1, source_target_pairs={{0,8},{8,16},{16,24},{24,0},{1,9},{9,17},{17,25},{25,1},{2,10},{10... | collective-permute-start | bytes 786440 | tf_op jit(solution)/shard_map/ppermute | solution.py:239
  32.1 2.8 %collective-permute-start.3 = (bf16[128,1024]{1,0:T(8,128)(2,1)}, bf16[128,1024]{1,0:T(8,128)(2,1)S(1)}, u32[]{:S(2)}, u32[]{:S(2)}) collective-permute-start(bf16[128,1024]{1,0:T(8,128)(2,1)} %get-tuple-element.10), channel_id=1, source_target_pairs={{0,8},{8,16},{16,24},{24,0},{1,9},{9,17},{17,25},{25,1},{2,10},{10... | collective-permute-start | bytes 786440 | tf_op jit(solution)/shard_map/ppermute | solution.py:239
  34.9 3.2 %collective-permute-start.4 = (bf16[128,1024]{1,0:T(8,128)(2,1)}, bf16[128,1024]{1,0:T(8,128)(2,1)}, u32[]{:S(2)}, u32[]{:S(2)}) collective-permute-start(bf16[128,1024]{1,0:T(8,128)(2,1)} %get-tuple-element.11), channel_id=1, source_target_pairs={{0,16},{8,24},{16,0},{24,8},{1,17},{9,25},{17,1},{25,9},{2,18},{10... | collective-permute-start | bytes 786440 | tf_op jit(solution)/shard_map/ppermute | solution.py:239
  38.1 3.3 %collective-permute-start.5 = (bf16[128,1024]{1,0:T(8,128)(2,1)}, bf16[128,1024]{1,0:T(8,128)(2,1)}, u32[]{:S(2)}, u32[]{:S(2)}) collective-permute-start(bf16[128,1024]{1,0:T(8,128)(2,1)} %get-tuple-element.12), channel_id=1, source_target_pairs={{0,24},{8,0},{16,8},{24,16},{1,25},{9,1},{17,9},{25,17},{2,26},{10... | collective-permute-start | bytes 786440 | tf_op jit(solution)/shard_map/ppermute | solution.py:239
  41.4 15.9 %all-to-all-done = bf16[16,128,256]{2,1,0:T(8,128)(2,1)S(1)} async-done(((bf16[16,128,256]{2,1,0:T(8,128)(2,1)}), bf16[16,128,256]{2,1,0:T(8,128)(2,1)S(1)}, u32[]{:S(2)}, u32[]{:S(2)}) %all-to-all-start) | async-done | bytes 1048608 | tf_op jit(solution)/shard_map/all_to_all | solution.py:234
  59.6 4.8 %all-to-all-start.1 = ((f32[4,3,4,512]{3,2,1,0:T(4,128)}), f32[4,3,4,512]{3,2,1,0:T(4,128)S(1)}, u32[]{:S(2)}, u32[]{:S(2)}) async-start(f32[4,3,4,512]{3,2,1,0:T(4,128)} %broadcast_in_dim.25), calls=%async_computation.1 | async-start | bytes 196608 | tf_op jit(solution)/shard_map/all_to_all | solution.py:234
  64.4 3.7 %all-to-all-done.1.refs_2_ = f32[4,3,4,512]{3,2,1,0:T(4,128)S(1)} async-done(((f32[4,3,4,512]{3,2,1,0:T(4,128)}), f32[4,3,4,512]{3,2,1,0:T(4,128)S(1)}, u32[]{:S(2)}, u32[]{:S(2)}) %all-to-all-start.1) | async-done | bytes 98336 | tf_op jit(solution)/shard_map/all_to_all | solution.py:234
  68.1 2.4 %shard_map.79.refs_8_ = bf16[2048,128]{1,0:T(8,128)(2,1)} custom-call(s32[4]{0:T(128)S(1)} %pad_add_fusion.refs_0_, s32[1,512]{1,0:T(1,128)S(1)} %bitcast.21, f32[4,3,4,512]{3,2,1,0:T(4,128)S(1)} %all-to-all-done.1.refs_2_, bf16[128,1024]{1,0:T(8,128)(2,1)S(1)} %constant_dynamic-update-slice_fusion.refs_2_.refs_3_, ...), custom_call_target="tpu_custom_call" | custom-call | tf_op jit(solution)/shard_map/pallas_call | solution.py:288
  70.5 16.0 %all-to-all-start.2 = ((bf16[16,128,128]{2,1,0:T(8,128)(2,1)}), bf16[16,128,128]{2,1,0:T(8,128)(2,1)}, u32[]{:S(2)}, u32[]{:S(2)}) async-start(bf16[16,128,128]{2,1,0:T(8,128)(2,1)} %bitcast.4), calls=%async_computation.2 | async-start | bytes 1048576 | tf_op jit(solution)/shard_map/all_to_all | solution.py:305
  86.5 2.4 %shard_map.80 = (bf16[128,512]{1,0:T(8,128)(2,1)S(1)}, bf16[128,512]{1,0:T(8,128)(2,1)S(1)}, bf16[128,512]{1,0:T(8,128)(2,1)S(1)}, bf16[128,512]{1,0:T(8,128)(2,1)S(1)}, f32[8,128]{1,0:T(8,128)S(1)}) custom-call(s32[4]{0:T(128)S(1)} %pad_add_fusion.refs_0_, s32[1,512]{1,0:T(1,128)S(1)} %bitcast.22, f32[4,3,4,512]{3,2,1,0:T(4,128)S(1)} %all-to-all-done.1.refs_2_, ...), custom_call_target="tpu_custom_call" | custom-call | tf_op jit(solution)/shard_map/pallas_call | solution.py:295
  91.5 14.8 %all-to-all-done.2.in_ref = bf16[16,128,128]{2,1,0:T(8,128)(2,1)} async-done(((bf16[16,128,128]{2,1,0:T(8,128)(2,1)}), bf16[16,128,128]{2,1,0:T(8,128)(2,1)}, u32[]{:S(2)}, u32[]{:S(2)}) %all-to-all-start.2) | async-done | bytes 524320 | tf_op jit(solution)/shard_map/all_to_all | solution.py:305
  107.5 8.3 %all_to_all.35.refs_1_ = bf16[4,128,128]{2,1,0:T(8,128)(2,1)S(1)} all-to-all(bf16[4,128,128]{2,1,0:T(8,128)(2,1)S(1)} %shard_map.81), channel_id=1, replica_groups=mesh['y'=8,'zh'=2,'x'=4,'zl'=4,'core'=2] {'x'}, dimensions={0} | all-to-all | bytes 262144 | tf_op jit(solution)/shard_map/all_to_all | solution.py:315
  117.2 15.4 %all_to_all.36 = bf16[8,8,16,128]{3,2,1,0:T(8,128)(2,1)S(1)} all-to-all(bf16[8,8,16,128]{3,2,1,0:T(8,128)(2,1)S(1)} %shard_map.82), channel_id=1, replica_groups=mesh['y'=8,'zh'=2,'x'=4,'zl'=4,'core'=2] {'y'}, dimensions={0} | all-to-all | bytes 524288 | tf_op jit(solution)/shard_map/all_to_all | solution.py:324
  132.6 10.8 %all_to_all.37 = bf16[16,16,128]{2,1,0:T(8,128)(2,1)S(1)} all-to-all(bf16[16,16,128]{2,1,0:T(8,128)(2,1)S(1)} %bitcast.23), channel_id=1, replica_groups=mesh['y'=8,'zh'=2,'x'=4,'zl'=4,'core'=2] {'zh','zl','core'}, dimensions={0} | all-to-all | bytes 131072 | tf_op jit(solution)/shard_map/all_to_all | solution.py:326
  144.5 5.8 %all-to-all-start.6 = ((bf16[32,16,1024]{2,1,0:T(8,128)(2,1)}), bf16[32,16,1024]{2,1,0:T(8,128)(2,1)S(1)}, u32[]{:S(2)}, u32[]{:S(2)}) async-start(bf16[32,16,1024]{2,1,0:T(8,128)(2,1)} %broadcast_in_dim.48), calls=%async_computation.6 | async-start | bytes 2097152 | tf_op jit(solution)/shard_map/all_to_all | solution.py:234
  150.4 2.7 %collective-permute-start.6 = (bf16[128,512]{1,0:T(8,128)(2,1)S(1)}, bf16[128,512]{1,0:T(8,128)(2,1)S(1)}, u32[]{:S(2)}, u32[]{:S(2)}) collective-permute-start(bf16[128,512]{1,0:T(8,128)(2,1)S(1)} %copy-done.8), channel_id=1, source_target_pairs={{0,24},{8,0},{16,8},{24,16},{1,25},{9,1},{17,9},{25,17},{2,26},{10... | collective-permute-start | bytes 393224 | tf_op jit(solution)/shard_map/ppermute | solution.py:239
  153.1 2.8 %collective-permute-start.7 = (bf16[128,512]{1,0:T(8,128)(2,1)S(1)}, bf16[128,512]{1,0:T(8,128)(2,1)S(1)}, u32[]{:S(2)}, u32[]{:S(2)}) collective-permute-start(bf16[128,512]{1,0:T(8,128)(2,1)S(1)} %copy-done.6), channel_id=1, source_target_pairs={{0,16},{8,24},{16,0},{24,8},{1,17},{9,25},{17,1},{25,9},{2,18},{10... | collective-permute-start | bytes 393224 | tf_op jit(solution)/shard_map/ppermute | solution.py:239
  155.9 4.2 %collective-permute-start.8 = (bf16[128,512]{1,0:T(8,128)(2,1)S(1)}, bf16[128,512]{1,0:T(8,128)(2,1)S(1)}, u32[]{:S(2)}, u32[]{:S(2)}) collective-permute-start(bf16[128,512]{1,0:T(8,128)(2,1)S(1)} %copy-done.4), channel_id=1, source_target_pairs={{0,8},{8,16},{16,24},{24,0},{1,9},{9,17},{17,25},{25,1},{2,10},{10... | collective-permute-start | bytes 393224 | tf_op jit(solution)/shard_map/ppermute | solution.py:239
  160.1 6.2 %collective-permute-done.6 = bf16[128,512]{1,0:T(8,128)(2,1)S(1)} collective-permute-done((bf16[128,512]{1,0:T(8,128)(2,1)S(1)}, bf16[128,512]{1,0:T(8,128)(2,1)S(1)}, u32[]{:S(2)}, u32[]{:S(2)}) %collective-permute-start.6) | collective-permute-done | bytes 131104 | tf_op jit(solution)/shard_map/ppermute | solution.py:239
  166.3 3.3 %collective-permute-done.8 = bf16[128,512]{1,0:T(8,128)(2,1)S(1)} collective-permute-done((bf16[128,512]{1,0:T(8,128)(2,1)S(1)}, bf16[128,512]{1,0:T(8,128)(2,1)S(1)}, u32[]{:S(2)}, u32[]{:S(2)}) %collective-permute-start.8) | collective-permute-done | bytes 131104 | tf_op jit(solution)/shard_map/ppermute | solution.py:239
  170.3 7.0 %all-to-all-done.6 = bf16[32,16,1024]{2,1,0:T(8,128)(2,1)S(1)} async-done(((bf16[32,16,1024]{2,1,0:T(8,128)(2,1)}), bf16[32,16,1024]{2,1,0:T(8,128)(2,1)S(1)}, u32[]{:S(2)}, u32[]{:S(2)}) %all-to-all-start.6) | async-done | bytes 1048608 | tf_op jit(solution)/shard_map/all_to_all | solution.py:234
  (52 shorter events, 17.0 us)
Async XLA Ops:
  0.6 17.7 %copy-start.9 = (bf16[128,512]{1,0:T(8,128)(2,1)S(1)}, bf16[128,512]{1,0:T(8,128)(2,1)}, u32[]{:S(2)}) copy-start(bf16[128,512]{1,0:T(8,128)(2,1)} %param.6) | copy-start | bytes 393220
  0.6 17.7 %copy-start.10 = (bf16[128,512]{1,0:T(8,128)(2,1)S(1)}, bf16[128,512]{1,0:T(8,128)(2,1)}, u32[]{:S(2)}) copy-start(bf16[128,512]{1,0:T(8,128)(2,1)} %param.9) | copy-start | bytes 393220
  0.7 27.5 %copy-start.11 = (s32[8192]{0:T(1024)S(1)}, s32[8192]{0:T(1024)}, u32[]{:S(2)}) copy-start(s32[8192]{0:T(1024)} %param.11) | copy-start | bytes 98308
  0.7 29.8 %copy-start = (bf16[128,4096]{1,0:T(8,128)(2,1)S(1)}, bf16[128,4096]{1,0:T(8,128)(2,1)}, u32[]{:S(2)}) copy-start(bf16[128,4096]{1,0:T(8,128)(2,1)} %refs_2_.1) | copy-start | bytes 3145732
  2.6 54.6 %all-to-all-start = ((bf16[16,128,256]{2,1,0:T(8,128)(2,1)}), bf16[16,128,256]{2,1,0:T(8,128)(2,1)S(1)}, u32[]{:S(2)}, u32[]{:S(2)}) async-start(bf16[16,128,256]{2,1,0:T(8,128)(2,1)} %broadcast_in_dim.24), calls=%async_computation | async-start | bytes 2097152 | tf_op jit(solution)/shard_map/all_to_all | solution.py:234
  18.3 19.7 %collective-permute-start.2 = (bf16[128,1024]{1,0:T(8,128)(2,1)S(1)}, bf16[128,1024]{1,0:T(8,128)(2,1)S(1)}, u32[]{:S(2)}, u32[]{:S(2)}) collective-permute-start(bf16[128,1024]{1,0:T(8,128)(2,1)S(1)} %constant_dynamic-update-slice_fusion.refs_2_.refs_3_), channel_id=1, source_target_pairs={{0,24},{8,0},{16,8},{24,16},{1,25},{9,1},{17,9},{25,17},{2,26},{10... | collective-permute-start | bytes 786440 | tf_op jit(solution)/shard_map/ppermute | solution.py:239
  21.1 20.3 %collective-permute-start.1 = (bf16[128,1024]{1,0:T(8,128)(2,1)S(1)}, bf16[128,1024]{1,0:T(8,128)(2,1)S(1)}, u32[]{:S(2)}, u32[]{:S(2)}) collective-permute-start(bf16[128,1024]{1,0:T(8,128)(2,1)S(1)} %constant_dynamic-update-slice_fusion.refs_2_.refs_3_), channel_id=1, source_target_pairs={{0,16},{8,24},{16,0},{24,8},{1,17},{9,25},{17,1},{25,9},{2,18},{10... | collective-permute-start | bytes 786440 | tf_op jit(solution)/shard_map/ppermute | solution.py:239
  24.1 17.3 %collective-permute-start = (bf16[128,1024]{1,0:T(8,128)(2,1)S(1)}, bf16[128,1024]{1,0:T(8,128)(2,1)S(1)}, u32[]{:S(2)}, u32[]{:S(2)}) collective-permute-start(bf16[128,1024]{1,0:T(8,128)(2,1)S(1)} %constant_dynamic-update-slice_fusion.refs_2_.refs_3_), channel_id=1, source_target_pairs={{0,8},{8,16},{16,24},{24,0},{1,9},{9,17},{17,25},{25,1},{2,10},{10... | collective-permute-start | bytes 786440 | tf_op jit(solution)/shard_map/ppermute | solution.py:239
  32.1 32.3 %collective-permute-start.3 = (bf16[128,1024]{1,0:T(8,128)(2,1)}, bf16[128,1024]{1,0:T(8,128)(2,1)S(1)}, u32[]{:S(2)}, u32[]{:S(2)}) collective-permute-start(bf16[128,1024]{1,0:T(8,128)(2,1)} %get-tuple-element.10), channel_id=1, source_target_pairs={{0,8},{8,16},{16,24},{24,0},{1,9},{9,17},{17,25},{25,1},{2,10},{10... | collective-permute-start | bytes 786440 | tf_op jit(solution)/shard_map/ppermute | solution.py:239
  34.9 29.5 %collective-permute-start.4 = (bf16[128,1024]{1,0:T(8,128)(2,1)}, bf16[128,1024]{1,0:T(8,128)(2,1)}, u32[]{:S(2)}, u32[]{:S(2)}) collective-permute-start(bf16[128,1024]{1,0:T(8,128)(2,1)} %get-tuple-element.11), channel_id=1, source_target_pairs={{0,16},{8,24},{16,0},{24,8},{1,17},{9,25},{17,1},{25,9},{2,18},{10... | collective-permute-start | bytes 786440 | tf_op jit(solution)/shard_map/ppermute | solution.py:239
  38.1 26.3 %collective-permute-start.5 = (bf16[128,1024]{1,0:T(8,128)(2,1)}, bf16[128,1024]{1,0:T(8,128)(2,1)}, u32[]{:S(2)}, u32[]{:S(2)}) collective-permute-start(bf16[128,1024]{1,0:T(8,128)(2,1)} %get-tuple-element.12), channel_id=1, source_target_pairs={{0,24},{8,0},{16,8},{24,16},{1,25},{9,1},{17,9},{25,17},{2,26},{10... | collective-permute-start | bytes 786440 | tf_op jit(solution)/shard_map/ppermute | solution.py:239
  59.6 8.5 %all-to-all-start.1 = ((f32[4,3,4,512]{3,2,1,0:T(4,128)}), f32[4,3,4,512]{3,2,1,0:T(4,128)S(1)}, u32[]{:S(2)}, u32[]{:S(2)}) async-start(f32[4,3,4,512]{3,2,1,0:T(4,128)} %broadcast_in_dim.25), calls=%async_computation.1 | async-start | bytes 196608 | tf_op jit(solution)/shard_map/all_to_all | solution.py:234
  70.5 35.8 %all-to-all-start.2 = ((bf16[16,128,128]{2,1,0:T(8,128)(2,1)}), bf16[16,128,128]{2,1,0:T(8,128)(2,1)}, u32[]{:S(2)}, u32[]{:S(2)}) async-start(bf16[16,128,128]{2,1,0:T(8,128)(2,1)} %bitcast.4), calls=%async_computation.2 | async-start | bytes 1048576 | tf_op jit(solution)/shard_map/all_to_all | solution.py:305
  88.9 0.7 copy-start.1
  89.6 0.7 copy-start.3
  90.9 0.7 copy-start.7
  132.6 17.8 %copy-start.8 = (bf16[128,512]{1,0:T(8,128)(2,1)S(1)}, bf16[128,512]{1,0:T(8,128)(2,1)}, u32[]{:S(2)}) copy-start(bf16[128,512]{1,0:T(8,128)(2,1)} %copy-done.7) | copy-start | bytes 393220
  132.6 20.5 %copy-start.6 = (bf16[128,512]{1,0:T(8,128)(2,1)S(1)}, bf16[128,512]{1,0:T(8,128)(2,1)}, u32[]{:S(2)}) copy-start(bf16[128,512]{1,0:T(8,128)(2,1)} %copy-done.5) | copy-start | bytes 393220
  132.6 23.3 %copy-start.4 = (bf16[128,512]{1,0:T(8,128)(2,1)S(1)}, bf16[128,512]{1,0:T(8,128)(2,1)}, u32[]{:S(2)}) copy-start(bf16[128,512]{1,0:T(8,128)(2,1)} %copy-done.3) | copy-start | bytes 393220
  132.6 37.1 %copy-start.2 = (bf16[128,512]{1,0:T(8,128)(2,1)S(1)}, bf16[128,512]{1,0:T(8,128)(2,1)}, u32[]{:S(2)}) copy-start(bf16[128,512]{1,0:T(8,128)(2,1)} %copy-done.1) | copy-start | bytes 393220
  144.5 32.8 %all-to-all-start.6 = ((bf16[32,16,1024]{2,1,0:T(8,128)(2,1)}), bf16[32,16,1024]{2,1,0:T(8,128)(2,1)S(1)}, u32[]{:S(2)}, u32[]{:S(2)}) async-start(bf16[32,16,1024]{2,1,0:T(8,128)(2,1)} %broadcast_in_dim.48), calls=%async_computation.6 | async-start | bytes 2097152 | tf_op jit(solution)/shard_map/all_to_all | solution.py:234
  150.4 15.9 %collective-permute-start.6 = (bf16[128,512]{1,0:T(8,128)(2,1)S(1)}, bf16[128,512]{1,0:T(8,128)(2,1)S(1)}, u32[]{:S(2)}, u32[]{:S(2)}) collective-permute-start(bf16[128,512]{1,0:T(8,128)(2,1)S(1)} %copy-done.8), channel_id=1, source_target_pairs={{0,24},{8,0},{16,8},{24,16},{1,25},{9,1},{17,9},{25,17},{2,26},{10... | collective-permute-start | bytes 393224 | tf_op jit(solution)/shard_map/ppermute | solution.py:239
  153.1 13.2 %collective-permute-start.7 = (bf16[128,512]{1,0:T(8,128)(2,1)S(1)}, bf16[128,512]{1,0:T(8,128)(2,1)S(1)}, u32[]{:S(2)}, u32[]{:S(2)}) collective-permute-start(bf16[128,512]{1,0:T(8,128)(2,1)S(1)} %copy-done.6), channel_id=1, source_target_pairs={{0,16},{8,24},{16,0},{24,8},{1,17},{9,25},{17,1},{25,9},{2,18},{10... | collective-permute-start | bytes 393224 | tf_op jit(solution)/shard_map/ppermute | solution.py:239
  155.9 13.8 %collective-permute-start.8 = (bf16[128,512]{1,0:T(8,128)(2,1)S(1)}, bf16[128,512]{1,0:T(8,128)(2,1)S(1)}, u32[]{:S(2)}, u32[]{:S(2)}) collective-permute-start(bf16[128,512]{1,0:T(8,128)(2,1)S(1)} %copy-done.4), channel_id=1, source_target_pairs={{0,8},{8,16},{16,24},{24,0},{1,9},{9,17},{17,25},{25,1},{2,10},{10... | collective-permute-start | bytes 393224 | tf_op jit(solution)/shard_map/ppermute | solution.py:239
  (1 other events, 0.6 us)

commit v9 on v6

--- a/solution.py
+++ b/solution.py
@@ -164,7 +164,7 @@
 
 
 def query_kernel(nx, sc_ref, start_ref, st_ref, *refs):
-    q_refs, kv_ref, (*dq_refs, done_ref, acc_ref) = refs[:nx], refs[nx], refs[nx + 2 :]
+    q_refs, kv_ref, (dq_ref, done_ref, acc_ref) = refs[:nx], refs[nx], refs[nx + 2 :]
     done_ref[...] = jnp.zeros(done_ref.shape, done_ref.dtype)
     g, low, high, x = sc_ref[0], sc_ref[1], sc_ref[2], sc_ref[3]
     places = places_of(x, nx)
@@ -191,7 +191,7 @@
     for n in range(GROUP):
         dq = (acc_ref[n] * SCALE).T.astype(jnp.bfloat16)
         for d in range(nx):
-            dq_refs[d][:, n * HD : (n + 1) * HD] = dq[d * BLOCK : (d + 1) * BLOCK]
+            dq_ref[d, :, n * HD : (n + 1) * HD] = dq[d * BLOCK : (d + 1) * BLOCK]
 
 
 def regroup_kernel(nx, tps, sc_ref, f_ref, *out_refs):
@@ -278,11 +278,11 @@
     stats = pl.pallas_call(
         lambda *refs: stats_kernel(nx, *refs),
         out_shape=jax.ShapeDtypeStruct((3, GROUP, span), f32),
-        in_specs=[smem, vmem] + [vmem] * (nx + 1) + [unread] * (nx - 1),
+        in_specs=[smem, vmem] + [vmem] * (nx + 1) + [unread] * nx,
         out_specs=vmem,
         scratch_shapes=[pltpu.VMEM((3, GROUP, span), f32)],
         compiler_params=params,
-    )(scalars, start, *qd, kv, *from_x[1:])
+    )(scalars, start, *qd, kv, *from_x)
     all_stats = spread(stats, "x", nx)
     dv_part = pl.pallas_call(
         lambda *refs: value_kernel(nx, *refs),
@@ -291,12 +291,14 @@
         out_specs=vmem,
         compiler_params=params,
     )(scalars, start, all_stats, *qd, kv)
-    *dq_parts, done = pl.pallas_call(
+    dq_parts, done = pl.pallas_call(
         lambda *refs: query_kernel(nx, *refs),
-        out_shape=[jax.ShapeDtypeStruct((rows, GROUP * HD), bf16)] * nx
-        + [jax.ShapeDtypeStruct((8, BLOCK), f32)],
+        out_shape=(
+            jax.ShapeDtypeStruct((nx, rows, GROUP * HD), bf16),
+            jax.ShapeDtypeStruct((8, BLOCK), f32),
+        ),
         in_specs=[smem, vmem, vmem] + [vmem] * (nx + 1) + [unread],
-        out_specs=[vmem] * (nx + 1),
+        out_specs=(vmem, vmem),
         scratch_shapes=[pltpu.VMEM((GROUP, HD, span), f32)],
         compiler_params=params,
     )(scalars, start, all_stats, *qd, kv, dv_part)

time: 177 us -> 177 us (level)
  local copies, waits for them, and re-layouts: 7.19 us -> 4.63 us
  waiting for transfers between devices: 46.3 us -> 48.4 us
    unnamed x29 -> x17, local copies, waits for them, and re-layouts: 4.28 us -> 1.77 us
    all_to_all x2, waiting for transfers between devices: 13.9 us -> 16 us  [spread(): return lax.all_to_all(copies, axes, split_axis=0, concat_axis=0, tiled=True)]
where the time goes in v9:
time: 177 us; the launch traced here: 174 us
  starting transfers between devices  65.5 us (37%)
  waiting for transfers between devices  48.4 us (27%)
  blocking collectives  41.9 us (24%)
  Pallas kernels  8.29 us (5%)
  other arithmetic  4.82 us (3%)
  local copies, waits for them, and re-layouts  4.63 us (3%)
    ppermute x9, starting transfers between devices, shift(): return lax.ppermute(a, axis, [(i, (i + by) % n) for i in range(n)])  28.1 us
    all_to_all x2, starting transfers between devices, spread(): return lax.all_to_all(copies, axes, split_axis=0, concat_axis=0, tiled=True)  21.5 us
    ppermute x9, waiting for transfers between devices, shift(): return lax.ppermute(a, axis, [(i, (i + by) % n) for i in range(n)])  17.9 us
    all_to_all x2, waiting for transfers between devices, spread(): return lax.all_to_all(copies, axes, split_axis=0, concat_axis=0, tiled=True)  16 us
    all_to_all x1, starting transfers between devices, per_device(): lax.all_to_all(dv_part.reshape(groups, rows, HD), ('y', 'zh'), split_axis...  15.9 us
    all_to_all x1, blocking collectives, per_device(): pieces = lax.all_to_all(term, 'y', split_axis=0, concat_axis=0, tiled=True)  14.5 us
    all_to_all x1, waiting for transfers between devices, per_device(): lax.all_to_all(dv_part.reshape(groups, rows, HD), ('y', 'zh'), split_axis...  14.4 us
    all_to_all x1, blocking collectives, per_device(): lax.all_to_all(jnp.broadcast_to(summed[None], (nzh,) + summed.shape).resh...  10.7 us
  transfers between devices with their start and end apart: 12, of which 8 were waited for; matrix products, arithmetic and copies ran while one was open for 2% of the time, Pallas kernels for 2%

profile of v9, /device:TPU:6, one launch (start us, length us, event | category | flops | bytes accessed | tf_op | source)
XLA Modules:
  0.0 174.4 jit_solution(2933719351703395335)
XLA Ops:
  2.6 15.6 %all-to-all-start = ((bf16[16,128,256]{2,1,0:T(8,128)(2,1)}), bf16[16,128,256]{2,1,0:T(8,128)(2,1)S(1)}, u32[]{:S(2)}, u32[]{:S(2)}) async-start(bf16[16,128,256]{2,1,0:T(8,128)(2,1)} %broadcast_in_dim.24), calls=%async_computation | async-start | bytes 2097152 | tf_op jit(solution)/shard_map/all_to_all | solution.py:233
  18.3 2.7 %collective-permute-start.2 = (bf16[128,1024]{1,0:T(8,128)(2,1)S(1)}, bf16[128,1024]{1,0:T(8,128)(2,1)S(1)}, u32[]{:S(2)}, u32[]{:S(2)}) collective-permute-start(bf16[128,1024]{1,0:T(8,128)(2,1)S(1)} %constant_dynamic-update-slice_fusion.refs_2_.refs_3_), channel_id=1, source_target_pairs={{0,24},{8,0},{16,8},{24,16},{1,25},{9,1},{17,9},{25,17},{2,26},{10... | collective-permute-start | bytes 786440 | tf_op jit(solution)/shard_map/ppermute | solution.py:238
  21.1 3.0 %collective-permute-start.1 = (bf16[128,1024]{1,0:T(8,128)(2,1)S(1)}, bf16[128,1024]{1,0:T(8,128)(2,1)S(1)}, u32[]{:S(2)}, u32[]{:S(2)}) collective-permute-start(bf16[128,1024]{1,0:T(8,128)(2,1)S(1)} %constant_dynamic-update-slice_fusion.refs_2_.refs_3_), channel_id=1, source_target_pairs={{0,16},{8,24},{16,0},{24,8},{1,17},{9,25},{17,1},{25,9},{2,18},{10... | collective-permute-start | bytes 786440 | tf_op jit(solution)/shard_map/ppermute | solution.py:238
  24.1 4.0 %collective-permute-start = (bf16[128,1024]{1,0:T(8,128)(2,1)S(1)}, bf16[128,1024]{1,0:T(8,128)(2,1)S(1)}, u32[]{:S(2)}, u32[]{:S(2)}) collective-permute-start(bf16[128,1024]{1,0:T(8,128)(2,1)S(1)} %constant_dynamic-update-slice_fusion.refs_2_.refs_3_), channel_id=1, source_target_pairs={{0,8},{8,16},{16,24},{24,0},{1,9},{9,17},{17,25},{25,1},{2,10},{10... | collective-permute-start | bytes 786440 | tf_op jit(solution)/shard_map/ppermute | solution.py:238
  31.1 2.8 %collective-permute-start.3 = (bf16[128,1024]{1,0:T(8,128)(2,1)S(1)}, bf16[128,1024]{1,0:T(8,128)(2,1)S(1)}, u32[]{:S(2)}, u32[]{:S(2)}) collective-permute-start(bf16[128,1024]{1,0:T(8,128)(2,1)S(1)} %get-tuple-element.9), channel_id=1, source_target_pairs={{0,8},{8,16},{16,24},{24,0},{1,9},{9,17},{17,25},{25,1},{2,10},{10... | collective-permute-start | bytes 786440 | tf_op jit(solution)/shard_map/ppermute | solution.py:238
  33.9 3.2 %collective-permute-start.4 = (bf16[128,1024]{1,0:T(8,128)(2,1)S(1)}, bf16[128,1024]{1,0:T(8,128)(2,1)S(1)}, u32[]{:S(2)}, u32[]{:S(2)}) collective-permute-start(bf16[128,1024]{1,0:T(8,128)(2,1)S(1)} %get-tuple-element.10), channel_id=1, source_target_pairs={{0,16},{8,24},{16,0},{24,8},{1,17},{9,25},{17,1},{25,9},{2,18},{10... | collective-permute-start | bytes 786440 | tf_op jit(solution)/shard_map/ppermute | solution.py:238
  37.1 3.3 %collective-permute-start.5 = (bf16[128,1024]{1,0:T(8,128)(2,1)S(1)}, bf16[128,1024]{1,0:T(8,128)(2,1)S(1)}, u32[]{:S(2)}, u32[]{:S(2)}) collective-permute-start(bf16[128,1024]{1,0:T(8,128)(2,1)S(1)} %get-tuple-element.11), channel_id=1, source_target_pairs={{0,24},{8,0},{16,8},{24,16},{1,25},{9,1},{17,9},{25,17},{2,26},{10... | collective-permute-start | bytes 786440 | tf_op jit(solution)/shard_map/ppermute | solution.py:238
  40.5 4.3 %collective-permute-done.3.refs_8_.refs_3_ = bf16[128,1024]{1,0:T(8,128)(2,1)S(1)} collective-permute-done((bf16[128,1024]{1,0:T(8,128)(2,1)S(1)}, bf16[128,1024]{1,0:T(8,128)(2,1)S(1)}, u32[]{:S(2)}, u32[]{:S(2)}) %collective-permute-start.3) | collective-permute-done | bytes 262176 | tf_op jit(solution)/shard_map/ppermute | solution.py:238
  46.2 3.4 %collective-permute-done.5.refs_10_.refs_5_ = bf16[128,1024]{1,0:T(8,128)(2,1)S(1)} collective-permute-done((bf16[128,1024]{1,0:T(8,128)(2,1)S(1)}, bf16[128,1024]{1,0:T(8,128)(2,1)S(1)}, u32[]{:S(2)}, u32[]{:S(2)}) %collective-permute-start.5) | collective-permute-done | bytes 262176 | tf_op jit(solution)/shard_map/ppermute | solution.py:238
  49.6 7.7 %all-to-all-done = bf16[16,128,256]{2,1,0:T(8,128)(2,1)S(1)} async-done(((bf16[16,128,256]{2,1,0:T(8,128)(2,1)}), bf16[16,128,256]{2,1,0:T(8,128)(2,1)S(1)}, u32[]{:S(2)}, u32[]{:S(2)}) %all-to-all-start) | async-done | bytes 1048608 | tf_op jit(solution)/shard_map/all_to_all | solution.py:233
  59.0 8.3 %all_to_all.35.refs_2_ = f32[4,3,4,512]{3,2,1,0:T(4,128)S(1)} all-to-all(f32[4,3,4,512]{3,2,1,0:T(4,128)S(1)} %broadcast_in_dim.25), channel_id=1, replica_groups=mesh['y'=8,'zh'=2,'x'=4,'zl'=4,'core'=2] {'x'}, dimensions={0} | all-to-all | bytes 196608 | tf_op jit(solution)/shard_map/all_to_all | solution.py:233
  67.3 2.4 %shard_map.79.refs_8_ = bf16[2048,128]{1,0:T(8,128)(2,1)} custom-call(s32[4]{0:T(128)S(1)} %pad_add_fusion.refs_0_, s32[1,512]{1,0:T(1,128)S(1)} %bitcast.30, f32[4,3,4,512]{3,2,1,0:T(4,128)S(1)} %all_to_all.35.refs_2_, bf16[128,1024]{1,0:T(8,128)(2,1)S(1)} %constant_dynamic-update-slice_fusion.refs_2_.refs_3_, ...), custom_call_target="tpu_custom_call" | custom-call | tf_op jit(solution)/shard_map/pallas_call | solution.py:287
  69.7 15.9 %all-to-all-start.2 = ((bf16[16,128,128]{2,1,0:T(8,128)(2,1)}), bf16[16,128,128]{2,1,0:T(8,128)(2,1)S(1)}, u32[]{:S(2)}, u32[]{:S(2)}) async-start(bf16[16,128,128]{2,1,0:T(8,128)(2,1)} %bitcast.8), calls=%async_computation.2 | async-start | bytes 1048576 | tf_op jit(solution)/shard_map/all_to_all | solution.py:306
  85.5 2.4 %shard_map.80 = (bf16[4,128,512]{2,1,0:T(8,128)(2,1)S(1)}, f32[8,128]{1,0:T(8,128)S(1)}) custom-call(s32[4]{0:T(128)S(1)} %pad_add_fusion.refs_0_, s32[1,512]{1,0:T(1,128)S(1)} %bitcast.31, f32[4,3,4,512]{3,2,1,0:T(4,128)S(1)} %all_to_all.35.refs_2_, bf16[128,1024]{1,0:T(8,128)(2,1)S(1)} %constant_dynamic-update-slice_fusion.refs_2_.refs_3_, ...), custom_call_target="tpu_custom_call" | custom-call | tf_op jit(solution)/shard_map/pallas_call | solution.py:294
  88.7 14.4 %all-to-all-done.2.in_ref = bf16[16,128,128]{2,1,0:T(8,128)(2,1)S(1)} async-done(((bf16[16,128,128]{2,1,0:T(8,128)(2,1)}), bf16[16,128,128]{2,1,0:T(8,128)(2,1)S(1)}, u32[]{:S(2)}, u32[]{:S(2)}) %all-to-all-start.2) | async-done | bytes 524320 | tf_op jit(solution)/shard_map/all_to_all | solution.py:306
  103.2 8.3 %all_to_all.36.refs_1_ = bf16[4,128,128]{2,1,0:T(8,128)(2,1)S(1)} all-to-all(bf16[4,128,128]{2,1,0:T(8,128)(2,1)S(1)} %shard_map.81), channel_id=1, replica_groups=mesh['y'=8,'zh'=2,'x'=4,'zl'=4,'core'=2] {'x'}, dimensions={0} | all-to-all | bytes 262144 | tf_op jit(solution)/shard_map/all_to_all | solution.py:316
  113.4 14.5 %all_to_all.37 = bf16[8,8,16,128]{3,2,1,0:T(8,128)(2,1)S(1)} all-to-all(bf16[8,8,16,128]{3,2,1,0:T(8,128)(2,1)S(1)} %shard_map.82), channel_id=1, replica_groups=mesh['y'=8,'zh'=2,'x'=4,'zl'=4,'core'=2] {'y'}, dimensions={0} | all-to-all | bytes 524288 | tf_op jit(solution)/shard_map/all_to_all | solution.py:325
  128.0 10.7 %all_to_all.38 = bf16[16,16,128]{2,1,0:T(8,128)(2,1)S(1)} all-to-all(bf16[16,16,128]{2,1,0:T(8,128)(2,1)S(1)} %bitcast.32), channel_id=1, replica_groups=mesh['y'=8,'zh'=2,'x'=4,'zl'=4,'core'=2] {'zh','zl','core'}, dimensions={0} | all-to-all | bytes 131072 | tf_op jit(solution)/shard_map/all_to_all | solution.py:327
  139.9 5.8 %all-to-all-start.6 = ((bf16[32,16,1024]{2,1,0:T(8,128)(2,1)}), bf16[32,16,1024]{2,1,0:T(8,128)(2,1)S(1)}, u32[]{:S(2)}, u32[]{:S(2)}) async-start(bf16[32,16,1024]{2,1,0:T(8,128)(2,1)} %broadcast_in_dim.48), calls=%async_computation.6 | async-start | bytes 2097152 | tf_op jit(solution)/shard_map/all_to_all | solution.py:233
  145.7 2.7 %collective-permute-start.6 = (bf16[128,512]{1,0:T(8,128)(2,1)S(1)}, bf16[128,512]{1,0:T(8,128)(2,1)S(1)}, u32[]{:S(2)}, u32[]{:S(2)}) collective-permute-start(bf16[128,512]{1,0:T(8,128)(2,1)S(1)} %get-tuple-element.14), channel_id=1, source_target_pairs={{0,24},{8,0},{16,8},{24,16},{1,25},{9,1},{17,9},{25,17},{2,26},{10... | collective-permute-start | bytes 393224 | tf_op jit(solution)/shard_map/ppermute | solution.py:238
  148.5 4.3 %collective-permute-start.8 = (bf16[128,512]{1,0:T(8,128)(2,1)S(1)}, bf16[128,512]{1,0:T(8,128)(2,1)S(1)}, u32[]{:S(2)}, u32[]{:S(2)}) collective-permute-start(bf16[128,512]{1,0:T(8,128)(2,1)S(1)} %get-tuple-element.15), channel_id=1, source_target_pairs={{0,8},{8,16},{16,24},{24,0},{1,9},{9,17},{17,25},{25,1},{2,10},{10... | collective-permute-start | bytes 393224 | tf_op jit(solution)/shard_map/ppermute | solution.py:238
  154.9 2.9 %collective-permute-done.6 = bf16[128,512]{1,0:T(8,128)(2,1)S(1)} collective-permute-done((bf16[128,512]{1,0:T(8,128)(2,1)S(1)}, bf16[128,512]{1,0:T(8,128)(2,1)S(1)}, u32[]{:S(2)}, u32[]{:S(2)}) %collective-permute-start.6) | collective-permute-done | bytes 131104 | tf_op jit(solution)/shard_map/ppermute | solution.py:238
  157.8 5.9 %collective-permute-done.8 = bf16[128,512]{1,0:T(8,128)(2,1)S(1)} collective-permute-done((bf16[128,512]{1,0:T(8,128)(2,1)S(1)}, bf16[128,512]{1,0:T(8,128)(2,1)S(1)}, u32[]{:S(2)}, u32[]{:S(2)}) %collective-permute-start.8) | collective-permute-done | bytes 131104 | tf_op jit(solution)/shard_map/ppermute | solution.py:238
  164.4 8.4 %all-to-all-done.6 = bf16[32,16,1024]{2,1,0:T(8,128)(2,1)S(1)} async-done(((bf16[32,16,1024]{2,1,0:T(8,128)(2,1)}), bf16[32,16,1024]{2,1,0:T(8,128)(2,1)S(1)}, u32[]{:S(2)}, u32[]{:S(2)}) %all-to-all-start.6) | async-done | bytes 1048608 | tf_op jit(solution)/shard_map/all_to_all | solution.py:233
  (44 shorter events, 16.6 us)
Async XLA Ops:
  0.6 17.7 %copy-start.5 = (bf16[128,512]{1,0:T(8,128)(2,1)S(1)}, bf16[128,512]{1,0:T(8,128)(2,1)}, u32[]{:S(2)}) copy-start(bf16[128,512]{1,0:T(8,128)(2,1)} %param.6) | copy-start | bytes 393220
  0.6 17.7 %copy-start.6 = (bf16[128,512]{1,0:T(8,128)(2,1)S(1)}, bf16[128,512]{1,0:T(8,128)(2,1)}, u32[]{:S(2)}) copy-start(bf16[128,512]{1,0:T(8,128)(2,1)} %param.9) | copy-start | bytes 393220
  0.7 27.5 %copy-start.7 = (s32[8192]{0:T(1024)S(1)}, s32[8192]{0:T(1024)}, u32[]{:S(2)}) copy-start(s32[8192]{0:T(1024)} %param.11) | copy-start | bytes 98308
  0.7 29.6 %copy-start = (bf16[128,4096]{1,0:T(8,128)(2,1)S(1)}, bf16[128,4096]{1,0:T(8,128)(2,1)}, u32[]{:S(2)}) copy-start(bf16[128,4096]{1,0:T(8,128)(2,1)} %refs_1_.1) | copy-start | bytes 3145732
  2.6 54.6 %all-to-all-start = ((bf16[16,128,256]{2,1,0:T(8,128)(2,1)}), bf16[16,128,256]{2,1,0:T(8,128)(2,1)S(1)}, u32[]{:S(2)}, u32[]{:S(2)}) async-start(bf16[16,128,256]{2,1,0:T(8,128)(2,1)} %broadcast_in_dim.24), calls=%async_computation | async-start | bytes 2097152 | tf_op jit(solution)/shard_map/all_to_all | solution.py:233
  18.3 18.8 %collective-permute-start.2 = (bf16[128,1024]{1,0:T(8,128)(2,1)S(1)}, bf16[128,1024]{1,0:T(8,128)(2,1)S(1)}, u32[]{:S(2)}, u32[]{:S(2)}) collective-permute-start(bf16[128,1024]{1,0:T(8,128)(2,1)S(1)} %constant_dynamic-update-slice_fusion.refs_2_.refs_3_), channel_id=1, source_target_pairs={{0,24},{8,0},{16,8},{24,16},{1,25},{9,1},{17,9},{25,17},{2,26},{10... | collective-permute-start | bytes 786440 | tf_op jit(solution)/shard_map/ppermute | solution.py:238
  21.1 19.4 %collective-permute-start.1 = (bf16[128,1024]{1,0:T(8,128)(2,1)S(1)}, bf16[128,1024]{1,0:T(8,128)(2,1)S(1)}, u32[]{:S(2)}, u32[]{:S(2)}) collective-permute-start(bf16[128,1024]{1,0:T(8,128)(2,1)S(1)} %constant_dynamic-update-slice_fusion.refs_2_.refs_3_), channel_id=1, source_target_pairs={{0,16},{8,24},{16,0},{24,8},{1,17},{9,25},{17,1},{25,9},{2,18},{10... | collective-permute-start | bytes 786440 | tf_op jit(solution)/shard_map/ppermute | solution.py:238
  24.1 16.3 %collective-permute-start = (bf16[128,1024]{1,0:T(8,128)(2,1)S(1)}, bf16[128,1024]{1,0:T(8,128)(2,1)S(1)}, u32[]{:S(2)}, u32[]{:S(2)}) collective-permute-start(bf16[128,1024]{1,0:T(8,128)(2,1)S(1)} %constant_dynamic-update-slice_fusion.refs_2_.refs_3_), channel_id=1, source_target_pairs={{0,8},{8,16},{16,24},{24,0},{1,9},{9,17},{17,25},{25,1},{2,10},{10... | collective-permute-start | bytes 786440 | tf_op jit(solution)/shard_map/ppermute | solution.py:238
  31.1 13.6 %collective-permute-start.3 = (bf16[128,1024]{1,0:T(8,128)(2,1)S(1)}, bf16[128,1024]{1,0:T(8,128)(2,1)S(1)}, u32[]{:S(2)}, u32[]{:S(2)}) collective-permute-start(bf16[128,1024]{1,0:T(8,128)(2,1)S(1)} %get-tuple-element.9), channel_id=1, source_target_pairs={{0,8},{8,16},{16,24},{24,0},{1,9},{9,17},{17,25},{25,1},{2,10},{10... | collective-permute-start | bytes 786440 | tf_op jit(solution)/shard_map/ppermute | solution.py:238
  33.9 12.3 %collective-permute-start.4 = (bf16[128,1024]{1,0:T(8,128)(2,1)S(1)}, bf16[128,1024]{1,0:T(8,128)(2,1)S(1)}, u32[]{:S(2)}, u32[]{:S(2)}) collective-permute-start(bf16[128,1024]{1,0:T(8,128)(2,1)S(1)} %get-tuple-element.10), channel_id=1, source_target_pairs={{0,16},{8,24},{16,0},{24,8},{1,17},{9,25},{17,1},{25,9},{2,18},{10... | collective-permute-start | bytes 786440 | tf_op jit(solution)/shard_map/ppermute | solution.py:238
  37.1 12.5 %collective-permute-start.5 = (bf16[128,1024]{1,0:T(8,128)(2,1)S(1)}, bf16[128,1024]{1,0:T(8,128)(2,1)S(1)}, u32[]{:S(2)}, u32[]{:S(2)}) collective-permute-start(bf16[128,1024]{1,0:T(8,128)(2,1)S(1)} %get-tuple-element.11), channel_id=1, source_target_pairs={{0,24},{8,0},{16,8},{24,16},{1,25},{9,1},{17,9},{25,17},{2,26},{10... | collective-permute-start | bytes 786440 | tf_op jit(solution)/shard_map/ppermute | solution.py:238
  49.6 20.1 %copy-start.1 = (bf16[128,1024]{1,0:T(8,128)(2,1)}, bf16[128,1024]{1,0:T(8,128)(2,1)S(1)}, u32[]{:S(2)}) copy-start(bf16[128,1024]{1,0:T(8,128)(2,1)S(1)} %collective-permute-done.5.refs_10_.refs_5_) | copy-start | bytes 786436
  69.7 33.5 %all-to-all-start.2 = ((bf16[16,128,128]{2,1,0:T(8,128)(2,1)}), bf16[16,128,128]{2,1,0:T(8,128)(2,1)S(1)}, u32[]{:S(2)}, u32[]{:S(2)}) async-start(bf16[16,128,128]{2,1,0:T(8,128)(2,1)} %bitcast.8), calls=%async_computation.2 | async-start | bytes 1048576 | tf_op jit(solution)/shard_map/all_to_all | solution.py:306
  87.9 0.8 copy-start.3
  111.5 1.0 copy-start.2
  127.9 17.8 %copy-start.4 = (bf16[4,128,512]{2,1,0:T(8,128)(2,1)S(1)}, bf16[4,128,512]{2,1,0:T(8,128)(2,1)}, u32[]{:S(2)}) copy-start(bf16[4,128,512]{2,1,0:T(8,128)(2,1)} %copy-done.3) | copy-start | bytes 1572868
  139.9 32.8 %all-to-all-start.6 = ((bf16[32,16,1024]{2,1,0:T(8,128)(2,1)}), bf16[32,16,1024]{2,1,0:T(8,128)(2,1)S(1)}, u32[]{:S(2)}, u32[]{:S(2)}) async-start(bf16[32,16,1024]{2,1,0:T(8,128)(2,1)} %broadcast_in_dim.48), calls=%async_computation.6 | async-start | bytes 2097152 | tf_op jit(solution)/shard_map/all_to_all | solution.py:233
  145.7 12.0 %collective-permute-start.6 = (bf16[128,512]{1,0:T(8,128)(2,1)S(1)}, bf16[128,512]{1,0:T(8,128)(2,1)S(1)}, u32[]{:S(2)}, u32[]{:S(2)}) collective-permute-start(bf16[128,512]{1,0:T(8,128)(2,1)S(1)} %get-tuple-element.14), channel_id=1, source_target_pairs={{0,24},{8,0},{16,8},{24,16},{1,25},{9,1},{17,9},{25,17},{2,26},{10... | collective-permute-start | bytes 393224 | tf_op jit(solution)/shard_map/ppermute | solution.py:238
  148.5 15.2 %collective-permute-start.8 = (bf16[128,512]{1,0:T(8,128)(2,1)S(1)}, bf16[128,512]{1,0:T(8,128)(2,1)S(1)}, u32[]{:S(2)}, u32[]{:S(2)}) collective-permute-start(bf16[128,512]{1,0:T(8,128)(2,1)S(1)} %get-tuple-element.15), channel_id=1, source_target_pairs={{0,8},{8,16},{16,24},{24,0},{1,9},{9,17},{17,25},{25,1},{2,10},{10... | collective-permute-start | bytes 393224 | tf_op jit(solution)/shard_map/ppermute | solution.py:238
  152.8 10.8 %collective-permute-start.7 = (bf16[128,512]{1,0:T(8,128)(2,1)S(1)}, bf16[128,512]{1,0:T(8,128)(2,1)S(1)}, u32[]{:S(2)}, u32[]{:S(2)}) collective-permute-start(bf16[128,512]{1,0:T(8,128)(2,1)S(1)} %get-tuple-element.16), channel_id=1, source_target_pairs={{0,16},{8,24},{16,0},{24,8},{1,17},{9,25},{17,1},{25,9},{2,18},{10... | collective-permute-start | bytes 393224 | tf_op jit(solution)/shard_map/ppermute | solution.py:238

commit v10 on v9

--- a/solution.py
+++ b/solution.py
@@ -134,7 +134,7 @@
 
 
 def value_kernel(nx, sc_ref, start_ref, st_ref, *refs):
-    q_refs, kv_ref, dv_ref = refs[:nx], refs[nx], refs[nx + 1]
+    q_refs, kv_ref, dv_ref = refs[:nx], refs[nx], refs[-1]
     g, low, high, x = sc_ref[0], sc_ref[1], sc_ref[2], sc_ref[3]
     places = places_of(x, nx)
     pos_q = positions_of(g, x, nx)
@@ -278,19 +278,19 @@
     stats = pl.pallas_call(
         lambda *refs: stats_kernel(nx, *refs),
         out_shape=jax.ShapeDtypeStruct((3, GROUP, span), f32),
-        in_specs=[smem, vmem] + [vmem] * (nx + 1) + [unread] * nx,
+        in_specs=[smem, vmem] + [vmem] * (nx + 1),
         out_specs=vmem,
         scratch_shapes=[pltpu.VMEM((3, GROUP, span), f32)],
         compiler_params=params,
-    )(scalars, start, *qd, kv, *from_x)
+    )(scalars, start, *qd, kv)
     all_stats = spread(stats, "x", nx)
     dv_part = pl.pallas_call(
         lambda *refs: value_kernel(nx, *refs),
         out_shape=jax.ShapeDtypeStruct((groups * rows, HD), bf16),
-        in_specs=[smem, vmem, vmem] + [vmem] * (nx + 1),
+        in_specs=[smem, vmem, vmem] + [vmem] * (nx + 1) + [unread] * nx,
         out_specs=vmem,
         compiler_params=params,
-    )(scalars, start, all_stats, *qd, kv)
+    )(scalars, start, all_stats, *qd, kv, *from_x)
     dq_parts, done = pl.pallas_call(
         lambda *refs: query_kernel(nx, *refs),
         out_shape=(

time: 177 us -> 179 us (1.011)
  the two profiles are of different devices: /device:TPU:6 before, /device:TPU:8 now
where the time goes in v10:
time: 179 us; the launch traced here: 177 us
  starting transfers between devices  71.5 us (40%)
  waiting for transfers between devices  46.6 us (26%)
  blocking collectives  33.7 us (19%)
  Pallas kernels  12.6 us (7%)
  local copies, waits for them, and re-layouts  6.61 us (4%)
  other arithmetic  4.96 us (3%)
    ppermute x9, starting transfers between devices, shift(): return lax.ppermute(a, axis, [(i, (i + by) % n) for i in range(n)])  31.2 us
    all_to_all x3, starting transfers between devices, spread(): return lax.all_to_all(copies, axes, split_axis=0, concat_axis=0, tiled=True)  25.3 us
    all_to_all x3, waiting for transfers between devices, spread(): return lax.all_to_all(copies, axes, split_axis=0, concat_axis=0, tiled=True)  24.9 us
    all_to_all x1, starting transfers between devices, per_device(): lax.all_to_all(dv_part.reshape(groups, rows, HD), ('y', 'zh'), split_axis...  15 us
    all_to_all x1, blocking collectives, per_device(): pieces = lax.all_to_all(term, 'y', split_axis=0, concat_axis=0, tiled=True)  14.6 us
    all_to_all x1, waiting for transfers between devices, per_device(): lax.all_to_all(dv_part.reshape(groups, rows, HD), ('y', 'zh'), split_axis...  11.4 us
    all_to_all x1, blocking collectives, per_device(): lax.all_to_all(jnp.broadcast_to(summed[None], (nzh,) + summed.shape).resh...  10.8 us
    ppermute x9, waiting for transfers between devices, shift(): return lax.ppermute(a, axis, [(i, (i + by) % n) for i in range(n)])  10.3 us
  transfers between devices with their start and end apart: 13, of which 5 were waited for; matrix products, arithmetic and copies ran while one was open for 2% of the time, Pallas kernels for 5%

profile of v10, /device:TPU:8, one launch (start us, length us, event | category | flops | bytes accessed | tf_op | source)
XLA Modules:
  0.0 176.9 jit_solution(14164512781671259738)
XLA Ops:
  2.6 16.0 %all-to-all-start = ((bf16[16,128,256]{2,1,0:T(8,128)(2,1)}), bf16[16,128,256]{2,1,0:T(8,128)(2,1)S(1)}, u32[]{:S(2)}, u32[]{:S(2)}) async-start(bf16[16,128,256]{2,1,0:T(8,128)(2,1)} %broadcast_in_dim.24), calls=%async_computation | async-start | bytes 2097152 | tf_op jit(solution)/shard_map/all_to_all | solution.py:233
  18.6 4.7 %collective-permute-start.2 = (bf16[128,1024]{1,0:T(8,128)(2,1)S(1)}, bf16[128,1024]{1,0:T(8,128)(2,1)S(1)}, u32[]{:S(2)}, u32[]{:S(2)}) collective-permute-start(bf16[128,1024]{1,0:T(8,128)(2,1)S(1)} %constant_dynamic-update-slice_fusion.refs_2_.refs_3_), channel_id=1, source_target_pairs={{0,24},{8,0},{16,8},{24,16},{1,25},{9,1},{17,9},{25,17},{2,26},{10... | collective-permute-start | bytes 786440 | tf_op jit(solution)/shard_map/ppermute | solution.py:238
  23.3 2.7 %collective-permute-start.1 = (bf16[128,1024]{1,0:T(8,128)(2,1)S(1)}, bf16[128,1024]{1,0:T(8,128)(2,1)S(1)}, u32[]{:S(2)}, u32[]{:S(2)}) collective-permute-start(bf16[128,1024]{1,0:T(8,128)(2,1)S(1)} %constant_dynamic-update-slice_fusion.refs_2_.refs_3_), channel_id=1, source_target_pairs={{0,16},{8,24},{16,0},{24,8},{1,17},{9,25},{17,1},{25,9},{2,18},{10... | collective-permute-start | bytes 786440 | tf_op jit(solution)/shard_map/ppermute | solution.py:238
  26.0 2.8 %collective-permute-start = (bf16[128,1024]{1,0:T(8,128)(2,1)S(1)}, bf16[128,1024]{1,0:T(8,128)(2,1)S(1)}, u32[]{:S(2)}, u32[]{:S(2)}) collective-permute-start(bf16[128,1024]{1,0:T(8,128)(2,1)S(1)} %constant_dynamic-update-slice_fusion.refs_2_.refs_3_), channel_id=1, source_target_pairs={{0,8},{8,16},{16,24},{24,0},{1,9},{9,17},{17,25},{25,1},{2,10},{10... | collective-permute-start | bytes 786440 | tf_op jit(solution)/shard_map/ppermute | solution.py:238
  34.2 3.7 %collective-permute-start.3 = (bf16[128,1024]{1,0:T(8,128)(2,1)}, bf16[128,1024]{1,0:T(8,128)(2,1)S(1)}, u32[]{:S(2)}, u32[]{:S(2)}) collective-permute-start(bf16[128,1024]{1,0:T(8,128)(2,1)} %get-tuple-element.9), channel_id=1, source_target_pairs={{0,8},{8,16},{16,24},{24,0},{1,9},{9,17},{17,25},{25,1},{2,10},{10... | collective-permute-start | bytes 786440 | tf_op jit(solution)/shard_map/ppermute | solution.py:238
  37.9 3.9 %collective-permute-start.4 = (bf16[128,1024]{1,0:T(8,128)(2,1)}, bf16[128,1024]{1,0:T(8,128)(2,1)S(1)}, u32[]{:S(2)}, u32[]{:S(2)}) collective-permute-start(bf16[128,1024]{1,0:T(8,128)(2,1)} %get-tuple-element.10), channel_id=1, source_target_pairs={{0,16},{8,24},{16,0},{24,8},{1,17},{9,25},{17,1},{25,9},{2,18},{10... | collective-permute-start | bytes 786440 | tf_op jit(solution)/shard_map/ppermute | solution.py:238
  41.8 2.6 %collective-permute-start.5 = (bf16[128,1024]{1,0:T(8,128)(2,1)}, bf16[128,1024]{1,0:T(8,128)(2,1)S(1)}, u32[]{:S(2)}, u32[]{:S(2)}) collective-permute-start(bf16[128,1024]{1,0:T(8,128)(2,1)} %get-tuple-element.11), channel_id=1, source_target_pairs={{0,24},{8,0},{16,8},{24,16},{1,25},{9,1},{17,9},{25,17},{2,26},{10... | collective-permute-start | bytes 786440 | tf_op jit(solution)/shard_map/ppermute | solution.py:238
  44.4 12.0 %all-to-all-done = bf16[16,128,256]{2,1,0:T(8,128)(2,1)S(1)} async-done(((bf16[16,128,256]{2,1,0:T(8,128)(2,1)}), bf16[16,128,256]{2,1,0:T(8,128)(2,1)S(1)}, u32[]{:S(2)}, u32[]{:S(2)}) %all-to-all-start) | async-done | bytes 1048608 | tf_op jit(solution)/shard_map/all_to_all | solution.py:233
  56.4 2.8 %shard_map.77 = f32[3,4,512]{2,1,0:T(4,128)S(1)} custom-call(s32[4]{0:T(128)S(1)} %pad_add_fusion.refs_0_, s32[1,512]{1,0:T(1,128)S(1)} %bitcast.29, bf16[128,1024]{1,0:T(8,128)(2,1)S(1)} %constant_dynamic-update-slice_fusion.refs_2_.refs_3_, bf16[128,1024]{1,0:T(8,128)(2,1)S(1)} %collective-permute-done.refs_3_.refs_4_, ...), custom_call_target="tpu_custom_call" | custom-call | tf_op jit(solution)/shard_map/pallas_call | solution.py:278
  59.9 4.3 %all-to-all-start.1 = ((f32[4,3,4,512]{3,2,1,0:T(4,128)}), f32[4,3,4,512]{3,2,1,0:T(4,128)S(1)}, u32[]{:S(2)}, u32[]{:S(2)}) async-start(f32[4,3,4,512]{3,2,1,0:T(4,128)} %broadcast_in_dim.25), calls=%async_computation.1 | async-start | bytes 196608 | tf_op jit(solution)/shard_map/all_to_all | solution.py:233
  64.2 5.8 %all-to-all-done.1.refs_2_ = f32[4,3,4,512]{3,2,1,0:T(4,128)S(1)} async-done(((f32[4,3,4,512]{3,2,1,0:T(4,128)}), f32[4,3,4,512]{3,2,1,0:T(4,128)S(1)}, u32[]{:S(2)}, u32[]{:S(2)}) %all-to-all-start.1) | async-done | bytes 98336 | tf_op jit(solution)/shard_map/all_to_all | solution.py:233
  69.9 3.3 %shard_map.79.refs_8_ = bf16[2048,128]{1,0:T(8,128)(2,1)} custom-call(s32[4]{0:T(128)S(1)} %pad_add_fusion.refs_0_, s32[1,512]{1,0:T(1,128)S(1)} %bitcast.30, f32[4,3,4,512]{3,2,1,0:T(4,128)S(1)} %all-to-all-done.1.refs_2_, bf16[128,1024]{1,0:T(8,128)(2,1)S(1)} %constant_dynamic-update-slice_fusion.refs_2_.refs_3_, ...), custom_call_target="tpu_custom_call" | custom-call | tf_op jit(solution)/shard_map/pallas_call | solution.py:287
  73.2 15.0 %all-to-all-start.2 = ((bf16[16,128,128]{2,1,0:T(8,128)(2,1)}), bf16[16,128,128]{2,1,0:T(8,128)(2,1)S(1)}, u32[]{:S(2)}, u32[]{:S(2)}) async-start(bf16[16,128,128]{2,1,0:T(8,128)(2,1)} %bitcast.8), calls=%async_computation.2 | async-start | bytes 1048576 | tf_op jit(solution)/shard_map/all_to_all | solution.py:306
  88.2 3.9 %shard_map.80 = (bf16[4,128,512]{2,1,0:T(8,128)(2,1)S(1)}, f32[8,128]{1,0:T(8,128)S(1)}) custom-call(s32[4]{0:T(128)S(1)} %pad_add_fusion.refs_0_, s32[1,512]{1,0:T(1,128)S(1)} %bitcast.31, f32[4,3,4,512]{3,2,1,0:T(4,128)S(1)} %all-to-all-done.1.refs_2_, bf16[128,1024]{1,0:T(8,128)(2,1)S(1)} %constant_dynamic-update-slice_fusion.refs_2_.refs_3_, ...), custom_call_target="tpu_custom_call" | custom-call | tf_op jit(solution)/shard_map/pallas_call | solution.py:294
  92.9 11.4 %all-to-all-done.2.in_ref = bf16[16,128,128]{2,1,0:T(8,128)(2,1)S(1)} async-done(((bf16[16,128,128]{2,1,0:T(8,128)(2,1)}), bf16[16,128,128]{2,1,0:T(8,128)(2,1)S(1)}, u32[]{:S(2)}, u32[]{:S(2)}) %all-to-all-start.2) | async-done | bytes 524320 | tf_op jit(solution)/shard_map/all_to_all | solution.py:306
  104.4 8.4 %all_to_all.35.refs_1_ = bf16[4,128,128]{2,1,0:T(8,128)(2,1)S(1)} all-to-all(bf16[4,128,128]{2,1,0:T(8,128)(2,1)S(1)} %shard_map.81), channel_id=1, replica_groups=mesh['y'=8,'zh'=2,'x'=4,'zl'=4,'core'=2] {'x'}, dimensions={0} | all-to-all | bytes 262144 | tf_op jit(solution)/shard_map/all_to_all | solution.py:316
  114.7 14.6 %all_to_all.36 = bf16[8,8,16,128]{3,2,1,0:T(8,128)(2,1)S(1)} all-to-all(bf16[8,8,16,128]{3,2,1,0:T(8,128)(2,1)S(1)} %shard_map.82), channel_id=1, replica_groups=mesh['y'=8,'zh'=2,'x'=4,'zl'=4,'core'=2] {'y'}, dimensions={0} | all-to-all | bytes 524288 | tf_op jit(solution)/shard_map/all_to_all | solution.py:325
  129.4 10.8 %all_to_all.37 = bf16[16,16,128]{2,1,0:T(8,128)(2,1)S(1)} all-to-all(bf16[16,16,128]{2,1,0:T(8,128)(2,1)S(1)} %bitcast.32), channel_id=1, replica_groups=mesh['y'=8,'zh'=2,'x'=4,'zl'=4,'core'=2] {'zh','zl','core'}, dimensions={0} | all-to-all | bytes 131072 | tf_op jit(solution)/shard_map/all_to_all | solution.py:327
  141.2 5.0 %all-to-all-start.6 = ((bf16[32,16,1024]{2,1,0:T(8,128)(2,1)}), bf16[32,16,1024]{2,1,0:T(8,128)(2,1)S(1)}, u32[]{:S(2)}, u32[]{:S(2)}) async-start(bf16[32,16,1024]{2,1,0:T(8,128)(2,1)} %broadcast_in_dim.48), calls=%async_computation.6 | async-start | bytes 2097152 | tf_op jit(solution)/shard_map/all_to_all | solution.py:233
  146.3 4.7 %collective-permute-start.6 = (bf16[128,512]{1,0:T(8,128)(2,1)S(1)}, bf16[128,512]{1,0:T(8,128)(2,1)S(1)}, u32[]{:S(2)}, u32[]{:S(2)}) collective-permute-start(bf16[128,512]{1,0:T(8,128)(2,1)S(1)} %get-tuple-element.14), channel_id=1, source_target_pairs={{0,24},{8,0},{16,8},{24,16},{1,25},{9,1},{17,9},{25,17},{2,26},{10... | collective-permute-start | bytes 393224 | tf_op jit(solution)/shard_map/ppermute | solution.py:238
  151.1 1.9 %collective-permute-start.8 = (bf16[128,512]{1,0:T(8,128)(2,1)S(1)}, bf16[128,512]{1,0:T(8,128)(2,1)S(1)}, u32[]{:S(2)}, u32[]{:S(2)}) collective-permute-start(bf16[128,512]{1,0:T(8,128)(2,1)S(1)} %get-tuple-element.15), channel_id=1, source_target_pairs={{0,8},{8,16},{16,24},{24,0},{1,9},{9,17},{17,25},{25,1},{2,10},{10... | collective-permute-start | bytes 393224 | tf_op jit(solution)/shard_map/ppermute | solution.py:238
  153.0 4.2 %collective-permute-start.7 = (bf16[128,512]{1,0:T(8,128)(2,1)S(1)}, bf16[128,512]{1,0:T(8,128)(2,1)S(1)}, u32[]{:S(2)}, u32[]{:S(2)}) collective-permute-start(bf16[128,512]{1,0:T(8,128)(2,1)S(1)} %get-tuple-element.16), channel_id=1, source_target_pairs={{0,16},{8,24},{16,0},{24,8},{1,17},{9,25},{17,1},{25,9},{2,18},{10... | collective-permute-start | bytes 393224 | tf_op jit(solution)/shard_map/ppermute | solution.py:238
  157.2 10.2 %collective-permute-done.8 = bf16[128,512]{1,0:T(8,128)(2,1)S(1)} collective-permute-done((bf16[128,512]{1,0:T(8,128)(2,1)S(1)}, bf16[128,512]{1,0:T(8,128)(2,1)S(1)}, u32[]{:S(2)}, u32[]{:S(2)}) %collective-permute-start.8) | collective-permute-done | bytes 131104 | tf_op jit(solution)/shard_map/ppermute | solution.py:238
  168.2 7.1 %all-to-all-done.6 = bf16[32,16,1024]{2,1,0:T(8,128)(2,1)S(1)} async-done(((bf16[32,16,1024]{2,1,0:T(8,128)(2,1)}), bf16[32,16,1024]{2,1,0:T(8,128)(2,1)S(1)}, u32[]{:S(2)}, u32[]{:S(2)}) %all-to-all-start.6) | async-done | bytes 1048608 | tf_op jit(solution)/shard_map/all_to_all | solution.py:233
  (45 shorter events, 14.3 us)
Async XLA Ops:
  0.6 17.9 %copy-start.5 = (bf16[128,512]{1,0:T(8,128)(2,1)S(1)}, bf16[128,512]{1,0:T(8,128)(2,1)}, u32[]{:S(2)}) copy-start(bf16[128,512]{1,0:T(8,128)(2,1)} %param.6) | copy-start | bytes 393220
  0.6 18.0 %copy-start.6 = (bf16[128,512]{1,0:T(8,128)(2,1)S(1)}, bf16[128,512]{1,0:T(8,128)(2,1)}, u32[]{:S(2)}) copy-start(bf16[128,512]{1,0:T(8,128)(2,1)} %param.9) | copy-start | bytes 393220
  0.7 28.2 %copy-start.7 = (s32[8192]{0:T(1024)S(1)}, s32[8192]{0:T(1024)}, u32[]{:S(2)}) copy-start(s32[8192]{0:T(1024)} %param.11) | copy-start | bytes 98308
  2.6 53.9 %all-to-all-start = ((bf16[16,128,256]{2,1,0:T(8,128)(2,1)}), bf16[16,128,256]{2,1,0:T(8,128)(2,1)S(1)}, u32[]{:S(2)}, u32[]{:S(2)}) async-start(bf16[16,128,256]{2,1,0:T(8,128)(2,1)} %broadcast_in_dim.24), calls=%async_computation | async-start | bytes 2097152 | tf_op jit(solution)/shard_map/all_to_all | solution.py:233
  18.6 23.2 %collective-permute-start.2 = (bf16[128,1024]{1,0:T(8,128)(2,1)S(1)}, bf16[128,1024]{1,0:T(8,128)(2,1)S(1)}, u32[]{:S(2)}, u32[]{:S(2)}) collective-permute-start(bf16[128,1024]{1,0:T(8,128)(2,1)S(1)} %constant_dynamic-update-slice_fusion.refs_2_.refs_3_), channel_id=1, source_target_pairs={{0,24},{8,0},{16,8},{24,16},{1,25},{9,1},{17,9},{25,17},{2,26},{10... | collective-permute-start | bytes 786440 | tf_op jit(solution)/shard_map/ppermute | solution.py:238
  23.3 21.1 %collective-permute-start.1 = (bf16[128,1024]{1,0:T(8,128)(2,1)S(1)}, bf16[128,1024]{1,0:T(8,128)(2,1)S(1)}, u32[]{:S(2)}, u32[]{:S(2)}) collective-permute-start(bf16[128,1024]{1,0:T(8,128)(2,1)S(1)} %constant_dynamic-update-slice_fusion.refs_2_.refs_3_), channel_id=1, source_target_pairs={{0,16},{8,24},{16,0},{24,8},{1,17},{9,25},{17,1},{25,9},{2,18},{10... | collective-permute-start | bytes 786440 | tf_op jit(solution)/shard_map/ppermute | solution.py:238
  26.0 18.4 %collective-permute-start = (bf16[128,1024]{1,0:T(8,128)(2,1)S(1)}, bf16[128,1024]{1,0:T(8,128)(2,1)S(1)}, u32[]{:S(2)}, u32[]{:S(2)}) collective-permute-start(bf16[128,1024]{1,0:T(8,128)(2,1)S(1)} %constant_dynamic-update-slice_fusion.refs_2_.refs_3_), channel_id=1, source_target_pairs={{0,8},{8,16},{16,24},{24,0},{1,9},{9,17},{17,25},{25,1},{2,10},{10... | collective-permute-start | bytes 786440 | tf_op jit(solution)/shard_map/ppermute | solution.py:238
  31.3 1.2 copy-start.2
  34.2 30.0 %collective-permute-start.3 = (bf16[128,1024]{1,0:T(8,128)(2,1)}, bf16[128,1024]{1,0:T(8,128)(2,1)S(1)}, u32[]{:S(2)}, u32[]{:S(2)}) collective-permute-start(bf16[128,1024]{1,0:T(8,128)(2,1)} %get-tuple-element.9), channel_id=1, source_target_pairs={{0,8},{8,16},{16,24},{24,0},{1,9},{9,17},{17,25},{25,1},{2,10},{10... | collective-permute-start | bytes 786440 | tf_op jit(solution)/shard_map/ppermute | solution.py:238
  37.9 26.3 %collective-permute-start.4 = (bf16[128,1024]{1,0:T(8,128)(2,1)}, bf16[128,1024]{1,0:T(8,128)(2,1)S(1)}, u32[]{:S(2)}, u32[]{:S(2)}) collective-permute-start(bf16[128,1024]{1,0:T(8,128)(2,1)} %get-tuple-element.10), channel_id=1, source_target_pairs={{0,16},{8,24},{16,0},{24,8},{1,17},{9,25},{17,1},{25,9},{2,18},{10... | collective-permute-start | bytes 786440 | tf_op jit(solution)/shard_map/ppermute | solution.py:238
  41.8 22.3 %collective-permute-start.5 = (bf16[128,1024]{1,0:T(8,128)(2,1)}, bf16[128,1024]{1,0:T(8,128)(2,1)S(1)}, u32[]{:S(2)}, u32[]{:S(2)}) collective-permute-start(bf16[128,1024]{1,0:T(8,128)(2,1)} %get-tuple-element.11), channel_id=1, source_target_pairs={{0,24},{8,0},{16,8},{24,16},{1,25},{9,1},{17,9},{25,17},{2,26},{10... | collective-permute-start | bytes 786440 | tf_op jit(solution)/shard_map/ppermute | solution.py:238
  59.9 10.1 %all-to-all-start.1 = ((f32[4,3,4,512]{3,2,1,0:T(4,128)}), f32[4,3,4,512]{3,2,1,0:T(4,128)S(1)}, u32[]{:S(2)}, u32[]{:S(2)}) async-start(f32[4,3,4,512]{3,2,1,0:T(4,128)} %broadcast_in_dim.25), calls=%async_computation.1 | async-start | bytes 196608 | tf_op jit(solution)/shard_map/all_to_all | solution.py:233
  64.2 9.1 %copy-start = (bf16[128,1024]{1,0:T(8,128)(2,1)}, bf16[128,1024]{1,0:T(8,128)(2,1)S(1)}, u32[]{:S(2)}) copy-start(bf16[128,1024]{1,0:T(8,128)(2,1)S(1)} %collective-permute-done.5.refs_11_.refs_5_) | copy-start | bytes 786436
  73.2 31.1 %all-to-all-start.2 = ((bf16[16,128,128]{2,1,0:T(8,128)(2,1)}), bf16[16,128,128]{2,1,0:T(8,128)(2,1)S(1)}, u32[]{:S(2)}, u32[]{:S(2)}) async-start(bf16[16,128,128]{2,1,0:T(8,128)(2,1)} %bitcast.8), calls=%async_computation.2 | async-start | bytes 1048576 | tf_op jit(solution)/shard_map/all_to_all | solution.py:306
  92.1 0.8 copy-start.3
  112.8 1.0 copy-start.1
  129.3 17.0 %copy-start.4 = (bf16[4,128,512]{2,1,0:T(8,128)(2,1)S(1)}, bf16[4,128,512]{2,1,0:T(8,128)(2,1)}, u32[]{:S(2)}) copy-start(bf16[4,128,512]{2,1,0:T(8,128)(2,1)} %copy-done.3) | copy-start | bytes 1572868
  141.2 34.0 %all-to-all-start.6 = ((bf16[32,16,1024]{2,1,0:T(8,128)(2,1)}), bf16[32,16,1024]{2,1,0:T(8,128)(2,1)S(1)}, u32[]{:S(2)}, u32[]{:S(2)}) async-start(bf16[32,16,1024]{2,1,0:T(8,128)(2,1)} %broadcast_in_dim.48), calls=%async_computation.6 | async-start | bytes 2097152 | tf_op jit(solution)/shard_map/all_to_all | solution.py:233
  146.3 10.9 %collective-permute-start.6 = (bf16[128,512]{1,0:T(8,128)(2,1)S(1)}, bf16[128,512]{1,0:T(8,128)(2,1)S(1)}, u32[]{:S(2)}, u32[]{:S(2)}) collective-permute-start(bf16[128,512]{1,0:T(8,128)(2,1)S(1)} %get-tuple-element.14), channel_id=1, source_target_pairs={{0,24},{8,0},{16,8},{24,16},{1,25},{9,1},{17,9},{25,17},{2,26},{10... | collective-permute-start | bytes 393224 | tf_op jit(solution)/shard_map/ppermute | solution.py:238
  151.1 16.3 %collective-permute-start.8 = (bf16[128,512]{1,0:T(8,128)(2,1)S(1)}, bf16[128,512]{1,0:T(8,128)(2,1)S(1)}, u32[]{:S(2)}, u32[]{:S(2)}) collective-permute-start(bf16[128,512]{1,0:T(8,128)(2,1)S(1)} %get-tuple-element.15), channel_id=1, source_target_pairs={{0,8},{8,16},{16,24},{24,0},{1,9},{9,17},{17,25},{25,1},{2,10},{10... | collective-permute-start | bytes 393224 | tf_op jit(solution)/shard_map/ppermute | solution.py:238
  153.0 14.4 %collective-permute-start.7 = (bf16[128,512]{1,0:T(8,128)(2,1)S(1)}, bf16[128,512]{1,0:T(8,128)(2,1)S(1)}, u32[]{:S(2)}, u32[]{:S(2)}) collective-permute-start(bf16[128,512]{1,0:T(8,128)(2,1)S(1)} %get-tuple-element.16), channel_id=1, source_target_pairs={{0,16},{8,24},{16,0},{24,8},{1,17},{9,25},{17,1},{25,9},{2,18},{10... | collective-permute-start | bytes 393224 | tf_op jit(solution)/shard_map/ppermute | solution.py:238
